TPU v7x, 32 devices: a whole 2x2x4 slice. The times are simulated.
32 devices in a mesh: dp: 8 (over z, x), tensor: 4 (over y, core).
Axes of the slice: x: 2, y: 2, z: 4, core: 2. Of those that a mesh axis runs over, the one named last changes fastest.
Arguments:
- tokens: bfloat16 [2048, 1024], P(('dp', 'tensor')), may hold values from -6 to 6
- segments: int32 [2048], P('dp'), may hold values from 0 to 2, as said below
- zx_weight: bfloat16 [2, 1024, 1536], P(None, 'dp', 'tensor'), may hold values from -0.1875 to 0.1875
- dt_weight: bfloat16 [1024, 24], P('dp', 'tensor'), may hold values from -0.1875 to 0.1875
- query_weight: bfloat16 [1024, 512], P('dp', 'tensor'), may hold values from -0.1875 to 0.1875
- ssm_out_weight: bfloat16 [1536, 1024], P('tensor', 'dp'), may hold values from -0.3125 to 0.3125
- attn_out_weight: bfloat16 [512, 1024], P('tensor', 'dp'), may hold values from -2 to 2
- gate_up_weight: bfloat16 [2, 1024, 2048], P(None, 'dp', 'tensor'), may hold values from -0.1875 to 0.1875
- down_weight: bfloat16 [2048, 1024], P('tensor', 'dp'), may hold values from -0.125 to 0.125
- shared_weight: bfloat16 [1024, 512], P(('dp', 'tensor')), may hold values from -0.1875 to 0.1875
- norm_gains: float32 [2, 1024], replicated, may hold values from 0.25 to 1.75
- conv_params: float32 [5, 1792], replicated, may hold values from -3 to 3
- head_params: float32 [3, 24], replicated, may hold values from -7 to 2.7, as said below
- cotangent: bfloat16 [2048, 1024], P(('dp', 'tensor')), may hold values from -6 to 6
Outputs:
- output: bfloat16 [2048, 1024], P(('dp', 'tensor'))
- tokens_grad: float32 [2048, 1024], P(('dp', 'tensor'))
- zx_grad: float32 [2, 1024, 1536], P(None, 'dp', 'tensor')
- dt_grad: float32 [1024, 24], P('dp', 'tensor')
- query_grad: float32 [1024, 512], P('dp', 'tensor')
- ssm_out_grad: float32 [1536, 1024], P('tensor', 'dp')
- attn_out_grad: float32 [512, 1024], P('tensor', 'dp')
- gate_up_grad: float32 [2, 1024, 2048], P(None, 'dp', 'tensor')
- down_grad: float32 [2048, 1024], P('tensor', 'dp')
- shared_grad: float32 [1024, 512], P(('dp', 'tensor'))
- gains_grad: float32 [2, 1024], replicated
- conv_grad: float32 [5, 1792], replicated
- head_grad: float32 [3, 24], replicated
Inputs may be any that keep to these rules, and one draw needn't show every extreme that they name: `segments`: each sequence of 256 tokens holds three documents numbered 0, 1, 2 in order; the first and the last hold at least min(60, 32) tokens each; the middle one runs at least from the last token of the sequence's first quarter to the first token of its last quarter. `head_params`: row 0 holds step biases, row 1 logarithms of decay rates, row 2 skip gains.
All inputs are finite; a program needn't handle non-finite values.
Results may differ from a plain program's by a relative error of at most 0.014.
Values may be sent and summed in bfloat16 or wider, within the bound.
No kernel may reach another device: no remote copies, remote signals or barrier semaphores. Data moves between devices by JAX's collectives and lax.ppermute only.
A program may use at most 128 MiB of HBM per device.

v0:
```python
import math

import jax
import jax.numpy as jnp
from jax import lax
from jax.sharding import PartitionSpec as P

HDM = 64
NSTATE = 128
QH = 8
KVH = 2
HD = 64


EPSILON = 1e-05
FLOAT = jnp.float32
BFLOAT = jnp.bfloat16


def rms_norm(values, scale_vec):
    return (
        values * lax.rsqrt(jnp.mean(values * values, axis=-1, keepdims=True) + EPSILON) * scale_vec
    )


def causal_conv(values, segment, taps_all):
    running = taps_all[-1] + taps_all[-2] * values
    for offset in range(1, taps_all.shape[0] - 1):
        shifted = jnp.concatenate(
            [jnp.zeros_like(values[..., :offset, :]), values[..., :-offset, :]], axis=-2
        )
        same_doc = (segment[..., offset:] == segment[..., :-offset]).astype(values.dtype)
        same_doc = jnp.concatenate([jnp.zeros_like(same_doc[..., :offset]), same_doc], axis=-1)
        running = running + taps_all[-2 - offset] * shifted * same_doc[..., None]
    return running


def doc_mask(segment):
    length = segment.shape[0]
    row_index = lax.broadcasted_iota(jnp.int32, (length, length), 0)
    col_index = lax.broadcasted_iota(jnp.int32, (length, length), 1)
    return jnp.logical_and(row_index >= col_index, segment[:, None] == segment[None, :])


def einsum_f32(pattern, op_left, op_right):
    return jnp.einsum(pattern, op_left, op_right, preferred_element_type=jnp.float32)


def silu_gate(gate_proj, up_proj):
    return jax.nn.silu(gate_proj) * up_proj


def reduce_ffn(gate_up_grad, down_grad):
    return (
        lax.psum_scatter(gate_up_grad, "dp", scatter_dimension=1, tiled=True),
        lax.psum_scatter(down_grad, "dp", scatter_dimension=1, tiled=True),
    )


def per_device(
    tokens,
    segments,
    zx_weight,
    dt_weight,
    query_weight,
    ssm_out_weight,
    attn_out_weight,
    gate_up_weight,
    down_weight,
    shared_weight,
    norm_gains,
    conv_params,
    head_params,
    cotangent,
):
    shard_index = lax.axis_index("tensor")
    length = segments.shape[0]
    head_local = dt_weight.shape[1]
    width_local = zx_weight.shape[2]
    query_local = query_weight.shape[1] // HD
    kv_width = KVH * HD
    score_scale = 1.0 / math.sqrt(HD)
    zx_full, dt_full, query_full, ssm_out_full, attn_out_full, gate_up_full, down_full = (
        lax.all_gather(zx_weight, "dp", axis=1, tiled=True),
        lax.all_gather(dt_weight, "dp", axis=0, tiled=True),
        lax.all_gather(query_weight, "dp", axis=0, tiled=True),
        lax.all_gather(ssm_out_weight, "dp", axis=1, tiled=True),
        lax.all_gather(attn_out_weight, "dp", axis=1, tiled=True),
        lax.all_gather(gate_up_weight, "dp", axis=1, tiled=True),
        lax.all_gather(down_weight, "dp", axis=1, tiled=True),
    )
    shared_full = lax.all_gather(shared_weight, ("dp", "tensor"), axis=0, tiled=True)
    head_mine = lax.dynamic_slice_in_dim(head_params, shard_index * head_local, head_local, 1)
    bc_start = conv_params.shape[1] - 2 * NSTATE
    conv_mine = jnp.concatenate(
        [
            lax.dynamic_slice_in_dim(conv_params, shard_index * width_local, width_local, 1),
            conv_params[:, bc_start:],
        ],
        axis=1,
    )
    token_f = tokens.astype(FLOAT)
    normed_one, norm_one_back = jax.vjp(rms_norm, token_f, norm_gains[0])
    normed_low = normed_one.astype(BFLOAT)
    shared_local = einsum_f32("ld,dk->lk", normed_low, shared_full).astype(BFLOAT)
    normed_rows, shared_proj = (
        lax.all_gather(normed_low, "tensor", axis=0, tiled=True),
        lax.all_gather(shared_local, "tensor", axis=0, tiled=True),
    )
    gate_z = einsum_f32("ld,dc->lc", normed_rows, zx_full[0])
    x_raw = einsum_f32("ld,dc->lc", normed_rows, zx_full[1])
    step_raw = einsum_f32("ld,dh->lh", normed_rows, dt_full)
    queries = einsum_f32("ld,dq->lq", normed_rows, query_full).astype(BFLOAT)
    mask_bool = doc_mask(segments)
    mask_float = mask_bool.astype(FLOAT)

    def conv_piece(x_part, bc_part, taps_all):
        return jax.nn.silu(
            causal_conv(jnp.concatenate([x_part, bc_part], axis=1), segments, taps_all)
        )

    conv_act, conv_back = jax.vjp(
        conv_piece, x_raw, shared_proj[:, 2 * kv_width :].astype(FLOAT), conv_mine
    )
    x_conv = conv_act[:, :width_local].astype(BFLOAT)
    b_state = conv_act[:, width_local : width_local + NSTATE].astype(BFLOAT)
    c_state = conv_act[:, width_local + NSTATE :].astype(BFLOAT)

    def decay_piece(raw_steps, bias_vec, log_rate):
        step_vals = jax.nn.softplus(raw_steps + bias_vec)
        return (step_vals, jnp.cumsum(step_vals * -jnp.exp(log_rate), axis=0))

    (step_size, decay_sum), decay_back = jax.vjp(decay_piece, step_raw, head_mine[0], head_mine[1])
    gram_mat = einsum_f32("in,jn->ij", c_state, b_state)

    def weight_piece(gram_heads, step_vals, sum_vals):
        log_gap = sum_vals.T[:, :, None] - sum_vals.T[:, None, :]
        decay_mat = jnp.exp(jnp.where(mask_bool, log_gap, 0.0)) * mask_float
        return gram_heads * decay_mat * step_vals.T[:, None, :]

    mix_weights, weight_back = jax.vjp(
        weight_piece, jnp.broadcast_to(gram_mat, (head_local, length, length)), step_size, decay_sum
    )
    weights_low = mix_weights.astype(BFLOAT)
    x_heads = x_conv.reshape(length, head_local, HDM)
    y_heads = einsum_f32("hij,jhp->ihp", weights_low, x_heads)

    def gate_piece(y_part, x_part, z_part, skip_gain):
        return (y_part + skip_gain[None, :, None] * x_part).reshape(length, -1) * jax.nn.silu(
            z_part
        )

    gated_out, gate_back = jax.vjp(gate_piece, y_heads, x_heads.astype(FLOAT), gate_z, head_mine[2])
    gated_low = gated_out.astype(BFLOAT)
    kv_owner = (shard_index * query_local + jnp.arange(query_local)) // (QH // KVH)
    kv_select = (kv_owner[:, None] == jnp.arange(KVH)[None, :]).astype(BFLOAT)
    key_heads = einsum_f32(
        "jkd,hk->jhd", shared_proj[:, :kv_width].reshape(length, KVH, HD), kv_select
    ).astype(BFLOAT)
    value_heads = einsum_f32(
        "jkd,hk->jhd", shared_proj[:, kv_width : 2 * kv_width].reshape(length, KVH, HD), kv_select
    ).astype(BFLOAT)
    query_heads = queries.reshape(length, query_local, HD)

    def attn_scores():
        scores = einsum_f32("ihd,jhd->hij", query_heads, key_heads) * score_scale
        return jnp.where(mask_bool, scores, -1000000000.0)

    masked = attn_scores()
    row_max = jnp.max(masked, axis=-1, keepdims=True)
    exp_scores = jnp.exp(masked - row_max)
    row_total = jnp.sum(exp_scores, axis=-1, keepdims=True)
    log_total = row_max + jnp.log(row_total)
    probs_low = (exp_scores / row_total).astype(BFLOAT)
    attn_low = einsum_f32("hij,jhd->ihd", probs_low, value_heads).reshape(length, -1).astype(BFLOAT)
    mixer_terms = einsum_f32("lc,cd->ld", gated_low, ssm_out_full) + einsum_f32(
        "lq,qd->ld", attn_low, attn_out_full
    )
    mixer_sum = lax.psum_scatter(mixer_terms, "tensor", scatter_dimension=0, tiled=True)
    hidden = token_f + mixer_sum
    normed_two, norm_two_back = jax.vjp(rms_norm, hidden, norm_gains[1])
    ffn_rows = lax.all_gather(normed_two.astype(BFLOAT), "tensor", axis=0, tiled=True)
    gate_proj = einsum_f32("ld,df->lf", ffn_rows, gate_up_full[0])
    up_proj = einsum_f32("ld,df->lf", ffn_rows, gate_up_full[1])
    ffn_act, act_back = jax.vjp(silu_gate, gate_proj, up_proj)
    act_low = ffn_act.astype(BFLOAT)
    ffn_sum = lax.psum_scatter(
        einsum_f32("lf,fd->ld", act_low, down_full).astype(jnp.bfloat16),
        "tensor",
        scatter_dimension=0,
        tiled=True,
    ).astype(jnp.float32)
    output = (hidden + ffn_sum).astype(BFLOAT)
    cot_rows = lax.all_gather(cotangent, "tensor", axis=0, tiled=True)
    down_grad = einsum_f32("lf,ld->fd", act_low, cot_rows)
    act_grad = einsum_f32("ld,fd->lf", cot_rows, down_full)
    gate_grad, up_grad = act_back(act_grad)
    gate_low = gate_grad.astype(BFLOAT)
    up_low = up_grad.astype(BFLOAT)
    gate_up_grad = jnp.stack(
        [einsum_f32("ld,lf->df", ffn_rows, gate_low), einsum_f32("ld,lf->df", ffn_rows, up_low)]
    )
    ffn_input_grad = einsum_f32("lf,df->ld", gate_low, gate_up_full[0]) + einsum_f32(
        "lf,df->ld", up_low, gate_up_full[1]
    )
    normed_two_grad = lax.psum_scatter(ffn_input_grad, "tensor", scatter_dimension=0, tiled=True)
    hidden_norm_grad, gain_two_grad = norm_two_back(normed_two_grad)
    hidden_grad = cotangent.astype(FLOAT) + hidden_norm_grad
    mix_grad_rows = lax.all_gather(hidden_grad.astype(BFLOAT), "tensor", axis=0, tiled=True)
    ssm_out_grad = einsum_f32("lc,ld->cd", gated_low, mix_grad_rows)
    attn_out_grad = einsum_f32("lq,ld->qd", attn_low, mix_grad_rows)
    gated_grad = einsum_f32("ld,cd->lc", mix_grad_rows, ssm_out_full)
    attn_grad = einsum_f32("ld,qd->lq", mix_grad_rows, attn_out_full)
    y_grad, x_skip_grad, z_grad, skip_grad = gate_back(gated_grad)
    y_low = y_grad.astype(BFLOAT)
    z_low = z_grad.astype(BFLOAT)
    weights_grad = einsum_f32("ihp,jhp->hij", y_low, x_heads)
    x_conv_grad = x_skip_grad + einsum_f32("hij,ihp->jhp", weights_low, y_low)
    gram_grad, step_grad, sum_grad = weight_back(weights_grad)
    gram_low = gram_grad.astype(BFLOAT)
    c_grad = einsum_f32("hij,jn->in", gram_low, b_state)
    b_grad = einsum_f32("hij,in->jn", gram_low, c_state)
    raw_step_grad, bias_grad, rate_grad = decay_back((step_grad, sum_grad))
    x_raw_grad, bc_raw_grad, taps_grad = conv_back(
        jnp.concatenate([x_conv_grad.reshape(length, -1), b_grad, c_grad], axis=1)
    )
    out_low = attn_grad.astype(BFLOAT).reshape(length, query_local, HD)
    value_sel_grad = einsum_f32("hij,ihd->jhd", probs_low, out_low)
    prob_grad = einsum_f32("ihd,jhd->hij", out_low, value_heads)
    softmax_rows = jnp.exp(attn_scores() - log_total) * mask_float
    score_grad = softmax_rows * (
        prob_grad - jnp.sum(softmax_rows * prob_grad, axis=-1, keepdims=True)
    )
    score_low = score_grad.astype(BFLOAT)
    query_grad_rows = (
        (einsum_f32("hij,jhd->ihd", score_low, key_heads) * score_scale)
        .reshape(length, -1)
        .astype(BFLOAT)
    )
    key_sel_grad = einsum_f32("hij,ihd->jhd", score_low, query_heads) * score_scale
    select_float = kv_select.astype(FLOAT)
    key_grad = jnp.einsum("jhd,hk->jkd", key_sel_grad, select_float).reshape(length, kv_width)
    value_grad = jnp.einsum("jhd,hk->jkd", value_sel_grad, select_float).reshape(length, kv_width)
    x_raw_low = x_raw_grad.astype(BFLOAT)
    step_low = raw_step_grad.astype(BFLOAT)
    normed_one_terms = (
        einsum_f32("lc,dc->ld", z_low, zx_full[0])
        + einsum_f32("lc,dc->ld", x_raw_low, zx_full[1])
        + einsum_f32("lh,dh->ld", step_low, dt_full)
        + einsum_f32("lq,dq->ld", query_grad_rows, query_full)
    )
    shared_terms = jnp.concatenate([key_grad, value_grad, bc_raw_grad], axis=1)
    normed_one_grad, shared_rows_grad = (
        lax.psum_scatter(
            normed_one_terms.astype(jnp.bfloat16), "tensor", scatter_dimension=0, tiled=True
        ).astype(jnp.float32),
        lax.psum_scatter(
            shared_terms.astype(jnp.bfloat16), "tensor", scatter_dimension=0, tiled=True
        ).astype(jnp.float32),
    )
    shared_low = shared_rows_grad.astype(BFLOAT)
    normed_one_grad = normed_one_grad + einsum_f32("lk,dk->ld", shared_low, shared_full)
    token_norm_grad, gain_one_grad = norm_one_back(normed_one_grad)
    tokens_grad = hidden_grad + token_norm_grad
    shared_part = einsum_f32("ld,lk->dk", normed_low, shared_low)
    zx_grad = jnp.stack(
        [
            einsum_f32("ld,lc->dc", normed_rows, z_low),
            einsum_f32("ld,lc->dc", normed_rows, x_raw_low),
        ]
    )
    dt_grad = einsum_f32("ld,lh->dh", normed_rows, step_low)
    query_grad = einsum_f32("ld,lq->dq", normed_rows, query_grad_rows)
    summed = (
        lax.psum_scatter(zx_grad, "dp", scatter_dimension=1, tiled=True),
        lax.psum_scatter(dt_grad, "dp", scatter_dimension=0, tiled=True),
        lax.psum_scatter(query_grad, "dp", scatter_dimension=0, tiled=True),
        lax.psum_scatter(ssm_out_grad, "dp", scatter_dimension=1, tiled=True),
        lax.psum_scatter(attn_out_grad, "dp", scatter_dimension=1, tiled=True),
    )
    gate_up_sum, down_sum = reduce_ffn(gate_up_grad, down_grad)
    shared_grad = lax.psum_scatter(shared_part, ("dp", "tensor"), scatter_dimension=0, tiled=True)
    conv_full = lax.dynamic_update_slice_in_dim(
        jnp.zeros_like(conv_params), taps_grad[:, :width_local], shard_index * width_local, 1
    )
    conv_full = conv_full.at[:, bc_start:].set(taps_grad[:, width_local:])
    head_full = lax.dynamic_update_slice_in_dim(
        jnp.zeros_like(head_params),
        jnp.stack([bias_grad, rate_grad, skip_grad]),
        shard_index * head_local,
        1,
    )
    gains_sum, conv_sum, head_sum = lax.psum(
        (jnp.stack([gain_one_grad, gain_two_grad]), conv_full, head_full), ("dp", "tensor")
    )
    return (
        output,
        tokens_grad,
        summed[0],
        summed[1],
        summed[2],
        summed[3],
        summed[4],
        gate_up_sum,
        down_sum,
        shared_grad,
        gains_sum,
        conv_sum,
        head_sum,
    )


def solution(mesh):
    placed = (
        P(("dp", "tensor"), None),
        P("dp"),
        P(None, "dp", "tensor"),
        P("dp", "tensor"),
        P("dp", "tensor"),
        P("tensor", "dp"),
        P("tensor", "dp"),
        P(None, "dp", "tensor"),
        P("tensor", "dp"),
        P(("dp", "tensor"), None),
        P(),
        P(),
        P(),
        P(("dp", "tensor"), None),
    )
    return jax.shard_map(
        per_device,
        mesh=mesh,
        in_specs=placed,
        out_specs=(
            P(("dp", "tensor"), None),
            P(("dp", "tensor"), None),
            P(None, "dp", "tensor"),
            P("dp", "tensor"),
            P("dp", "tensor"),
            P("tensor", "dp"),
            P("tensor", "dp"),
            P(None, "dp", "tensor"),
            P("tensor", "dp"),
            P(("dp", "tensor"), None),
            P(),
            P(),
            P(),
        ),
        check_vma=False,
    )
```

profile of v0, /device:TPU:0, one launch (start us, length us, event | category | flops | bytes accessed | tf_op | source)
XLA Modules:
  0.0 1055.7 jit_solution(13470731296200077744)
XLA Ops:
  15.0 8.6 all_gather.39
  25.5 26.3 %all_gather.43 = bf16[1024,6]{0,1:T(8,128)(2,1)S(1)} all-gather(bf16[128,6]{0,1:T(8,128)(2,1)S(1)} %copy-done.100), channel_id=1, replica_groups=mesh['dp'=8,'tensor'=4] {'dp'}, dimensions={0}, use_global_device_ids=true | all-gather | bytes 13824 | tf_op jit(solution)/shard_map/all_gather | solution.py:85
  55.0 31.0 %all_gather.45 = bf16[1024,128]{1,0:T(8,128)(2,1)S(1)} all-gather(bf16[128,128]{1,0:T(8,128)(2,1)S(1)} %copy-done.66), channel_id=1, replica_groups=mesh['dp'=8,'tensor'=4] {'dp'}, dimensions={0}, use_global_device_ids=true | all-gather | bytes 294912 | tf_op jit(solution)/shard_map/all_gather | solution.py:86
  86.3 27.4 %all_gather.46 = bf16[128,1024]{1,0:T(8,128)(2,1)S(1)} all-gather(bf16[128,128]{1,0:T(8,128)(2,1)S(1)} %copy-done.67), channel_id=1, replica_groups=mesh['dp'=8,'tensor'=4] {'dp'}, dimensions={1}, use_global_device_ids=true | all-gather | bytes 294912 | tf_op jit(solution)/shard_map/all_gather | solution.py:88
  116.7 29.5 %all_gather.44 = bf16[384,1024]{1,0:T(8,128)(2,1)} all-gather(bf16[384,128]{1,0:T(8,128)(2,1)S(1)} %copy-done.51), channel_id=1, replica_groups=mesh['dp'=8,'tensor'=4] {'dp'}, dimensions={1}, use_global_device_ids=true | all-gather | bytes 884736 | tf_op jit(solution)/shard_map/all_gather | solution.py:87
  147.7 5.8 all_gather.42
  169.6 7.7 all_gather.50
  177.4 13.7 %reduce-scatter.14.cloned.1.call-done = f32[64,1024]{1,0:T(8,128)} async-done(((f32[256,1024]{1,0:T(8,128)}), f32[64,1024]{1,0:T(8,128)}) %reduce-scatter.14.cloned.1.call-update) | async-done | bytes 262160 | tf_op jit(solution)/shard_map/reduce_scatter | solution.py:179
  192.8 6.8 all_gather.47
  199.6 43.1 %all-gather.9.cloned.1.call-done = bf16[2,1024,512]{2,1,0:T(8,128)(2,1)} async-done(((bf16[2,128,512]{2,1,0:T(8,128)(2,1)}), bf16[2,1024,512]{2,1,0:T(8,128)(2,1)}) %all-gather.9.cloned.1.call-update) | async-done | bytes 2097168 | tf_op jit(solution)/shard_map/all_gather | solution.py:89
  246.5 36.3 %all-gather.11.cloned.1.call-done = bf16[512,1024]{1,0:T(8,128)(2,1)} async-done(((bf16[512,128]{1,0:T(8,128)(2,1)}), bf16[512,1024]{1,0:T(8,128)(2,1)}) %all-gather.11.cloned.1.call-update) | async-done | bytes 1048592 | tf_op jit(solution)/shard_map/all_gather | solution.py:90
  289.4 22.6 %reduce-scatter.18.cloned.1.call-done = f32[64,1024]{1,0:T(8,128)} async-done(((f32[256,1024]{1,0:T(8,128)}), f32[64,1024]{1,0:T(8,128)}) %reduce-scatter.18.cloned.1.call-update) | async-done | bytes 262160 | tf_op jit(solution)/shard_map/reduce_scatter | solution.py:206
  315.4 6.9 all_gather.51
  346.9 7.6 reduce-window.16
  380.8 10.7 %reduce-scatter.20.cloned.1.call-done = bf16[64,1024]{1,0:T(8,128)(2,1)} async-done(((bf16[256,1024]{1,0:T(8,128)(2,1)}), bf16[64,1024]{1,0:T(8,128)(2,1)}) %reduce-scatter.20.cloned.1.call-update) | async-done | bytes 131088 | tf_op jit(solution)/shard_map/reduce_scatter | solution.py:254
  393.0 40.8 %all-reduce.13 = (f32[2,1024]{1,0:T(2,128)}, f32[5,1792]{1,0:T(8,128)}, f32[3,24]{1,0:T(4,128)}) all-reduce(f32[2,1024]{1,0:T(2,128)S(1)} %pad_maximum_fusion.5, f32[5,1792]{1,0:T(8,128)S(1)} %add_dynamic-update-slice_fusion, f32[3,24]{1,0:T(4,128)S(1)} %dynamic_update_slice.7), channel_id=1, replica_groups=mesh['dp'=8,'tensor'=4] {'dp','tensor'}, use_global_device_ids=true, to_apply=%region_30.31 | all-reduce | flops 11080 | bytes 88640 | tf_op jit(solution)/shard_map/psum | solution.py:293
  435.7 37.4 %reduce-scatter.26.cloned.1.call-done = f32[128,6]{0,1:T(8,128)} async-done(((f32[1024,6]{0,1:T(8,128)}), f32[128,6]{0,1:T(8,128)}) %reduce-scatter.26.cloned.1.call-update) | async-done | bytes 3088 | tf_op jit(solution)/shard_map/reduce_scatter | solution.py:276
  473.1 65.3 %reduce-scatter.28.cloned.1.call-done = f32[128,128]{1,0:T(8,128)} async-done(((f32[1024,128]{1,0:T(8,128)}), f32[128,128]{1,0:T(8,128)}) %reduce-scatter.28.cloned.1.call-update) | async-done | bytes 65552 | tf_op jit(solution)/shard_map/reduce_scatter | solution.py:277
  538.4 65.2 %reduce-scatter.32.cloned.1.call-done = f32[128,128]{1,0:T(8,128)} async-done(((f32[128,1024]{1,0:T(8,128)}), f32[128,128]{1,0:T(8,128)}) %reduce-scatter.32.cloned.1.call-update) | async-done | bytes 65552 | tf_op jit(solution)/shard_map/reduce_scatter | solution.py:279
  603.7 71.7 %reduce-scatter.36.cloned.1.call-done = f32[512,128]{1,0:T(8,128)} async-done(((f32[512,1024]{1,0:T(8,128)}), f32[512,128]{1,0:T(8,128)}) %reduce-scatter.36.cloned.1.call-update) | async-done | bytes 262160 | tf_op jit(solution)/shard_map/reduce_scatter | solution.py:56
  675.4 68.9 %reduce-scatter.30.cloned.1.call-done = f32[384,128]{1,0:T(8,128)} async-done(((f32[384,1024]{1,0:T(8,128)}), f32[384,128]{1,0:T(8,128)}) %reduce-scatter.30.cloned.1.call-update) | async-done | bytes 196624 | tf_op jit(solution)/shard_map/reduce_scatter | solution.py:278
  744.3 138.6 %reduce-scatter.38.cloned.1.call-done = f32[32,512]{1,0:T(8,128)} async-done(((f32[1024,512]{1,0:T(8,128)}), f32[32,512]{1,0:T(8,128)}) %reduce-scatter.38.cloned.1.call-update) | async-done | bytes 65552 | tf_op jit(solution)/shard_map/reduce_scatter | solution.py:282
  882.9 74.7 %reduce-scatter.24.cloned.1.call-done = f32[2,128,384]{2,1,0:T(8,128)} async-done(((f32[2,1024,384]{2,1,0:T(8,128)}), f32[2,128,384]{2,1,0:T(8,128)}) %reduce-scatter.24.cloned.1.call-update) | async-done | bytes 393232 | tf_op jit(solution)/shard_map/reduce_scatter | solution.py:275
  957.6 91.5 %reduce-scatter.34.cloned.1.call-done = f32[2,128,512]{2,1,0:T(8,128)} async-done(((f32[2,1024,512]{2,1,0:T(8,128)}), f32[2,128,512]{2,1,0:T(8,128)}) %reduce-scatter.34.cloned.1.call-update) | async-done | bytes 524304 | tf_op jit(solution)/shard_map/reduce_scatter | solution.py:55
  (401 shorter events, 102.1 us)
Async XLA Ops:
  7.2 139.0 %all-gather.7.cloned.1.call-start = ((), (), s32[]{:S(2)}) async-start(), calls=%async_computation.14 | async-start | bytes 1081344 | tf_op jit(solution)/shard_map/all_gather | solution.py:92
  7.9 148.7 %all-gather.5.cloned.1.call-start = ((), (), s32[]{:S(2)}) async-start(), calls=%async_computation.13 | async-start | bytes 1769472 | tf_op jit(solution)/shard_map/all_gather | solution.py:84
  8.7 182.3 %reduce-scatter.14.cloned.1.call-start = ((), (), s32[]{:S(2)}) async-start(), calls=%async_computation.15 | async-start | bytes 1310720 | tf_op jit(solution)/shard_map/reduce_scatter | solution.py:179
  11.2 75.1 %copy-start.67 = (bf16[128,128]{1,0:T(8,128)(2,1)S(1)}, bf16[128,128]{1,0:T(8,128)(2,1)}, u32[]{:S(2)}) copy-start(bf16[128,128]{1,0:T(8,128)(2,1)} %param.22) | copy-start | bytes 98308
  13.1 100.6 %copy-start.68 = (f32[5,1792]{1,0:T(8,128)S(1)}, f32[5,1792]{1,0:T(8,128)}, u32[]{:S(2)}) copy-start(f32[5,1792]{1,0:T(8,128)} %param.27) | copy-start | bytes 107524
  15.0 131.2 %copy-start.18 = (bf16[64,1024]{1,0:T(8,128)(2,1)}, bf16[64,1024]{1,0:T(8,128)(2,1)S(1)}, u32[]{:S(2)}) copy-start(bf16[64,1024]{1,0:T(8,128)(2,1)S(1)} %fusion.37) | copy-start | bytes 393220
  23.7 92.4 %slice-start = ((f32[5,1792]{1,0:T(8,128)}), f32[5,256]{1,0:T(8,128)S(1)}, s32[]{:S(2)}) async-start(f32[5,1792]{1,0:T(8,128)} %param.27), calls=%async_computation.30 | async-start | bytes 16384 | tf_op jit(solution)/shard_map/slice | solution.py:98
  23.7 93.1 %copy-start.51 = (bf16[384,128]{1,0:T(8,128)(2,1)S(1)}, bf16[384,128]{1,0:T(8,128)(2,1)}, u32[]{:S(2)}) copy-start(bf16[384,128]{1,0:T(8,128)(2,1)} %param.21) | copy-start | bytes 294916
  86.0 61.7 %copy-start.14 = (bf16[1024,128]{1,0:T(8,128)(2,1)}, bf16[1024,128]{1,0:T(8,128)(2,1)S(1)}, u32[]{:S(2)}) copy-start(bf16[1024,128]{1,0:T(8,128)(2,1)S(1)} %all_gather.45) | copy-start | bytes 786436
  86.3 67.7 %copy-start.49 = (bf16[256,128]{0,1:T(8,128)(2,1)}, bf16[256,128]{0,1:T(8,128)(2,1)S(1)}, u32[]{:S(2)}) copy-start(bf16[256,128]{0,1:T(8,128)(2,1)S(1)} %convolution_convert_fusion.6) | copy-start | bytes 196612
  168.4 74.2 %all-gather.9.cloned.1.call-start = ((), (), s32[]{:S(2)}) async-start(), calls=%async_computation.16 | async-start | bytes 2359296 | tf_op jit(solution)/shard_map/all_gather | solution.py:89
  169.0 113.8 %all-gather.11.cloned.1.call-start = ((), (), s32[]{:S(2)}) async-start(), calls=%async_computation.17 | async-start | bytes 1179648 | tf_op jit(solution)/shard_map/all_gather | solution.py:90
  169.6 142.5 %reduce-scatter.18.cloned.1.call-start = ((), (), s32[]{:S(2)}) async-start(), calls=%async_computation.19 | async-start | bytes 1310720 | tf_op jit(solution)/shard_map/reduce_scatter | solution.py:206
  288.1 80.8 %reduce-scatter.22.cloned.1.call-start = ((), (), s32[]{:S(2)}) async-start(), calls=%async_computation.21 | async-start | bytes 327680 | tf_op jit(solution)/shard_map/reduce_scatter | solution.py:257
  346.5 45.0 %reduce-scatter.20.cloned.1.call-start = ((), (), s32[]{:S(2)}) async-start(), calls=%async_computation.20 | async-start | bytes 655360 | tf_op jit(solution)/shard_map/reduce_scatter | solution.py:254
  358.6 75.3 %reduce-scatter.16.cloned.1.call-start = ((), (), s32[]{:S(2)}) async-start(), calls=%async_computation.18 | async-start | bytes 655360 | tf_op jit(solution)/shard_map/reduce_scatter | solution.py:187
  361.1 112.0 %reduce-scatter.26.cloned.1.call-start = ((), (), s32[]{:S(2)}) async-start(), calls=%async_computation.23 | async-start | bytes 36864 | tf_op jit(solution)/shard_map/reduce_scatter | solution.py:276
  362.0 176.4 %reduce-scatter.28.cloned.1.call-start = ((), (), s32[]{:S(2)}) async-start(), calls=%async_computation.24 | async-start | bytes 589824 | tf_op jit(solution)/shard_map/reduce_scatter | solution.py:277
  363.2 240.4 %reduce-scatter.32.cloned.1.call-start = ((), (), s32[]{:S(2)}) async-start(), calls=%async_computation.26 | async-start | bytes 589824 | tf_op jit(solution)/shard_map/reduce_scatter | solution.py:279
  364.3 311.0 %reduce-scatter.36.cloned.1.call-start = ((), (), s32[]{:S(2)}) async-start(), calls=%async_computation.28 | async-start | bytes 2359296 | tf_op jit(solution)/shard_map/reduce_scatter | solution.py:56
  366.3 378.0 %reduce-scatter.30.cloned.1.call-start = ((), (), s32[]{:S(2)}) async-start(), calls=%async_computation.25 | async-start | bytes 1769472 | tf_op jit(solution)/shard_map/reduce_scatter | solution.py:278
  368.8 514.1 %reduce-scatter.38.cloned.1.call-start = ((), (), s32[]{:S(2)}) async-start(), calls=%async_computation.29 | async-start | bytes 2162688 | tf_op jit(solution)/shard_map/reduce_scatter | solution.py:282
  371.5 586.1 %reduce-scatter.24.cloned.1.call-start = ((), (), s32[]{:S(2)}) async-start(), calls=%async_computation.22 | async-start | bytes 3538944 | tf_op jit(solution)/shard_map/reduce_scatter | solution.py:275
  374.4 674.7 %reduce-scatter.34.cloned.1.call-start = ((), (), s32[]{:S(2)}) async-start(), calls=%async_computation.27 | async-start | bytes 4718592 | tf_op jit(solution)/shard_map/reduce_scatter | solution.py:55
  (107 other events, 922.6 us)
Sparse Core Ops, SparseCore 0:
  10.9 56.8 all-gather.6
  70.0 45.6 all-gather.4
  168.5 22.4 reduce-scatter.13
  193.3 49.2 all-gather.8
  244.7 38.0 all-gather.10
  288.2 23.7 reduce-scatter.17
  346.6 20.5 reduce-scatter.21
  369.8 21.6 reduce-scatter.19
  394.0 21.6 reduce-scatter.15
  419.5 53.4 reduce-scatter.25
  477.4 61.0 reduce-scatter.27
  542.2 61.4 reduce-scatter.31
  608.2 67.1 reduce-scatter.35
  679.7 64.6 reduce-scatter.29
  747.0 135.9 reduce-scatter.37
  887.4 70.2 reduce-scatter.23
  962.1 86.9 reduce-scatter.33
where the time goes:
time: 1060 us
  waiting for transfers between devices  742 us (70%)
  blocking collectives  191 us (18%)
  matrix products  55 us (5%)
  other arithmetic  36.9 us (3%)
  between operations  15.4 us (1%)
  local copies, waits for them, and re-layouts  14.1 us (1%)
    reduce_scatter x1, waiting for transfers between devices, per_device(): lax.psum_scatter(shared_part, ('dp', 'tensor'), scatter_dimension=0, tile...  139 us
    reduce_scatter x1, waiting for transfers between devices, reduce_ffn(): lax.psum_scatter(gate_up_grad, 'dp', scatter_dimension=1, tiled=True)  91.5 us
    reduce_scatter x1, waiting for transfers between devices, per_device(): lax.psum_scatter(zx_grad, 'dp', scatter_dimension=1, tiled=True)  74.7 us
    reduce_scatter x1, waiting for transfers between devices, reduce_ffn(): lax.psum_scatter(down_grad, 'dp', scatter_dimension=1, tiled=True)  71.7 us
    reduce_scatter x1, waiting for transfers between devices, per_device(): lax.psum_scatter(ssm_out_grad, 'dp', scatter_dimension=1, tiled=True)  68.9 us
    reduce_scatter x1, waiting for transfers between devices, per_device(): lax.psum_scatter(query_grad, 'dp', scatter_dimension=0, tiled=True)  65.3 us
    reduce_scatter x1, waiting for transfers between devices, per_device(): lax.psum_scatter(attn_out_grad, 'dp', scatter_dimension=1, tiled=True)  65.2 us
    dot_general x44, matrix products, einsum_f32(): jnp.einsum(pattern, op_left, op_right, preferred_element_type=jnp.float32)  54.6 us
  transfers between devices with their start and end apart: 17, of which 13 were waited for; matrix products, arithmetic and copies ran while one was open for 6% of the time, Pallas kernels for 0%

commit v1 on v0

v1 whole, which is shorter than its diff:
```python
import math

import jax
import jax.numpy as jnp
from jax import lax
from jax.sharding import PartitionSpec as P

HDM = 64
NSTATE = 128
QH = 8
KVH = 2
HD = 64


EPSILON = 1e-05
FLOAT = jnp.float32
BFLOAT = jnp.bfloat16


def rms_norm(values, scale_vec):
    return (
        values * lax.rsqrt(jnp.mean(values * values, axis=-1, keepdims=True) + EPSILON) * scale_vec
    )


def causal_conv(values, segment, taps_all):
    running = taps_all[-1] + taps_all[-2] * values
    for offset in range(1, taps_all.shape[0] - 1):
        shifted = jnp.concatenate(
            [jnp.zeros_like(values[..., :offset, :]), values[..., :-offset, :]], axis=-2
        )
        same_doc = (segment[..., offset:] == segment[..., :-offset]).astype(values.dtype)
        same_doc = jnp.concatenate([jnp.zeros_like(same_doc[..., :offset]), same_doc], axis=-1)
        running = running + taps_all[-2 - offset] * shifted * same_doc[..., None]
    return running


def doc_mask(segment):
    length = segment.shape[0]
    row_index = lax.broadcasted_iota(jnp.int32, (length, length), 0)
    col_index = lax.broadcasted_iota(jnp.int32, (length, length), 1)
    return jnp.logical_and(row_index >= col_index, segment[:, None] == segment[None, :])


def einsum_f32(pattern, op_left, op_right):
    return jnp.einsum(pattern, op_left, op_right, preferred_element_type=jnp.float32)


def silu_gate(gate_proj, up_proj):
    return jax.nn.silu(gate_proj) * up_proj


def swap(values, axis, count, bits):
    return lax.ppermute(values, axis, [(i, i ^ bits) for i in range(count)])


def stages_of(count):
    top = count.bit_length() - 1
    groups = []
    while top > 0:
        low = max(0, top - 2)
        groups.append([m << low for m in range(1, 1 << (top - low))])
        top = low
    return groups


def block_order(count):
    order = [0]
    for group in stages_of(count):
        order = order + [r ^ m for m in group for r in order]
    return order


def reorder(values, index, count):
    blocks = values.reshape(values.shape[0], count, -1)
    for bit in range(count.bit_length() - 1):
        halves = blocks.reshape(values.shape[0], -1, 2, 1 << bit, blocks.shape[-1])
        flipped = jnp.flip(halves, axis=2)
        blocks = jnp.where((index >> bit) & 1 == 1, flipped, halves).reshape(blocks.shape)
    return blocks


def to_relative(values, index, count):
    blocks = reorder(values, index, count)
    return jnp.concatenate([blocks[:, r] for r in block_order(count)], axis=1)


def from_relative(values, index, count):
    order = block_order(count)
    blocks = values.reshape(values.shape[0], count, -1)
    plain = jnp.concatenate([blocks[:, order.index(r)] for r in range(count)], axis=1)
    return reorder(plain, index, count).reshape(values.shape)


def gather_dp(piece, count):
    parts = [piece]
    for group in stages_of(count):
        parts = parts + [swap(p, "dp", count, m) for m in group for p in parts]
    return jnp.concatenate(parts, axis=0)


def scatter_dp(left, right, count):
    groups = stages_of(count)
    size = left.shape[1]
    total = None
    for group in reversed(groups):
        share = size // (len(group) + 1)
        if total is None:
            kept = einsum_f32("ld,lc->dc", left[:, :share], right)
            sent = [
                einsum_f32("ld,lc->dc", left[:, k * share : (k + 1) * share], right).astype(BFLOAT)
                for k in range(1, len(group) + 1)
            ]
        else:
            kept = total[:share]
            sent = [
                total[k * share : (k + 1) * share].astype(BFLOAT) for k in range(1, len(group) + 1)
            ]
        for m, part in zip(group, sent):
            kept = kept + swap(part, "dp", count, m).astype(FLOAT)
        total = kept
        size = share
    return total


def sum_tensor(partial, index, axis):
    size = partial.shape[axis] // 4
    core, half = index & 1, index >> 1
    blocks = [lax.slice_in_dim(partial, k * size, (k + 1) * size, axis=axis) for k in range(4)]
    at_core = core == 0
    keep = [jnp.where(at_core, blocks[2 * y], blocks[2 * y + 1]) for y in range(2)]
    give = [jnp.where(at_core, blocks[2 * y + 1], blocks[2 * y]) for y in range(2)]
    got = swap(jnp.stack(give), "tensor", 4, 1)
    sums = [keep[y] + got[y] for y in range(2)]
    mine = jnp.where(half == 0, sums[0], sums[1])
    other = jnp.where(half == 0, sums[1], sums[0])
    return mine + swap(other.astype(BFLOAT), "tensor", 4, 2).astype(FLOAT)


def gather_tensor(values):
    return lax.all_gather(values, "tensor", axis=0, tiled=True)


def sum_all(values, count):
    def group_sum(items, axis, axis_count, bits):
        parts = [items] + [swap(items, axis, axis_count, m) for m in bits]
        while len(parts) > 1:
            parts = [parts[k] + parts[k + 1] for k in range(0, len(parts), 2)]
        return parts[0]

    total = group_sum(values, "tensor", 4, [1, 2, 3])
    for group in stages_of(count):
        total = group_sum(total, "dp", count, group)
    return total


def per_device(
    count,
    tokens,
    segments,
    zx_weight,
    dt_weight,
    query_weight,
    ssm_out_weight,
    attn_out_weight,
    gate_up_weight,
    down_weight,
    shared_weight,
    norm_gains,
    conv_params,
    head_params,
    cotangent,
):
    shard_index = lax.axis_index("tensor")
    dp_index = lax.axis_index("dp")
    length = segments.shape[0]
    rows = zx_weight.shape[1]
    head_local = dt_weight.shape[1]
    width_local = zx_weight.shape[2]
    query_cols = query_weight.shape[1]
    query_local = query_cols // HD
    ff_local = down_weight.shape[0]
    kv_width = KVH * HD
    score_scale = 1.0 / math.sqrt(HD)
    share_rows = shared_weight.shape[0]
    share_cols = shared_weight.shape[1]

    shared_pack = shared_weight.reshape(share_rows, 4, share_cols // 4)
    shared_pack = jnp.concatenate([shared_pack[:, k] for k in range(4)], axis=0)
    dt_pad = jnp.pad(dt_weight, ((0, 0), (0, 128 - head_local)))
    shared_got = gather_dp(shared_pack, count)
    in_full = gather_dp(
        jnp.concatenate([zx_weight[0], zx_weight[1], query_weight, dt_pad], axis=1), count
    )
    out_full = gather_dp(
        jnp.concatenate([ssm_out_weight, attn_out_weight], axis=0).T, count
    )
    gu_full = gather_dp(jnp.concatenate([gate_up_weight[0], gate_up_weight[1]], axis=1), count)
    down_full = gather_dp(down_weight.T, count)
    shared_got = shared_got.reshape(count, 4, share_rows, share_cols // 4)
    shared_got = jnp.concatenate([shared_got[:, k] for k in range(4)], axis=-1)
    near = jnp.stack([shared_got, swap(shared_got, "tensor", 4, 2)])
    both = jnp.stack([near, swap(near, "tensor", 4, 1)])
    both = jnp.where(shard_index & 1 == 1, both[::-1], both)
    both = jnp.where(shard_index >> 1 == 1, both[:, ::-1], both)
    shared_full = both.transpose(2, 1, 0, 3, 4).reshape(count * rows, share_cols)

    token_f = to_relative(tokens, dp_index, count).astype(FLOAT)
    cot_local = to_relative(cotangent, dp_index, count)
    gains = to_relative(norm_gains, dp_index, count)

    head_mine = lax.dynamic_slice_in_dim(head_params, shard_index * head_local, head_local, 1)
    bc_start = conv_params.shape[1] - 2 * NSTATE
    conv_mine = jnp.concatenate(
        [
            lax.dynamic_slice_in_dim(conv_params, shard_index * width_local, width_local, 1),
            conv_params[:, bc_start:],
        ],
        axis=1,
    )
    normed_one, norm_one_back = jax.vjp(rms_norm, token_f, gains[0])
    normed_rows = gather_tensor(normed_one.astype(BFLOAT))
    shared_proj = einsum_f32("ld,dk->lk", normed_rows, shared_full).astype(BFLOAT)
    projected = einsum_f32("ld,dc->lc", normed_rows, in_full)
    gate_z = projected[:, :width_local]
    x_raw = projected[:, width_local : 2 * width_local]
    queries = projected[:, 2 * width_local : 2 * width_local + query_cols].astype(BFLOAT)
    dt_start = 2 * width_local + query_cols
    step_raw = projected[:, dt_start : dt_start + head_local]
    mask_bool = doc_mask(segments)
    mask_float = mask_bool.astype(FLOAT)

    def conv_piece(x_part, bc_part, taps_all):
        return jax.nn.silu(
            causal_conv(jnp.concatenate([x_part, bc_part], axis=1), segments, taps_all)
        )

    conv_act, conv_back = jax.vjp(
        conv_piece, x_raw, shared_proj[:, 2 * kv_width :].astype(FLOAT), conv_mine
    )
    x_conv = conv_act[:, :width_local].astype(BFLOAT)
    b_state = conv_act[:, width_local : width_local + NSTATE].astype(BFLOAT)
    c_state = conv_act[:, width_local + NSTATE :].astype(BFLOAT)
    lower = (
        lax.broadcasted_iota(jnp.int32, (length, length), 0)
        >= lax.broadcasted_iota(jnp.int32, (length, length), 1)
    ).astype(FLOAT)

    def decay_piece(raw_steps, bias_vec, log_rate):
        step_vals = jax.nn.softplus(raw_steps + bias_vec)
        sums = jnp.dot(lower, step_vals * -jnp.exp(log_rate), precision=lax.Precision.HIGHEST)
        return (step_vals, sums)

    (step_size, decay_sum), decay_back = jax.vjp(decay_piece, step_raw, head_mine[0], head_mine[1])
    gram_mat = einsum_f32("in,jn->ij", c_state, b_state)

    def weight_piece(gram_heads, step_vals, sum_vals):
        log_gap = sum_vals.T[:, :, None] - sum_vals.T[:, None, :]
        decay_mat = jnp.exp(jnp.where(mask_bool, log_gap, 0.0)) * mask_float
        return gram_heads * decay_mat * step_vals.T[:, None, :]

    mix_weights, weight_back = jax.vjp(
        weight_piece, jnp.broadcast_to(gram_mat, (head_local, length, length)), step_size, decay_sum
    )
    weights_low = mix_weights.astype(BFLOAT)
    x_heads = x_conv.reshape(length, head_local, HDM)
    y_heads = einsum_f32("hij,jhp->ihp", weights_low, x_heads)

    def gate_piece(y_part, x_part, z_part, skip_gain):
        return (y_part + skip_gain[None, :, None] * x_part).reshape(length, -1) * jax.nn.silu(
            z_part
        )

    gated_out, gate_back = jax.vjp(gate_piece, y_heads, x_heads.astype(FLOAT), gate_z, head_mine[2])
    gated_low = gated_out.astype(BFLOAT)
    kv_owner = (shard_index * query_local) // (QH // KVH)
    key_rows = lax.dynamic_slice_in_dim(shared_proj, kv_owner * HD, HD, 1)
    value_rows = lax.dynamic_slice_in_dim(shared_proj, kv_width + kv_owner * HD, HD, 1)
    query_heads = queries.reshape(length, query_local, HD)
    scores = einsum_f32("ihd,jd->hij", query_heads, key_rows) * score_scale
    masked = jnp.where(mask_bool, scores, -1000000000.0)
    row_max = jnp.max(masked, axis=-1, keepdims=True)
    exp_scores = jnp.exp(masked - row_max)
    softmax_rows = exp_scores / jnp.sum(exp_scores, axis=-1, keepdims=True)
    probs_low = softmax_rows.astype(BFLOAT)
    attn_low = einsum_f32("hij,jd->ihd", probs_low, value_rows).reshape(length, -1).astype(BFLOAT)
    mixed_low = jnp.concatenate([gated_low, attn_low], axis=1)
    mixer_terms = einsum_f32("lc,dc->ld", mixed_low, out_full)
    hidden = token_f + sum_tensor(mixer_terms, shard_index, 0)
    normed_two, norm_two_back = jax.vjp(rms_norm, hidden, gains[1])
    ffn_rows = gather_tensor(normed_two.astype(BFLOAT))
    cot_rows = gather_tensor(cot_local)
    gate_up = einsum_f32("ld,df->lf", ffn_rows, gu_full)
    ffn_act, act_back = jax.vjp(silu_gate, gate_up[:, :ff_local], gate_up[:, ff_local:])
    act_low = ffn_act.astype(BFLOAT)
    act_grad = einsum_f32("ld,df->lf", cot_rows, down_full)
    gate_grad, up_grad = act_back(act_grad)
    gu_low = jnp.concatenate([gate_grad.astype(BFLOAT), up_grad.astype(BFLOAT)], axis=1)
    ffn_input_grad = einsum_f32("lf,df->ld", gu_low, gu_full)
    normed_two_grad = sum_tensor(ffn_input_grad, shard_index, 0)
    hidden_norm_grad, gain_two_grad = norm_two_back(normed_two_grad)
    hidden_grad = cot_local.astype(FLOAT) + hidden_norm_grad
    mix_grad_rows = gather_tensor(hidden_grad.astype(BFLOAT))
    gu_sum = scatter_dp(ffn_rows, gu_low, count)
    down_sum = scatter_dp(cot_rows, act_low, count)
    ffn_sum = sum_tensor(einsum_f32("lf,df->ld", act_low, down_full), shard_index, 0)
    output = (hidden + ffn_sum).astype(BFLOAT)

    mixed_grad = einsum_f32("ld,dc->lc", mix_grad_rows, out_full)
    gated_grad = mixed_grad[:, :width_local]
    attn_grad = mixed_grad[:, width_local:]
    out_sum = scatter_dp(mix_grad_rows, mixed_low, count)
    y_grad, x_skip_grad, z_grad, skip_grad = gate_back(gated_grad)
    y_low = y_grad.astype(BFLOAT)
    z_low = z_grad.astype(BFLOAT)
    weights_grad = einsum_f32("ihp,jhp->hij", y_low, x_heads)
    x_conv_grad = x_skip_grad + einsum_f32("hij,ihp->jhp", weights_low, y_low)
    gram_grad, step_grad, sum_grad = weight_back(weights_grad)
    gram_low = gram_grad.astype(BFLOAT)
    c_grad = einsum_f32("hij,jn->in", gram_low, b_state)
    b_grad = einsum_f32("hij,in->jn", gram_low, c_state)
    raw_step_grad, bias_grad, rate_grad = decay_back((step_grad, sum_grad))
    x_raw_grad, bc_raw_grad, taps_grad = conv_back(
        jnp.concatenate([x_conv_grad.reshape(length, -1), b_grad, c_grad], axis=1)
    )
    out_low = attn_grad.astype(BFLOAT).reshape(length, query_local, HD)
    value_grad = einsum_f32("hij,ihd->jd", probs_low, out_low)
    prob_grad = einsum_f32("ihd,jd->hij", out_low, value_rows)
    score_grad = softmax_rows * (
        prob_grad - jnp.sum(softmax_rows * prob_grad, axis=-1, keepdims=True)
    )
    score_low = score_grad.astype(BFLOAT)
    query_grad_rows = (
        (einsum_f32("hij,jd->ihd", score_low, key_rows) * score_scale)
        .reshape(length, -1)
        .astype(BFLOAT)
    )
    key_grad = einsum_f32("hij,ihd->jd", score_low, query_heads) * score_scale
    at_first = kv_owner == 0
    key_terms = jnp.concatenate(
        [jnp.where(at_first, key_grad, 0.0), jnp.where(at_first, 0.0, key_grad)], axis=1
    )
    value_terms = jnp.concatenate(
        [jnp.where(at_first, value_grad, 0.0), jnp.where(at_first, 0.0, value_grad)], axis=1
    )
    x_raw_low = x_raw_grad.astype(BFLOAT)
    step_low = raw_step_grad.astype(BFLOAT)
    shared_terms = jnp.concatenate([key_terms, value_terms, bc_raw_grad], axis=1)
    block_low = sum_tensor(shared_terms, shard_index, 1).astype(BFLOAT)
    block_width = share_cols // 4
    shared_mine = lax.dynamic_slice_in_dim(shared_full, shard_index * block_width, block_width, 1)
    step_pad = jnp.pad(step_low, ((0, 0), (0, 128 - head_local)))
    in_low = jnp.concatenate([z_low, x_raw_low, query_grad_rows, step_pad], axis=1)
    in_sum = scatter_dp(normed_rows, in_low, count)
    block_sum = scatter_dp(normed_rows, block_low, count)
    normed_one_terms = einsum_f32("lc,dc->ld", in_low, in_full) + einsum_f32(
        "lk,dk->ld", block_low, shared_mine
    )
    normed_one_grad = sum_tensor(normed_one_terms, shard_index, 0)
    token_norm_grad, gain_one_grad = norm_one_back(normed_one_grad)
    tokens_grad = from_relative(hidden_grad + token_norm_grad, dp_index, count)
    shared_sum = lax.all_to_all(
        block_sum, "tensor", split_axis=0, concat_axis=1, tiled=True
    )

    conv_full = lax.dynamic_update_slice_in_dim(
        jnp.zeros_like(conv_params), taps_grad[:, :width_local], shard_index * width_local, 1
    )
    conv_full = conv_full.at[:, bc_start:].set(taps_grad[:, width_local:])
    head_full = lax.dynamic_update_slice_in_dim(
        jnp.zeros_like(head_params),
        jnp.stack([bias_grad, rate_grad, skip_grad]),
        shard_index * head_local,
        1,
    )
    gains_grad = from_relative(jnp.stack([gain_one_grad, gain_two_grad]), dp_index, count)
    pieces = (gains_grad, conv_full, head_full)
    flat = jnp.concatenate([p.reshape(-1) for p in pieces])
    wide = -(-flat.shape[0] // 1024) * 1024
    summed = sum_all(jnp.pad(flat, (0, wide - flat.shape[0])).reshape(-1, 128), count).reshape(-1)
    small = []
    start = 0
    for p in pieces:
        small.append(summed[start : start + p.size].reshape(p.shape))
        start += p.size
    return (
        from_relative(output, dp_index, count),
        tokens_grad,
        jnp.stack([in_sum[:, :width_local], in_sum[:, width_local : 2 * width_local]]),
        in_sum[:, dt_start : dt_start + head_local],
        in_sum[:, 2 * width_local : dt_start],
        out_sum[:, :width_local].T,
        out_sum[:, width_local:].T,
        jnp.stack([gu_sum[:, :ff_local], gu_sum[:, ff_local:]]),
        down_sum.T,
        shared_sum,
        small[0],
        small[1],
        small[2],
    )


def solution(mesh):
    count = mesh.shape["dp"]
    placed = (
        P(("dp", "tensor"), None),
        P("dp"),
        P(None, "dp", "tensor"),
        P("dp", "tensor"),
        P("dp", "tensor"),
        P("tensor", "dp"),
        P("tensor", "dp"),
        P(None, "dp", "tensor"),
        P("tensor", "dp"),
        P(("dp", "tensor"), None),
        P(),
        P(),
        P(),
        P(("dp", "tensor"), None),
    )

    def body(*arrays):
        return per_device(count, *arrays)

    return jax.shard_map(
        body,
        mesh=mesh,
        in_specs=placed,
        out_specs=(
            P(("dp", "tensor"), None),
            P(("dp", "tensor"), None),
            P(None, "dp", "tensor"),
            P("dp", "tensor"),
            P("dp", "tensor"),
            P("tensor", "dp"),
            P("tensor", "dp"),
            P(None, "dp", "tensor"),
            P("tensor", "dp"),
            P(("dp", "tensor"), None),
            P(),
            P(),
            P(),
        ),
        check_vma=False,
    )
```

time: 1060 us -> 405 us (0.38)
  waiting for transfers between devices: 742 us -> 115 us
  blocking collectives: 191 us -> 29.2 us
  starting transfers between devices: 0.91 us -> 91.8 us
  local copies, waits for them, and re-layouts: 14.1 us -> 69.4 us
  between operations: 15.4 us -> 2.92 us
    reduce_scatter x13 -> x0, waiting for transfers between devices: 660 us -> none  [the longest x1 139 us: per_device(): lax.psum_scatter(shared_part, ('dp', 'tensor'), scatter_dimension=0, tile...]
    all_gather x9 -> x4, blocking collectives: 150 us -> 29.2 us  [gather_tensor(): return lax.all_gather(values, 'tensor', axis=0, tiled=True)]
    ppermute x0 -> x74, waiting for transfers between devices: none -> 113 us  [swap(): return lax.ppermute(values, axis, [(i, i ^ bits) for i in range(count)])]
    ppermute x0 -> x74, starting transfers between devices: none -> 88.2 us  [swap(): return lax.ppermute(values, axis, [(i, i ^ bits) for i in range(count)])]
    all_gather x4 -> x0, waiting for transfers between devices: 79.4 us -> none  [the longest x1 43.1 us: per_device(): lax.all_gather(gate_up_weight, 'dp', axis=1, tiled=True)]
    psum x1 -> x0, blocking collectives: 40.8 us -> none  [per_device(): lax.psum((jnp.stack([gain_one_grad, gain_two_grad]), conv_full, head_full...]
    unnamed x227 -> x291, local copies, waits for them, and re-layouts: 6.98 us -> 33.3 us
    dot_general x44 -> x31, matrix products: 54.6 us -> 43.9 us  [einsum_f32(): jnp.einsum(pattern, op_left, op_right, preferred_element_type=jnp.float32)]
  transfers between devices with their start and end apart: 17 -> 75, of which waited for: 13 -> 35; matrix products, arithmetic and copies ran while one was open for 6% -> 38% of each run, Pallas kernels for 0% -> 0%
where the time goes in v1:
time: 405 us; the launch traced here: 403 us
  waiting for transfers between devices  115 us (28%)
  starting transfers between devices  91.8 us (23%)
  local copies, waits for them, and re-layouts  69.4 us (17%)
  matrix products  50.2 us (12%)
  other arithmetic  44.7 us (11%)
  blocking collectives  29.2 us (7%)
    ppermute x74, waiting for transfers between devices, swap(): return lax.ppermute(values, axis, [(i, i ^ bits) for i in range(count)])  113 us
    ppermute x74, starting transfers between devices, swap(): return lax.ppermute(values, axis, [(i, i ^ bits) for i in range(count)])  88.2 us
    dot_general x31, matrix products, einsum_f32(): jnp.einsum(pattern, op_left, op_right, preferred_element_type=jnp.float32)  43.9 us
    unnamed x291, local copies, waits for them, and re-layouts  33.3 us
    all_gather x4, blocking collectives, gather_tensor(): return lax.all_gather(values, 'tensor', axis=0, tiled=True)  29.2 us
  transfers between devices with their start and end apart: 75, of which 35 were waited for; matrix products, arithmetic and copies ran while one was open for 38% of the time, Pallas kernels for 0%

profile of v1, /device:TPU:0, one launch (start us, length us, event | category | flops | bytes accessed | tf_op | source)
XLA Modules:
  0.0 402.7 jit_solution(3873963954033279170)
XLA Ops:
  2.2 2.9 collective-permute-start.19
  5.2 3.6 collective-permute-start.18
  27.7 7.2 %all_gather.12 = bf16[256,1024]{1,0:T(8,128)(2,1)S(1)} all-gather(bf16[64,1024]{1,0:T(8,128)(2,1)S(1)} %fusion.35), channel_id=1, replica_groups=mesh['dp'=8,'tensor'=4] {'tensor'}, dimensions={0}, use_global_device_ids=true | all-gather | bytes 655360 | tf_op jit(solution)/shard_map/all_gather | solution.py:141
  34.9 7.9 %all_gather.14 = bf16[256,1024]{1,0:T(8,128)(2,1)} all-gather(bf16[64,1024]{1,0:T(8,128)(2,1)S(1)} %constant_dynamic-update-slice_fusion.67), channel_id=1, replica_groups=mesh['dp'=8,'tensor'=4] {'tensor'}, dimensions={0}, use_global_device_ids=true | all-gather | bytes 655360 | tf_op jit(solution)/shard_map/all_gather | solution.py:141
  49.2 2.9 collective-permute-start.8
  57.2 3.6 collective-permute-done.9
  62.0 3.0 collective-permute-done.10
  94.3 3.8 collective-permute-done.33
  111.2 10.1 %collective-permute-done.26 = bf16[128,1024]{1,0:T(8,128)(2,1)} collective-permute-done((bf16[128,1024]{1,0:T(8,128)(2,1)}, bf16[128,1024]{1,0:T(8,128)(2,1)}, u32[]{:S(2)}, u32[]{:S(2)}) %collective-permute-start.26) | collective-permute-done | bytes 262176 | tf_op jit(solution)/shard_map/ppermute | solution.py:54
  125.8 3.8 collective-permute-done.1
  153.4 3.4 collective-permute-done.5
  195.2 3.5 collective-permute-done.29
  204.2 7.2 %all_gather.13 = bf16[256,1024]{1,0:T(8,128)(2,1)S(1)} all-gather(bf16[64,1024]{1,0:T(8,128)(2,1)S(1)} %multiply_convert_fusion.9), channel_id=1, replica_groups=mesh['dp'=8,'tensor'=4] {'tensor'}, dimensions={0}, use_global_device_ids=true | all-gather | bytes 655360 | tf_op jit(solution)/shard_map/all_gather | solution.py:141
  224.7 8.0 %collective-permute-done.59 = bf16[512,512]{1,0:T(8,128)(2,1)S(1)} collective-permute-done((bf16[512,512]{1,0:T(8,128)(2,1)S(1)}, bf16[512,512]{1,0:T(8,128)(2,1)S(1)}, u32[]{:S(2)}, u32[]{:S(2)}) %collective-permute-start.59) | collective-permute-done | bytes 524320 | tf_op jit(solution)/shard_map/ppermute | solution.py:54
  234.9 5.5 %collective-permute-start.60 = (bf16[128,512]{1,0:T(8,128)(2,1)}, bf16[128,512]{1,0:T(8,128)(2,1)}, u32[]{:S(2)}, u32[]{:S(2)}) collective-permute-start(bf16[128,512]{1,0:T(8,128)(2,1)} %get-tuple-element.206), channel_id=1, source_target_pairs={{0,8},{4,12},{8,0},{12,4},{16,24},{20,28},{24,16},{28,20},{1,9},{5... | collective-permute-start | bytes 393224 | tf_op jit(solution)/shard_map/ppermute | solution.py:54
  243.0 6.9 %all_gather.15 = bf16[256,1024]{1,0:T(8,128)(2,1)S(1)} all-gather(bf16[64,1024]{1,0:T(8,128)(2,1)S(1)} %fusion.153), channel_id=1, replica_groups=mesh['dp'=8,'tensor'=4] {'tensor'}, dimensions={0}, use_global_device_ids=true | all-gather | bytes 655360 | tf_op jit(solution)/shard_map/all_gather | solution.py:141
  255.7 3.1 fusion.13
  303.0 3.0 fusion.197
  318.1 3.5 all-to-all-start
  331.6 11.2 %collective-permute-done.57 = bf16[128,1024]{1,0:T(8,128)(2,1)} collective-permute-done((bf16[128,1024]{1,0:T(8,128)(2,1)}, bf16[128,1024]{1,0:T(8,128)(2,1)}, u32[]{:S(2)}, u32[]{:S(2)}) %collective-permute-start.57) | collective-permute-done | bytes 262176 | tf_op jit(solution)/shard_map/ppermute | solution.py:54
  345.6 5.5 %collective-permute-done.53 = bf16[128,512]{1,0:T(8,128)(2,1)S(1)} collective-permute-done((bf16[128,512]{1,0:T(8,128)(2,1)S(1)}, bf16[128,512]{1,0:T(8,128)(2,1)S(1)}, u32[]{:S(2)}, u32[]{:S(2)}) %collective-permute-start.53) | collective-permute-done | bytes 131104 | tf_op jit(solution)/shard_map/ppermute | solution.py:54
  356.6 3.9 collective-permute-done.46
  387.0 3.3 collective-permute-done.50
  390.3 10.1 %collective-permute-done.49 = bf16[128,1024]{1,0:T(8,128)(2,1)S(1)} collective-permute-done((bf16[128,1024]{1,0:T(8,128)(2,1)}, bf16[128,1024]{1,0:T(8,128)(2,1)S(1)}, u32[]{:S(2)}, u32[]{:S(2)}) %collective-permute-start.49) | collective-permute-done | bytes 262176 | tf_op jit(solution)/shard_map/ppermute | solution.py:54
  (648 shorter events, 272.7 us)
Async XLA Ops:
  2.2 85.9 %collective-permute-start.19 = (bf16[128,512]{0,1:T(8,128)(2,1)}, bf16[128,512]{0,1:T(8,128)(2,1)}, u32[]{:S(2)}, u32[]{:S(2)}) collective-permute-start(bf16[128,512]{0,1:T(8,128)(2,1)} %maximum_bitcast_fusion), channel_id=1, source_target_pairs={{0,4},{4,0},{8,12},{12,8},{16,20},{20,16},{24,28},{28,24},{1,5},{5... | collective-permute-start | bytes 393224 | tf_op jit(solution)/shard_map/ppermute | solution.py:54
  5.2 78.9 %collective-permute-start.18 = (bf16[128,512]{0,1:T(8,128)(2,1)}, bf16[128,512]{0,1:T(8,128)(2,1)}, u32[]{:S(2)}, u32[]{:S(2)}) collective-permute-start(bf16[128,512]{0,1:T(8,128)(2,1)} %maximum_bitcast_fusion), channel_id=1, source_target_pairs={{0,24},{4,28},{8,16},{12,20},{16,8},{20,12},{24,0},{28,4},{1,25},{... | collective-permute-start | bytes 393224 | tf_op jit(solution)/shard_map/ppermute | solution.py:54
  8.8 73.7 %collective-permute-start.17 = (bf16[128,512]{0,1:T(8,128)(2,1)}, bf16[128,512]{0,1:T(8,128)(2,1)}, u32[]{:S(2)}, u32[]{:S(2)}) collective-permute-start(bf16[128,512]{0,1:T(8,128)(2,1)} %maximum_bitcast_fusion), channel_id=1, source_target_pairs={{0,16},{4,20},{8,24},{12,28},{16,0},{20,4},{24,8},{28,12},{1,17},{... | collective-permute-start | bytes 393224 | tf_op jit(solution)/shard_map/ppermute | solution.py:54
  8.8 70.1 %collective-permute-start.16 = (bf16[128,512]{0,1:T(8,128)(2,1)}, bf16[128,512]{0,1:T(8,128)(2,1)}, u32[]{:S(2)}, u32[]{:S(2)}) collective-permute-start(bf16[128,512]{0,1:T(8,128)(2,1)} %maximum_bitcast_fusion), channel_id=1, source_target_pairs={{0,8},{4,12},{8,0},{12,4},{16,24},{20,28},{24,16},{28,20},{1,9},{5... | collective-permute-start | bytes 393224 | tf_op jit(solution)/shard_map/ppermute | solution.py:54
  13.4 35.8 %collective-permute-start.7 = (bf16[128,128]{1,0:T(8,128)(2,1)}, bf16[128,128]{1,0:T(8,128)(2,1)S(1)}, u32[]{:S(2)}, u32[]{:S(2)}) collective-permute-start(bf16[128,128]{1,0:T(8,128)(2,1)} %pad_maximum_fusion.21), channel_id=1, source_target_pairs={{0,8},{4,12},{8,0},{12,4},{16,24},{20,28},{24,16},{28,20},{1,9},{5... | collective-permute-start | bytes 98312 | tf_op jit(solution)/shard_map/ppermute | solution.py:54
  76.7 26.2 %collective-permute-start.35 = (bf16[128,512]{0,1:T(8,128)(2,1)}, bf16[128,512]{0,1:T(8,128)(2,1)S(1)}, u32[]{:S(2)}, u32[]{:S(2)}) collective-permute-start(bf16[128,512]{0,1:T(8,128)(2,1)} %bitcast.567), channel_id=1, source_target_pairs={{0,4},{4,0},{8,12},{12,8},{16,20},{20,16},{24,28},{28,24},{1,5},{5... | collective-permute-start | bytes 393224 | tf_op jit(solution)/shard_map/ppermute | solution.py:54
  88.1 102.0 %collective-permute-start.27 = (bf16[128,1024]{1,0:T(8,128)(2,1)}, bf16[128,1024]{1,0:T(8,128)(2,1)}, u32[]{:S(2)}, u32[]{:S(2)}) collective-permute-start(bf16[128,1024]{1,0:T(8,128)(2,1)} %get-tuple-element.228), channel_id=1, source_target_pairs={{0,24},{4,28},{8,16},{12,20},{16,8},{20,12},{24,0},{28,4},{1,25},{... | collective-permute-start | bytes 786440 | tf_op jit(solution)/shard_map/ppermute | solution.py:54
  93.2 28.1 %collective-permute-start.26 = (bf16[128,1024]{1,0:T(8,128)(2,1)}, bf16[128,1024]{1,0:T(8,128)(2,1)}, u32[]{:S(2)}, u32[]{:S(2)}) collective-permute-start(bf16[128,1024]{1,0:T(8,128)(2,1)} %get-tuple-element.228), channel_id=1, source_target_pairs={{0,16},{4,20},{8,24},{12,28},{16,0},{20,4},{24,8},{28,12},{1,17},{... | collective-permute-start | bytes 786440 | tf_op jit(solution)/shard_map/ppermute | solution.py:54
  99.8 94.4 %collective-permute-start.28 = (bf16[128,1024]{1,0:T(8,128)(2,1)}, bf16[128,1024]{1,0:T(8,128)(2,1)}, u32[]{:S(2)}, u32[]{:S(2)}) collective-permute-start(bf16[128,1024]{1,0:T(8,128)(2,1)} %get-tuple-element.228), channel_id=1, source_target_pairs={{0,4},{4,0},{8,12},{12,8},{16,20},{20,16},{24,28},{28,24},{1,5},{5... | collective-permute-start | bytes 786440 | tf_op jit(solution)/shard_map/ppermute | solution.py:54
  102.9 21.3 %collective-permute-start = (bf16[128,1024]{1,0:T(8,128)(2,1)S(1)}, bf16[128,1024]{1,0:T(8,128)(2,1)S(1)}, u32[]{:S(2)}, u32[]{:S(2)}) collective-permute-start(bf16[128,1024]{1,0:T(8,128)(2,1)S(1)} %get-tuple-element.232), channel_id=1, source_target_pairs={{0,8},{4,12},{8,0},{12,4},{16,24},{20,28},{24,16},{28,20},{1,9},{5... | collective-permute-start | bytes 786440 | tf_op jit(solution)/shard_map/ppermute | solution.py:54
  108.4 21.2 %collective-permute-start.1 = (bf16[128,1024]{1,0:T(8,128)(2,1)S(1)}, bf16[128,1024]{1,0:T(8,128)(2,1)S(1)}, u32[]{:S(2)}, u32[]{:S(2)}) collective-permute-start(bf16[128,1024]{1,0:T(8,128)(2,1)S(1)} %get-tuple-element.232), channel_id=1, source_target_pairs={{0,16},{4,20},{8,24},{12,28},{16,0},{20,4},{24,8},{28,12},{1,17},{... | collective-permute-start | bytes 786440 | tf_op jit(solution)/shard_map/ppermute | solution.py:54
  151.9 37.7 %collective-permute-start.38 = (bf16[128,512]{0,1:T(8,128)(2,1)}, bf16[128,512]{0,1:T(8,128)(2,1)}, u32[]{:S(2)}, u32[]{:S(2)}) collective-permute-start(bf16[128,512]{0,1:T(8,128)(2,1)} %collective-permute-done.34), channel_id=1, source_target_pairs={{0,4},{4,0},{8,12},{12,8},{16,20},{20,16},{24,28},{28,24},{1,5},{5... | collective-permute-start | bytes 393224 | tf_op jit(solution)/shard_map/ppermute | solution.py:54
  156.8 30.9 %collective-permute-start.37 = (bf16[128,512]{0,1:T(8,128)(2,1)}, bf16[128,512]{0,1:T(8,128)(2,1)}, u32[]{:S(2)}, u32[]{:S(2)}) collective-permute-start(bf16[128,512]{0,1:T(8,128)(2,1)} %collective-permute-done.33), channel_id=1, source_target_pairs={{0,4},{4,0},{8,12},{12,8},{16,20},{20,16},{24,28},{28,24},{1,5},{5... | collective-permute-start | bytes 393224 | tf_op jit(solution)/shard_map/ppermute | solution.py:54
  166.2 34.0 %collective-permute-start.30 = (bf16[128,1024]{1,0:T(8,128)(2,1)}, bf16[128,1024]{1,0:T(8,128)(2,1)}, u32[]{:S(2)}, u32[]{:S(2)}) collective-permute-start(bf16[128,1024]{1,0:T(8,128)(2,1)} %collective-permute-done.26), channel_id=1, source_target_pairs={{0,4},{4,0},{8,12},{12,8},{16,20},{20,16},{24,28},{28,24},{1,5},{5... | collective-permute-start | bytes 786440 | tf_op jit(solution)/shard_map/ppermute | solution.py:54
  220.1 82.6 %collective-permute-start.55 = (bf16[512,1024]{1,0:T(8,128)(2,1)}, bf16[512,1024]{1,0:T(8,128)(2,1)}, u32[]{:S(2)}, u32[]{:S(2)}) collective-permute-start(bf16[512,1024]{1,0:T(8,128)(2,1)} %convolution_convert_fusion), channel_id=1, source_target_pairs={{0,4},{4,0},{8,12},{12,8},{16,20},{20,16},{24,28},{28,24},{1,5},{5... | collective-permute-start | bytes 3145736 | tf_op jit(solution)/shard_map/ppermute | solution.py:54
  223.5 140.3 %collective-permute-start.40 = (bf16[64,1024]{1,0:T(8,128)(2,1)}, bf16[64,1024]{1,0:T(8,128)(2,1)}, u32[]{:S(2)}, u32[]{:S(2)}) collective-permute-start(bf16[64,1024]{1,0:T(8,128)(2,1)} %get-tuple-element.166), channel_id=1, source_target_pairs={{0,2},{1,3},{2,0},{3,1},{4,6},{5,7},{6,4},{7,5},{8,10},{9,11},{10,... | collective-permute-start | bytes 393224 | tf_op jit(solution)/shard_map/ppermute | solution.py:54
  234.9 50.7 %collective-permute-start.60 = (bf16[128,512]{1,0:T(8,128)(2,1)}, bf16[128,512]{1,0:T(8,128)(2,1)}, u32[]{:S(2)}, u32[]{:S(2)}) collective-permute-start(bf16[128,512]{1,0:T(8,128)(2,1)} %get-tuple-element.206), channel_id=1, source_target_pairs={{0,8},{4,12},{8,0},{12,4},{16,24},{20,28},{24,16},{28,20},{1,9},{5... | collective-permute-start | bytes 393224 | tf_op jit(solution)/shard_map/ppermute | solution.py:54
  240.4 45.8 %collective-permute-start.62 = (bf16[128,512]{1,0:T(8,128)(2,1)}, bf16[128,512]{1,0:T(8,128)(2,1)}, u32[]{:S(2)}, u32[]{:S(2)}) collective-permute-start(bf16[128,512]{1,0:T(8,128)(2,1)} %get-tuple-element.207), channel_id=1, source_target_pairs={{0,24},{4,28},{8,16},{12,20},{16,8},{20,12},{24,0},{28,4},{1,25},{... | collective-permute-start | bytes 393224 | tf_op jit(solution)/shard_map/ppermute | solution.py:54
  242.3 44.0 %collective-permute-start.61 = (bf16[128,512]{1,0:T(8,128)(2,1)}, bf16[128,512]{1,0:T(8,128)(2,1)}, u32[]{:S(2)}, u32[]{:S(2)}) collective-permute-start(bf16[128,512]{1,0:T(8,128)(2,1)} %get-tuple-element.208), channel_id=1, source_target_pairs={{0,16},{4,20},{8,24},{12,28},{16,0},{20,4},{24,8},{28,12},{1,17},{... | collective-permute-start | bytes 393224 | tf_op jit(solution)/shard_map/ppermute | solution.py:54
  285.6 36.1 %collective-permute-start.51 = (bf16[512,512]{1,0:T(8,128)(2,1)}, bf16[512,512]{1,0:T(8,128)(2,1)S(1)}, u32[]{:S(2)}, u32[]{:S(2)}) collective-permute-start(bf16[512,512]{1,0:T(8,128)(2,1)} %convolution_convert_fusion.3), channel_id=1, source_target_pairs={{0,4},{4,0},{8,12},{12,8},{16,20},{20,16},{24,28},{28,24},{1,5},{5... | collective-permute-start | bytes 1572872 | tf_op jit(solution)/shard_map/ppermute | solution.py:54
  311.7 41.4 %collective-permute-start.45 = (f32[2,64,1024]{2,1,0:T(8,128)}, f32[2,64,1024]{2,1,0:T(8,128)}, u32[]{:S(2)}, u32[]{:S(2)}) collective-permute-start(f32[2,64,1024]{2,1,0:T(8,128)} %pad_maximum_fusion.8), channel_id=1, source_target_pairs={{0,1},{1,0},{2,3},{3,2},{4,5},{5,4},{6,7},{7,6},{8,9},{9,8},{10,11... | collective-permute-start | bytes 1572872 | tf_op jit(solution)/shard_map/ppermute | solution.py:54
  321.7 21.1 %collective-permute-start.57 = (bf16[128,1024]{1,0:T(8,128)(2,1)}, bf16[128,1024]{1,0:T(8,128)(2,1)}, u32[]{:S(2)}, u32[]{:S(2)}) collective-permute-start(bf16[128,1024]{1,0:T(8,128)(2,1)} %get-tuple-element.190), channel_id=1, source_target_pairs={{0,16},{4,20},{8,24},{12,28},{16,0},{20,4},{24,8},{28,12},{1,17},{... | collective-permute-start | bytes 786440 | tf_op jit(solution)/shard_map/ppermute | solution.py:54
  345.1 27.1 %collective-permute-start.47 = (bf16[512,1024]{1,0:T(8,128)(2,1)}, bf16[512,1024]{1,0:T(8,128)(2,1)}, u32[]{:S(2)}, u32[]{:S(2)}) collective-permute-start(bf16[512,1024]{1,0:T(8,128)(2,1)} %convolution_convert_fusion.1), channel_id=1, source_target_pairs={{0,4},{4,0},{8,12},{12,8},{16,20},{20,16},{24,28},{28,24},{1,5},{5... | collective-permute-start | bytes 3145736 | tf_op jit(solution)/shard_map/ppermute | solution.py:54
  377.2 23.3 %collective-permute-start.49 = (bf16[128,1024]{1,0:T(8,128)(2,1)}, bf16[128,1024]{1,0:T(8,128)(2,1)S(1)}, u32[]{:S(2)}, u32[]{:S(2)}) collective-permute-start(bf16[128,1024]{1,0:T(8,128)(2,1)} %get-tuple-element.193), channel_id=1, source_target_pairs={{0,16},{4,20},{8,24},{12,28},{16,0},{20,4},{24,8},{28,12},{1,17},{... | collective-permute-start | bytes 786440 | tf_op jit(solution)/shard_map/ppermute | solution.py:54
  (159 other events, 1538.3 us)

commit v2 on v1

v2 whole, which is shorter than its diff:
```python
import functools
import math

import jax
import jax.numpy as jnp
from jax import lax
from jax.experimental import pallas as pl
from jax.experimental.pallas import tpu as pltpu
from jax.sharding import PartitionSpec as P

HDM = 64
NSTATE = 128
QH = 8
KVH = 2
HD = 64


EPSILON = 1e-05
FLOAT = jnp.float32
BFLOAT = jnp.bfloat16
WHOLE = pl.BlockSpec()


def rms_norm(values, scale_vec):
    return (
        values * lax.rsqrt(jnp.mean(values * values, axis=-1, keepdims=True) + EPSILON) * scale_vec
    )


def einsum_f32(pattern, op_left, op_right):
    return jnp.einsum(pattern, op_left, op_right, preferred_element_type=jnp.float32)


def silu_gate(gate_proj, up_proj):
    return jax.nn.silu(gate_proj) * up_proj


def swap(values, axis, count, bits):
    return lax.ppermute(values, axis, [(i, i ^ bits) for i in range(count)])


def stages_of(count):
    top = count.bit_length() - 1
    groups = []
    while top > 0:
        low = max(0, top - 2)
        groups.append([m << low for m in range(1, 1 << (top - low))])
        top = low
    return groups


def block_order(count):
    order = [0]
    for group in stages_of(count):
        order = order + [r ^ m for m in group for r in order]
    return order


def relocate_kernel(order, to_relative, index_ref, *refs):
    for source, target in zip(refs[: len(refs) // 2], refs[len(refs) // 2 :]):
        block = source.shape[1] // len(order)
        for k, r in enumerate(order):
            here = slice(k * block, (k + 1) * block)
            there = pl.ds(pl.multiple_of((index_ref[0] ^ r) * block, block), block)
            if to_relative:
                target[:, here] = source[:, there]
            else:
                target[:, there] = source[:, here]


def relocate(arrays, index, count, to_relative):
    order = block_order(count)
    if arrays[0].shape[1] // count % 128 == 0:
        return call(
            functools.partial(relocate_kernel, order, to_relative),
            [(a.shape, a.dtype) for a in arrays],
            index[None],
            *arrays,
        )
    places = jnp.array(order, jnp.int32) ^ index
    if not to_relative:
        places = jnp.argsort(places)
    moved = [a.reshape(a.shape[0], count, -1)[:, places].reshape(a.shape) for a in arrays]
    return moved


def together(*values):
    return lax.optimization_barrier(values)


def stack_kernel(*refs):
    *parts, out_ref = refs
    start = 0
    for part in parts:
        out_ref[start : start + part.shape[0], :] = part[...]
        start += part.shape[0]


def stacked(parts):
    rows = sum(p.shape[0] for p in parts)
    return pl.pallas_call(
        stack_kernel,
        out_shape=jax.ShapeDtypeStruct((rows, parts[0].shape[1]), parts[0].dtype),
        in_specs=[WHOLE] * len(parts),
        out_specs=WHOLE,
        compiler_params=pltpu.CompilerParams(vmem_limit_bytes=16 * 1024 * 1024),
        cost_estimate=pl.CostEstimate(flops=1000, bytes_accessed=1000, transcendentals=0),
    )(*parts)


def gather(stack, have, groups, count):
    parts, places = [stack], [have]
    for k, group in enumerate(groups):
        if k > 0:
            stack = stacked(parts)
            have = [r for p in places for r in p]
        parts = [stack] + [swap(stack, "dp", count, m) for m in group]
        places = [have] + [[r ^ m for r in have] for m in group]
    return parts, places


def joined(parts, places):
    return stacked(parts), [r for p in places for r in p]


def two(parts, places):
    far = parts[1] if len(parts) == 2 else stacked(parts[1:])
    return (parts[0], far), places


def column_runs(places, order):
    found = []
    for have in places:
        runs = []
        for row, r in enumerate(have):
            col = order.index(r)
            if runs and runs[-1][0] + runs[-1][2] == col:
                runs[-1] = (runs[-1][0], runs[-1][1], runs[-1][2] + 1)
            else:
                runs.append((col, row, 1))
        found.append(runs)
    return found


def products_kernel(runs_of, block, widths, *refs):
    lefts, rights, outs = refs[: len(widths)], refs[len(widths) : 2 * len(widths)], refs[2 * len(widths) :]
    start = 0
    for left, right, width in zip(lefts, rights, widths):
        right_now = right[...]
        for out, runs in zip(outs, runs_of):
            row = 0
            for col, n in runs:
                found = dot(left[:, col * block : (col + n) * block], right_now, 0, 0)
                out[row * block : (row + n) * block, start : start + width] = found.astype(out.dtype)
                row += n
        start += width


def parted(pairs, order, group):
    block = pairs[0][0].shape[1] // len(order)
    span = 0
    for m in group:
        span |= m
    stay = [r for r in order if r & span == 0]
    runs_of = []
    for blocks in [stay] + [[r ^ m for r in stay] for m in group]:
        runs = []
        for r in blocks:
            col = order.index(r)
            if runs and sum(runs[-1]) == col:
                runs[-1] = (runs[-1][0], runs[-1][1] + 1)
            else:
                runs.append((col, 1))
        runs_of.append(runs)
    widths = [right.shape[1] for _, right in pairs]
    shape = (len(stay) * block, sum(widths))
    kept, *sent = pl.pallas_call(
        functools.partial(products_kernel, runs_of, block, widths),
        out_shape=[jax.ShapeDtypeStruct(shape, FLOAT)]
        + [jax.ShapeDtypeStruct(shape, BFLOAT)] * len(group),
        in_specs=[WHOLE] * (2 * len(pairs)),
        out_specs=[WHOLE] * (1 + len(group)),
        compiler_params=pltpu.CompilerParams(vmem_limit_bytes=16 * 1024 * 1024),
        cost_estimate=pl.CostEstimate(flops=1000, bytes_accessed=1000, transcendentals=0),
    )(*[left for left, _ in pairs], *[right for _, right in pairs])
    return kept, sent, stay


def send(sent, group, count):
    return [swap(part, "dp", count, m) for m, part in zip(group, sent)]


def add(kept, got):
    for part in got:
        kept = kept + part.astype(FLOAT)
    return kept


def split(total, order, group, sizes):
    span = 0
    for m in group:
        span |= m
    stay = [r for r in order if r & span == 0]

    def rows(blocks):
        parts = []
        start = 0
        for size in sizes:
            parts += [total[start + order.index(r) * size :][:size] for r in blocks]
            start += size * len(order)
        return jnp.concatenate(parts, axis=0)

    return rows(stay), [rows([r ^ m for r in stay]).astype(BFLOAT) for m in group], stay


def finish(total, order, groups, count, sizes=None):
    if sizes is None:
        sizes = [total.shape[0] // len(order)]
    kept, got = total, []
    for group in groups:
        kept, sent, order = split(add(kept, got), order, group, sizes)
        got = send(sent, group, count)
    return kept, got


def dot(left, right, left_dim=1, right_dim=0):
    return lax.dot_general(
        left, right, (((left_dim,), (right_dim,)), ((), ())), preferred_element_type=FLOAT
    )


def exact_dot(left, right):
    return jnp.dot(left, right, precision=lax.Precision.HIGHEST, preferred_element_type=FLOAT)


def sigmoid(values):
    return 1.0 / (1.0 + jnp.exp(-values))


def softplus(values):
    return jnp.maximum(values, 0.0) + jnp.log1p(jnp.exp(-jnp.abs(values)))


def lanes_of(shape):
    return lax.broadcasted_iota(jnp.int32, shape, 1)


def same_document(seg_wide, offset):
    if offset == 0:
        return None
    row = lax.broadcasted_iota(jnp.int32, seg_wide.shape, 0)
    same = jnp.logical_and(pltpu.roll(seg_wide, offset, 0) == seg_wide, row >= offset)
    return jnp.where(same, 1.0, 0.0)


def square_mask(seg_wide, seg_row):
    length = seg_wide.shape[0]
    row = lax.broadcasted_iota(jnp.int32, (length, length), 0)
    col = lax.broadcasted_iota(jnp.int32, (length, length), 1)
    wide = jnp.concatenate([seg_wide] * (length // 128), axis=1)
    return jnp.logical_and(row >= col, wide == seg_row[0:1, :])


def triangle(length, flip):
    row = lax.broadcasted_iota(jnp.int32, (length, length), 0)
    col = lax.broadcasted_iota(jnp.int32, (length, length), 1)
    return jnp.where(row <= col if flip else row >= col, 1.0, 0.0)


def head_lanes(values, head, lane):
    return jnp.where((lane >= HDM) == (head == 1), values, jnp.zeros_like(values))


def softmax_of(queries, keys, mask, head, lane):
    scores = dot(head_lanes(queries, head, lane), keys, 1, 1) * (1.0 / math.sqrt(HD))
    masked = jnp.where(mask, scores, -1000000000.0)
    grown = jnp.exp(masked - jnp.max(masked, axis=-1, keepdims=True))
    return grown / jnp.sum(grown, axis=-1, keepdims=True)


def views(ref, widths):
    found = []
    start = 0
    for width in widths:
        found.append(ref.at[:, start : start + width])
        start += width
    return found


def kept_views(ref, width):
    return views(ref, (width + 256, width + 256, 128, 128, ref.shape[0]))


def low_views(ref, width):
    return views(ref, (width + 256, 128, 256))


def mixer_kernel(
    heads, owner_ref, normed_ref, near_ref, far_ref, shared_ref, taps_ref, head_ref, seg_ref, seg_row_ref,
    kept_ref, low_ref, pre_gate_ref, attn_ref,
):
    conv_in_ref, conv_pre_ref, step_ref, decay_ref, gram_ref = kept_views(kept_ref, pre_gate_ref.shape[1])
    conv_low_ref, query_ref, kv_ref = low_views(low_ref, pre_gate_ref.shape[1])
    length = normed_ref.shape[0]
    half = near_ref.shape[0]
    width = pre_gate_ref.shape[1]
    conv_width = conv_in_ref.shape[1]
    normed = normed_ref[...]
    taps = taps_ref[...]
    seg = seg_ref[...]
    mask = square_mask(seg, seg_row_ref[...])
    lead = dot(normed[:, :half], near_ref[:, 128:]) + dot(normed[:, half:], far_ref[:, 128:])
    x_raw = lead[:, 256:]
    shared = dot(normed, shared_ref[...]).astype(BFLOAT)
    queries = lead[:, :128].astype(BFLOAT)
    query_ref[...] = queries
    lane = lanes_of((length, 128))
    keep_half = (lane >= HD) == (owner_ref[0] == 1)
    shared_f = shared.astype(FLOAT)
    keys = jnp.where(keep_half, shared_f[:, :128], pltpu.roll(shared_f[:, :128], HD, 1)).astype(BFLOAT)
    values = jnp.where(keep_half, shared_f[:, 128:256], pltpu.roll(shared_f[:, 128:256], HD, 1)).astype(BFLOAT)
    kv_ref[:, :128] = keys
    kv_ref[:, 128:] = values
    outs = [dot(softmax_of(queries, keys, mask, h, lane).astype(BFLOAT), values) for h in range(2)]
    attn_ref[...] = jnp.where(lane < HD, outs[0], outs[1]).astype(BFLOAT)
    step_pre = lead[:, 128:256] + head_ref[0:1, :]
    step_ref[...] = step_pre
    step_size = softplus(step_pre)
    decay = exact_dot(triangle(length, False), step_size * -jnp.exp(head_ref[1:2, :]))
    decay_ref[...] = decay
    sames = [same_document(seg, o) for o in range(4)]
    for start in range(0, conv_width, 128):
        cols = slice(start, start + 128)
        if start < width:
            u = x_raw[:, cols]
        else:
            u = shared_f[:, 256 + start - width : 256 + start - width + 128]
        conv_in_ref[:, cols] = u
        pre = taps[4:5, cols] + taps[3:4, cols] * u
        for o in range(1, 4):
            pre = pre + taps[3 - o : 4 - o, cols] * (pltpu.roll(u, o, 0) * sames[o])
        conv_pre_ref[:, cols] = pre
        conv_low_ref[:, cols] = (pre * sigmoid(pre)).astype(BFLOAT)
    b_state = conv_low_ref[:, width : width + 128]
    c_state = conv_low_ref[:, width + 128 :]
    gram = dot(c_state, b_state, 1, 1)
    gram_ref[...] = gram
    step_rows, decay_rows = step_size.T, decay.T
    for pair in range(heads // 2):
        cols = slice(128 * pair, 128 * pair + 128)
        x_pair = conv_low_ref[:, cols]
        found = []
        for h in (2 * pair, 2 * pair + 1):
            gap = decay[:, h : h + 1] - decay_rows[h : h + 1, :]
            grown = jnp.where(mask, jnp.exp(jnp.where(mask, gap, 0.0)), 0.0)
            found.append(dot((gram * grown * step_rows[h : h + 1, :]).astype(BFLOAT), x_pair))
        y_pair = jnp.where(lane < HDM, found[0], found[1])
        pre_gate_ref[:, cols] = y_pair + taps[5:6, cols] * x_pair.astype(FLOAT)


def pieces_of(terms, at_core, axis):
    size = terms.shape[axis] // 4
    blocks = [lax.slice_in_dim(terms, k * size, (k + 1) * size, axis=axis) for k in range(4)]
    keep = [jnp.where(at_core, blocks[2 * y], blocks[2 * y + 1]) for y in range(2)]
    give = [jnp.where(at_core, blocks[2 * y + 1], blocks[2 * y]) for y in range(2)]
    return keep, give


def gate_kernel(
    core_ref, normed_ref, near_ref, far_ref, pre_gate_ref, attn_ref, gates_ref, mixed_ref, keep_ref, give_ref
):
    half = near_ref.shape[0]
    width = pre_gate_ref.shape[1]
    normed = normed_ref[...]
    gate_z = dot(normed[:, :half], near_ref[:, :width]) + dot(normed[:, half:], far_ref[:, :width])
    gates_ref[:, :width] = gate_z
    gates_ref[:, width:] = pre_gate_ref[...]
    gated = (pre_gate_ref[...] * (gate_z * sigmoid(gate_z))).astype(BFLOAT)
    mixed_ref[:, :width] = gated
    mixed_ref[:, width:] = attn_ref[...]
    mixed = mixed_ref[...]
    at_core = core_ref[0] == 0
    start = 0
    for part in (near_ref, far_ref):
        terms = dot(mixed, part[:, width:], 1, 1)
        cols = slice(start, start + part.shape[0])
        start += part.shape[0]
        keep, give = pieces_of(terms, at_core, 0)
        for y in range(2):
            keep_ref[y, :, cols] = keep[y]
            give_ref[y, :, cols] = give[y]


def input_back_kernel(
    core_ref, in_low_ref, zq_ref, block_ref, early_near_ref, early_far_ref, near_ref, far_ref,
    shared_ref, keep_ref, give_ref,
):
    width = zq_ref.shape[1] - 128
    x_low, step_low = in_low_ref[:, :width], in_low_ref[:, width:]
    z_low, query_low = zq_ref[:, :width], zq_ref[:, width:]
    block = block_ref[...]
    at_core = core_ref[0] == 0
    start = 0
    for early, part in ((early_near_ref, near_ref), (early_far_ref, far_ref)):
        cols = slice(start, start + part.shape[0])
        start += part.shape[0]
        terms = (
            dot(x_low, early[:, 384:], 1, 1)
            + dot(query_low, early[:, 128:256], 1, 1)
            + dot(step_low, early[:, 256:384], 1, 1)
            + dot(z_low, part[:, :width], 1, 1)
            + dot(block, shared_ref[cols, :], 1, 1)
        )
        keep, give = pieces_of(terms, at_core, 0)
        for y in range(2):
            keep_ref[y, :, cols] = keep[y]
            give_ref[y, :, cols] = give[y]


def gate_back_kernel(
    owner_ref, grad_ref, near_ref, far_ref, gates_ref, low_ref, seg_ref, seg_row_ref,
    zq_ref, pre_grad_ref, skip_ref, kv_grad_ref,
):
    half = near_ref.shape[0]
    width = pre_grad_ref.shape[1]
    conv_low_ref, query_ref, kv_ref = low_views(low_ref, width)
    grad = grad_ref[...]
    mixed_grad = dot(grad[:, :half], near_ref[:, width:]) + dot(grad[:, half:], far_ref[:, width:])
    gated_grad = mixed_grad[:, :width]
    gate_z = gates_ref[:, :width]
    s = sigmoid(gate_z)
    pre_grad = gated_grad * (gate_z * s)
    pre_grad_ref[...] = pre_grad
    zq_ref[:, :width] = (gated_grad * gates_ref[:, width:] * (s * (1.0 + gate_z * (1.0 - s)))).astype(BFLOAT)
    skip = jnp.sum(pre_grad * conv_low_ref[:, :width].astype(FLOAT), axis=0, keepdims=True)
    row = lax.broadcasted_iota(jnp.int32, (width, 128), 0)
    col = lax.broadcasted_iota(jnp.int32, (width, 128), 1)
    of_head = jnp.where(jnp.logical_and(row >= col * HDM, row < (col + 1) * HDM), 1.0, 0.0)
    skip_ref[...] = exact_dot(jnp.broadcast_to(skip, (8, width)), of_head)
    lane = lanes_of((grad.shape[0], 128))
    out_low = mixed_grad[:, width:].astype(BFLOAT)
    mask = square_mask(seg_ref[...], seg_row_ref[...])
    queries, keys, values = query_ref[...], kv_ref[:, :128], kv_ref[:, 128:]
    query_grads, key_sum, value_sum = [], 0.0, 0.0
    for h in range(2):
        probs = softmax_of(queries, keys, mask, h, lane)
        out_head = head_lanes(out_low, h, lane)
        prob_grad = dot(out_head, values, 1, 1)
        score = probs * (prob_grad - jnp.sum(probs * prob_grad, axis=-1, keepdims=True))
        score_low = score.astype(BFLOAT)
        query_grads.append(dot(score_low, keys))
        key_sum = key_sum + dot(score_low, head_lanes(queries, h, lane), 0, 0)
        value_sum = value_sum + dot(probs.astype(BFLOAT), out_head, 0, 0)
    scale = 1.0 / math.sqrt(HD)
    zq_ref[:, width:] = (jnp.where(lane < HD, query_grads[0], query_grads[1]) * scale).astype(BFLOAT)
    mine = (lane >= HD) == (owner_ref[0] == 1)
    for k, total in enumerate((key_sum * scale, value_sum)):
        both = total + pltpu.roll(total, HD, 1)
        kv_grad_ref[:, 128 * k : 128 * k + 128] = jnp.where(mine, both, 0.0)


def mixer_back_kernel(
    heads, owner_ref, pre_grad_ref, kept_ref, low_ref, kv_grad_ref, taps_ref, head_ref, seg_ref, seg_row_ref,
    in_low_ref, taps_grad_ref, head_grad_ref, share_ref, act_grad_ref,
):
    conv_in_ref, conv_pre_ref, step_ref, decay_ref, gram_ref = kept_views(kept_ref, pre_grad_ref.shape[1])
    conv_low_ref = low_views(low_ref, pre_grad_ref.shape[1])[0]
    length = pre_grad_ref.shape[0]
    width = pre_grad_ref.shape[1]
    conv_width = conv_in_ref.shape[1]
    taps = taps_ref[...]
    seg = seg_ref[...]
    mask = square_mask(seg, seg_row_ref[...])
    lane = lanes_of((length, 128))
    step_pre = step_ref[...]
    step_size = softplus(step_pre)
    decay = decay_ref[...]
    step_rows, decay_rows = step_size.T, decay.T
    gram = gram_ref[...]
    b_state = conv_low_ref[:, width : width + 128]
    c_state = conv_low_ref[:, width + 128 :]
    b_grad, c_grad = 0.0, 0.0
    step_grad_rows, row_sums = [], jnp.zeros((length, 128), FLOAT)
    for pair in range(heads // 2):
        cols = slice(128 * pair, 128 * pair + 128)
        x_pair = conv_low_ref[:, cols]
        pre_grad = pre_grad_ref[:, cols]
        y_pair = pre_grad.astype(BFLOAT)
        found = []
        for k in range(2):
            h = 2 * pair + k
            gap = decay[:, h : h + 1] - decay_rows[h : h + 1, :]
            grown = jnp.where(mask, jnp.exp(jnp.where(mask, gap, 0.0)), 0.0)
            step_row = step_rows[h : h + 1, :]
            y_head = head_lanes(y_pair, k, lane)
            weights_grad = dot(y_head, x_pair, 1, 1)
            shaped = weights_grad * grown
            gram_grad = (shaped * step_row).astype(BFLOAT)
            c_grad = c_grad + dot(gram_grad, b_state)
            b_grad = b_grad + dot(gram_grad, c_state, 0, 0)
            terms = shaped * gram
            step_grad_rows.append(jnp.sum(terms, axis=0, keepdims=True))
            sums = jnp.sum(terms * step_row, axis=1, keepdims=True)
            row_sums = jnp.where(lane == h, sums, row_sums)
            weights_low = (gram * grown * step_row).astype(BFLOAT)
            found.append(dot(weights_low, y_head, 0, 0))
        x_grad = pre_grad * taps[5:6, cols] + jnp.where(lane < HDM, found[0], found[1])
        act_grad_ref[:, cols] = x_grad
    act_grad_ref[:, width : width + 128] = b_grad
    act_grad_ref[:, width + 128 :] = c_grad
    step_grad = jnp.concatenate(
        step_grad_rows + [jnp.zeros((128 - heads, length), FLOAT)], axis=0
    ).T
    rate = -jnp.exp(head_ref[1:2, :])
    back_sum = exact_dot(triangle(length, True), row_sums - step_grad * step_size)
    raw_grad = (step_grad + rate * back_sum) * sigmoid(step_pre)
    raw_grad = jnp.where(lane < heads, raw_grad, 0.0)
    in_low_ref[:, width:] = raw_grad.astype(BFLOAT)
    head_grad_ref[0:1, :] = jnp.sum(raw_grad, axis=0, keepdims=True)
    head_grad_ref[1:2, :] = jnp.sum(rate * step_size * back_sum, axis=0, keepdims=True)
    head_grad_ref[2:8, :] = jnp.zeros((6, 128), FLOAT)
    sames = [same_document(seg, o) for o in range(4)]
    share_ref[:, :256] = kv_grad_ref[...]
    for start in range(0, conv_width, 128):
        cols = slice(start, start + 128)
        pre = conv_pre_ref[:, cols]
        s = sigmoid(pre)
        a = act_grad_ref[:, cols] * (s * (1.0 + pre * (1.0 - s)))
        u = conv_in_ref[:, cols]
        raw = taps[3:4, cols] * a
        taps_grad_ref[3:4, cols] = jnp.sum(a * u, axis=0, keepdims=True)
        taps_grad_ref[4:5, cols] = jnp.sum(a, axis=0, keepdims=True)
        for o in range(1, 4):
            masked = a * sames[o]
            raw = raw + taps[3 - o : 4 - o, cols] * pltpu.roll(masked, length - o, 0)
            taps_grad_ref[3 - o : 4 - o, cols] = jnp.sum(
                masked * pltpu.roll(u, o, 0), axis=0, keepdims=True
            )
        if start < width:
            in_low_ref[:, cols] = raw.astype(BFLOAT)
        else:
            share_ref[:, 256 + start - width : 256 + start - width + 128] = raw
    taps_grad_ref[5:8, :] = jnp.zeros((3, conv_width), FLOAT)


def call(kernel, outs, scalar, *arrays, scratch=()):
    return pl.pallas_call(
        kernel,
        out_shape=[jax.ShapeDtypeStruct(shape, dtype) for shape, dtype in outs],
        in_specs=[pl.BlockSpec(memory_space=pltpu.SMEM)]
        + [WHOLE] * len(arrays),
        out_specs=[WHOLE] * len(outs),
        scratch_shapes=list(scratch),
        compiler_params=pltpu.CompilerParams(vmem_limit_bytes=16 * 1024 * 1024),
        cost_estimate=pl.CostEstimate(flops=1000, bytes_accessed=1000, transcendentals=0),
    )(scalar, *arrays)


def finish_tensor(keep, give, index):
    sums = keep + swap(give, "tensor", 4, 1)
    half = index >> 1
    mine = jnp.where(half == 0, sums[0], sums[1])
    other = jnp.where(half == 0, sums[1], sums[0])
    return mine + swap(other.astype(BFLOAT), "tensor", 4, 2).astype(FLOAT)


def sum_tensor(partial, index):
    keep, give = pieces_of(partial, index & 1 == 0, 0)
    return finish_tensor(jnp.stack(keep), jnp.stack(give), index)


def ffn_kernel(
    gu_runs, down_runs, core_ref, rows_ref, cot_ref, *refs
):
    gu_refs, refs = refs[: len(gu_runs)], refs[len(gu_runs) :]
    down_refs, refs = refs[: len(down_runs)], refs[len(down_runs) :]
    gu_low_ref, act_ref, keep_ref, give_ref, out_keep_ref, out_give_ref = refs
    width = act_ref.shape[1]
    block = sum(n for runs in gu_runs for _, _, n in runs)
    block = rows_ref.shape[1] // block

    def inner(left_ref, parts, found):
        total = 0.0
        for part, runs in zip(parts, found):
            for col, row, n in runs:
                total = total + dot(
                    left_ref[:, col * block : (col + n) * block], part[row * block : (row + n) * block, :]
                )
        return total

    def outer(left, parts, found, to_keep, to_give):
        for part, runs in zip(parts, found):
            for col, row, n in runs:
                terms = dot(left, part[row * block : (row + n) * block, :], 1, 1)
                keep, give = pieces_of(terms, at_core, 0)
                for y in range(2):
                    to_keep[y, :, col * block : (col + n) * block] = keep[y]
                    to_give[y, :, col * block : (col + n) * block] = give[y]

    at_core = core_ref[0] == 0
    gate_up = inner(rows_ref, gu_refs, gu_runs)
    gate_proj, up_proj = gate_up[:, :width], gate_up[:, width:]
    s = sigmoid(gate_proj)
    silu = gate_proj * s
    act = (silu * up_proj).astype(BFLOAT)
    act_ref[...] = act
    act_grad = inner(cot_ref, down_refs, down_runs)
    gu_low_ref[:, :width] = (act_grad * up_proj * (s * (1.0 + gate_proj * (1.0 - s)))).astype(BFLOAT)
    gu_low_ref[:, width:] = (act_grad * silu).astype(BFLOAT)
    outer(gu_low_ref[...], gu_refs, gu_runs, keep_ref, give_ref)
    outer(act, down_refs, down_runs, out_keep_ref, out_give_ref)


def gather_tensor(values):
    return lax.all_gather(values, "tensor", axis=0, tiled=True)


def group_sum(values, axis, axis_count, bits):
    parts = [values] + [swap(values, axis, axis_count, m) for m in bits]
    while len(parts) > 1:
        parts = [parts[k] + parts[k + 1] for k in range(0, len(parts), 2)]
    return parts[0]


def per_device(
    count,
    tokens,
    segments,
    zx_weight,
    dt_weight,
    query_weight,
    ssm_out_weight,
    attn_out_weight,
    gate_up_weight,
    down_weight,
    shared_weight,
    norm_gains,
    conv_params,
    head_params,
    cotangent,
):
    shard_index = lax.axis_index("tensor")
    dp_index = lax.axis_index("dp")
    length = segments.shape[0]
    rows = zx_weight.shape[1]
    head_local = dt_weight.shape[1]
    width_local = zx_weight.shape[2]
    query_cols = query_weight.shape[1]
    query_local = query_cols // HD
    ff_local = down_weight.shape[0]
    share_rows = shared_weight.shape[0]
    share_cols = shared_weight.shape[1]

    token_rel, cot_local = relocate([tokens, cotangent], dp_index, count, True)
    token_f = token_rel.astype(FLOAT)
    gains = relocate([norm_gains], dp_index, count, True)[0]
    normed_one, norm_one_back = jax.vjp(rms_norm, token_f, gains[0])
    normed_rows = gather_tensor(normed_one.astype(BFLOAT))
    cot_rows = gather_tensor(cot_local)

    shared_pack = shared_weight.reshape(share_rows, 4, share_cols // 4)
    shared_pack = jnp.concatenate([shared_pack[:, k] for k in range(4)], axis=0)
    dt_pad = jnp.pad(dt_weight, ((0, 0), (0, 128 - head_local)))
    groups = stages_of(count)
    first, last = groups[:-1], groups[-1:]
    order = block_order(count)
    lead_piece = jnp.concatenate([shared_pack, query_weight, dt_pad, zx_weight[1]], axis=1)
    mid_piece = jnp.concatenate([zx_weight[0], ssm_out_weight.T, attn_out_weight.T], axis=1)
    gu_piece = jnp.concatenate([gate_up_weight[0], gate_up_weight[1]], axis=1)
    down_half, down_have = joined(*gather(down_weight.T, [0], last, count))
    early_half, have = joined(*gather(lead_piece, [0], first, count))
    early_half, down_half, mid_piece, normed_rows = lax.optimization_barrier(
        (early_half, down_half, mid_piece, normed_rows)
    )
    (early_near, early_far), _ = two(*gather(early_half, have, last, count))
    mid_half, _ = joined(*gather(mid_piece, [0], first, count))
    mid_half, early_far, gu_piece, cot_rows = lax.optimization_barrier(
        (mid_half, early_far, gu_piece, cot_rows)
    )
    (mid_near, mid_far), _ = two(*gather(mid_half, have, last, count))
    gu_half, _ = joined(*gather(gu_piece, [0], first, count))
    gu_half, mid_far, down_half = lax.optimization_barrier((gu_half, mid_far, down_half))
    gu_parts, gu_places = gather(gu_half, have, last, count)
    down_parts, down_places = gather(down_half, down_have, first, count)
    shared_got = jnp.concatenate([early_near[:, :128], early_far[:, :128]], axis=0)
    shared_got = shared_got.reshape(count, 4, share_rows, share_cols // 4)
    shared_got = jnp.concatenate([shared_got[:, k] for k in range(4)], axis=-1)
    near = jnp.stack([shared_got, swap(shared_got, "tensor", 4, 2)])
    both = jnp.stack([near, swap(near, "tensor", 4, 1)])
    both = jnp.where(shard_index & 1 == 1, both[::-1], both)
    both = jnp.where(shard_index >> 1 == 1, both[:, ::-1], both)
    shared_full = both.transpose(2, 1, 0, 3, 4).reshape(count * rows, share_cols)

    head_mine = lax.dynamic_slice_in_dim(head_params, shard_index * head_local, head_local, 1)
    bc_start = conv_params.shape[1] - 2 * NSTATE
    conv_mine = jnp.concatenate(
        [
            lax.dynamic_slice_in_dim(conv_params, shard_index * width_local, width_local, 1),
            conv_params[:, bc_start:],
        ],
        axis=1,
    )
    conv_width = width_local + 2 * NSTATE
    taps = jnp.concatenate([conv_mine, jnp.pad(jnp.repeat(head_mine[2], HDM), (0, 2 * NSTATE))[None]], axis=0)
    taps = jnp.pad(taps, ((0, 8 - taps.shape[0]), (0, 0)))
    head_pack = jnp.pad(head_mine, ((0, 5), (0, 128 - head_local)))
    seg_wide = jnp.broadcast_to(segments.astype(FLOAT)[:, None], (length, 128))
    seg_row = jnp.broadcast_to(segments.astype(FLOAT)[None], (8, length))
    core = (shard_index & 1)[None]
    owner = ((shard_index * query_local) // (QH // KVH))[None]
    width_full = count * rows
    kept_width = 2 * conv_width + 256 + length
    low_width = conv_width + 128 + 256
    mixer_kept, mixer_low, pre_gate, attn_low = call(
        functools.partial(mixer_kernel, head_local),
        [
            ((length, kept_width), FLOAT),
            ((length, low_width), BFLOAT),
            ((length, width_local), FLOAT),
            ((length, 128), BFLOAT),
        ],
        owner,
        normed_rows,
        early_near,
        early_far,
        shared_full,
        taps,
        head_pack,
        seg_wide,
        seg_row,
    )
    halves = ((2, length // 4, width_full), FLOAT)
    gates, mixed_low, keep, give = call(
        gate_kernel,
        [((length, 2 * width_local), FLOAT), ((length, width_local + 128), BFLOAT), halves, halves],
        core,
        normed_rows,
        mid_near,
        mid_far,
        pre_gate,
        attn_low,
    )
    hidden = token_f + finish_tensor(keep, give, shard_index)
    normed_two, norm_two_back = jax.vjp(rms_norm, hidden, gains[1])
    ffn_rows = gather_tensor(normed_two.astype(BFLOAT))
    gu_low, act_low, keep, give, out_keep, out_give = call(
        functools.partial(ffn_kernel, column_runs(gu_places, order), column_runs(down_places, order)),
        [((length, 2 * ff_local), BFLOAT), ((length, ff_local), BFLOAT), halves, halves, halves, halves],
        core,
        ffn_rows,
        cot_rows,
        *gu_parts,
        *down_parts,
    )
    normed_two_grad = finish_tensor(keep, give, shard_index)
    hidden_norm_grad, gain_two_grad = norm_two_back(normed_two_grad)
    hidden_grad = cot_local.astype(FLOAT) + hidden_norm_grad
    mix_grad_rows = gather_tensor(hidden_grad.astype(BFLOAT))
    last_group = last[0]
    back = groups[:-1][::-1]
    down_kept, down_sent, down_stay = parted([(cot_rows, act_low)], order, back[0])
    gu_kept, gu_sent, stay = parted([(ffn_rows, gu_low)], order, last_group)
    gu_sent, down_sent = together(gu_sent, down_sent)
    gu_half_sum = add(gu_kept, send(gu_sent, last_group, count))
    down_half_sum = add(down_kept, send(down_sent, back[0], count))
    gu_half_sum, down_half_sum, mix_grad_rows = lax.optimization_barrier(
        (gu_half_sum, down_half_sum, mix_grad_rows)
    )
    gu_kept, gu_got = finish(gu_half_sum, stay, back, count)
    zq_low, pre_grad, skip_lanes, kv_grad = call(
        gate_back_kernel,
        [
            ((length, width_local + 128), BFLOAT),
            ((length, width_local), FLOAT),
            ((8, 128), FLOAT),
            ((length, 256), FLOAT),
        ],
        owner,
        mix_grad_rows,
        mid_near,
        mid_far,
        gates,
        mixer_low,
        seg_wide,
        seg_row,
    )
    dt_start = width_local + query_cols
    pre_grad, *gu_got = together(pre_grad, *gu_got)
    gu_sum = add(gu_kept, gu_got)
    in_low, taps_grad, head_grad, share_terms = call(
        functools.partial(mixer_back_kernel, head_local),
        [
            ((length, width_local + 128), BFLOAT),
            ((8, conv_width), FLOAT),
            ((8, 128), FLOAT),
            ((length, share_cols), FLOAT),
        ],
        owner,
        pre_grad,
        mixer_kept,
        mixer_low,
        kv_grad,
        taps,
        head_pack,
        seg_wide,
        seg_row,
        scratch=[pltpu.VMEM((length, conv_width), FLOAT)],
    )
    share_terms = share_terms + swap(share_terms, "tensor", 4, 1)
    share_terms = share_terms + swap(share_terms.astype(BFLOAT), "tensor", 4, 2).astype(FLOAT)
    share_low = share_terms.astype(BFLOAT)
    block_width = share_cols // 4
    shared_mine = lax.dynamic_slice_in_dim(shared_full, shard_index * block_width, block_width, 1)
    block_low = lax.dynamic_slice_in_dim(share_low, shard_index * block_width, block_width, 1)
    share_grad = einsum_f32("ld,lk->dk", normed_rows, share_low).reshape(count, 4, share_rows, share_cols)
    share_grad = lax.dynamic_index_in_dim(share_grad, shard_index, 1, keepdims=False)
    share_grad = share_grad.reshape(count * share_rows, share_cols)
    mid_kept, mid_sent, _ = parted(
        [(normed_rows, zq_low), (mix_grad_rows, mixed_low)], order, last_group
    )
    mid_half_sum = add(mid_kept, send(mid_sent, last_group, count))
    in_kept, in_sent, _ = parted([(normed_rows, in_low)], order, last_group)
    share_kept, share_sent, _ = split(share_grad, order, last_group, [share_rows])
    in_kept = jnp.concatenate([in_kept, share_kept], axis=0)
    in_sent = [jnp.concatenate(pair, axis=0) for pair in zip(in_sent, share_sent)]
    mid_half_sum, gu_sum, block_low, *in_sent = lax.optimization_barrier(
        (mid_half_sum, gu_sum, block_low, *in_sent)
    )
    mid_sum = add(*finish(mid_half_sum, stay, back, count))
    in_half_sum = add(in_kept, send(in_sent, last_group, count))
    keep, give = call(
        input_back_kernel,
        [halves, halves],
        core,
        in_low,
        zq_low,
        block_low,
        early_near,
        early_far,
        mid_near,
        mid_far,
        shared_mine,
    )
    normed_one_grad = finish_tensor(keep, give, shard_index)
    token_norm_grad, gain_one_grad = norm_one_back(normed_one_grad)
    conv_full = lax.dynamic_update_slice_in_dim(
        jnp.zeros_like(conv_params), taps_grad[:5, :width_local], shard_index * width_local, 1
    )
    conv_full = conv_full.at[:, bc_start:].set(taps_grad[:5, width_local:])
    head_full = lax.dynamic_update_slice_in_dim(
        jnp.zeros_like(head_params),
        jnp.concatenate([head_grad[:2, :head_local], skip_lanes[:1, :head_local]], axis=0),
        shard_index * head_local,
        1,
    )
    wide = conv_params.shape[1]
    features, head_count = gains.shape[1], head_params.shape[1]
    gains_grad = relocate([jnp.stack([gain_one_grad, gain_two_grad])], dp_index, count, False)[0]
    small = jnp.concatenate(
        [
            jnp.pad(
                jnp.concatenate([gains_grad, head_full[:2]], axis=1),
                ((0, 0), (0, wide - features - head_count)),
            ),
            conv_full,
            jnp.pad(head_full[2:], ((0, 0), (0, wide - head_count))),
        ],
        axis=0,
    )
    for bits in (1, 2):
        small = group_sum(small, "tensor", 4, [bits])
    in_half_sum, mid_sum, down_half_sum, out_give, small = together(
        in_half_sum, mid_sum, down_half_sum, out_give, small
    )
    in_sum = add(*finish(in_half_sum, stay, back, count, [rows, share_rows]))
    down_sum = add(*finish(down_half_sum, down_stay, back[1:] + last, count))
    ffn_sum = finish_tensor(out_keep, out_give, shard_index)
    output = (hidden + ffn_sum).astype(BFLOAT)
    z_sum = mid_sum[:, :dt_start]
    out_sum = mid_sum[:, dt_start:]
    small = group_sum(small, "dp", count, last_group)
    small, in_sum = together(small, in_sum)
    for group in first:
        small = group_sum(small, "dp", count, group)
    shared_sum = in_sum[rows:]
    in_sum = in_sum[:rows]
    return (
        *relocate([output, hidden_grad + token_norm_grad], dp_index, count, False),
        jnp.stack([z_sum[:, :width_local], in_sum[:, :width_local]]),
        in_sum[:, width_local : width_local + head_local],
        z_sum[:, width_local:],
        out_sum[:, :width_local].T,
        out_sum[:, width_local:].T,
        jnp.stack([gu_sum[:, :ff_local], gu_sum[:, ff_local:]]),
        down_sum.T,
        shared_sum,
        small[:2, :features],
        small[2:7],
        jnp.concatenate(
            [small[:2, features : features + head_count], small[7:, :head_count]], axis=0
        ),
    )


def solution(mesh):
    count = mesh.shape["dp"]
    placed = (
        P(("dp", "tensor"), None),
        P("dp"),
        P(None, "dp", "tensor"),
        P("dp", "tensor"),
        P("dp", "tensor"),
        P("tensor", "dp"),
        P("tensor", "dp"),
        P(None, "dp", "tensor"),
        P("tensor", "dp"),
        P(("dp", "tensor"), None),
        P(),
        P(),
        P(),
        P(("dp", "tensor"), None),
    )

    def body(*arrays):
        return per_device(count, *arrays)

    return jax.shard_map(
        body,
        mesh=mesh,
        in_specs=placed,
        out_specs=(
            P(("dp", "tensor"), None),
            P(("dp", "tensor"), None),
            P(None, "dp", "tensor"),
            P("dp", "tensor"),
            P("dp", "tensor"),
            P("tensor", "dp"),
            P("tensor", "dp"),
            P(None, "dp", "tensor"),
            P("tensor", "dp"),
            P(("dp", "tensor"), None),
            P(),
            P(),
            P(),
        ),
        check_vma=False,
    )
```

time: 405 us -> 280 us (0.69)
  matrix products: 50.2 us -> 0.47 us
  local copies, waits for them, and re-layouts: 69.4 us -> 34.6 us
  starting transfers between devices: 91.8 us -> 63.4 us
  other arithmetic: 44.7 us -> 21.7 us
  Pallas kernels: 0 us -> 18.6 us
  waiting for transfers between devices: 115 us -> 109 us
    dot_general x31 -> x1, matrix products: 43.9 us -> 0.47 us  [einsum_f32(): jnp.einsum(pattern, op_left, op_right, preferred_element_type=jnp.float32)]
    ppermute x74 -> x50, starting transfers between devices: 88.2 us -> 63.4 us  [swap(): return lax.ppermute(values, axis, [(i, i ^ bits) for i in range(count)])]
    pallas_call x0 -> x18, Pallas kernels: none -> 18.6 us  [the longest x10 13.7 us: call(): pl.pallas_call(kernel, out_shape=[jax.ShapeDtypeStruct(shape, dtype) for...]
    reshape x12 -> x1, local copies, waits for them, and re-layouts: 8.16 us -> 0.08 us  [per_device(): jnp.repeat(head_mine[2], HDM)]
    unnamed x291 -> x162, local copies, waits for them, and re-layouts: 33.3 us -> 25.2 us
    convert_element_type x10 -> x7, other arithmetic: 6.97 us -> 0.29 us  [the longest x4 0.11 us: finish_tensor(): return mine + swap(other.astype(BFLOAT), 'tensor', 4, 2).astype(FLOAT)]
    add x4 -> x12, other arithmetic: 3.23 us -> 8.93 us  [the longest x7 6.07 us: add(): kept = kept + part.astype(FLOAT)]
    reduce_sum x5 -> x0, other arithmetic: 5.44 us -> none  [the longest x2 3.44 us: gate_piece(): skip_gain[None, :, None] * x_part]
  transfers between devices with their start and end apart: 75 -> 50, of which waited for: 35 -> 22; matrix products, arithmetic and copies ran while one was open for 38% -> 10% of each run, Pallas kernels for 0% -> 4%
where the time goes in v2:
time: 280 us; the launch traced here: 279 us
  waiting for transfers between devices  109 us (39%)
  starting transfers between devices  63.4 us (23%)
  local copies, waits for them, and re-layouts  34.6 us (12%)
  blocking collectives  29.4 us (10%)
  other arithmetic  21.7 us (8%)
  Pallas kernels  18.6 us (7%)
    ppermute x50, waiting for transfers between devices, swap(): return lax.ppermute(values, axis, [(i, i ^ bits) for i in range(count)])  109 us
    ppermute x50, starting transfers between devices, swap(): return lax.ppermute(values, axis, [(i, i ^ bits) for i in range(count)])  63.4 us
    all_gather x4, blocking collectives, gather_tensor(): return lax.all_gather(values, 'tensor', axis=0, tiled=True)  29.4 us
    unnamed x162, local copies, waits for them, and re-layouts  25.2 us
    pallas_call x10, Pallas kernels, call(): pl.pallas_call(kernel, out_shape=[jax.ShapeDtypeStruct(shape, dtype) for...  13.7 us
    add x7, other arithmetic, add(): kept = kept + part.astype(FLOAT)  6.07 us
  transfers between devices with their start and end apart: 50, of which 22 were waited for; matrix products, arithmetic and copies ran while one was open for 10% of the time, Pallas kernels for 4%

profile of v2, /device:TPU:0, one launch (start us, length us, event | category | flops | bytes accessed | tf_op | source)
XLA Modules:
  0.0 279.4 jit_solution(17295577303118975286)
XLA Ops:
  4.1 5.1 %collective-permute-start.2 = (bf16[128,768]{1,0:T(8,128)(2,1)S(1)}, bf16[128,768]{1,0:T(8,128)(2,1)S(1)}, u32[]{:S(2)}, u32[]{:S(2)}) collective-permute-start(bf16[128,768]{1,0:T(8,128)(2,1)S(1)} %fusion.15.refs_0_), channel_id=1, source_target_pairs={{0,24},{4,28},{8,16},{12,20},{16,8},{20,12},{24,0},{28,4},{1,25},{... | collective-permute-start | bytes 589832 | tf_op jit(solution)/shard_map/ppermute | solution.py:39
  16.1 7.2 %all_gather.12.normed_ref.refs_0_ = bf16[256,1024]{1,0:T(8,128)(2,1)S(1)} all-gather(bf16[64,1024]{1,0:T(8,128)(2,1)S(1)} %fusion.6), channel_id=1, replica_groups=mesh['dp'=8,'tensor'=4] {'tensor'}, dimensions={0}, use_global_device_ids=true | all-gather | bytes 655360 | tf_op jit(solution)/shard_map/all_gather | solution.py:615
  32.8 7.6 %all_gather.13.cot_ref.refs_0_ = bf16[256,1024]{1,0:T(8,128)(2,1)} all-gather(bf16[64,1024]{1,0:T(8,128)(2,1)S(1)} %get-tuple-element.100), channel_id=1, replica_groups=mesh['dp'=8,'tensor'=4] {'tensor'}, dimensions={0}, use_global_device_ids=true | all-gather | bytes 655360 | tf_op jit(solution)/shard_map/all_gather | solution.py:615
  40.5 7.6 %collective-permute-done.5.refs_2_ = bf16[128,896]{1,0:T(8,128)(2,1)S(1)} collective-permute-done((bf16[128,896]{1,0:T(8,128)(2,1)S(1)}, bf16[128,896]{1,0:T(8,128)(2,1)S(1)}, u32[]{:S(2)}, u32[]{:S(2)}) %collective-permute-start.5) | collective-permute-done | bytes 229408 | tf_op jit(solution)/shard_map/ppermute | solution.py:39
  50.4 5.2 %collective-permute-done.12 = bf16[8,32,512]{2,1,0:T(8,128)(2,1)S(1)} collective-permute-done((bf16[8,32,512]{2,1,0:T(8,128)(2,1)S(1)}, bf16[8,32,512]{2,1,0:T(8,128)(2,1)S(1)}, u32[]{:S(2)}, u32[]{:S(2)}) %collective-permute-start.12) | collective-permute-done | bytes 262176 | tf_op jit(solution)/shard_map/ppermute | solution.py:39
  56.8 3.4 %collective-permute-start.10 = (bf16[128,1024]{1,0:T(8,128)(2,1)}, bf16[128,1024]{1,0:T(8,128)(2,1)}, u32[]{:S(2)}, u32[]{:S(2)}) collective-permute-start(bf16[128,1024]{1,0:T(8,128)(2,1)} %pad_maximum_fusion.4.refs_0_), channel_id=1, source_target_pairs={{0,24},{4,28},{8,16},{12,20},{16,8},{20,12},{24,0},{28,4},{1,25},{... | collective-permute-start | bytes 786440 | tf_op jit(solution)/shard_map/ppermute | solution.py:39
  64.0 4.2 %collective-permute-done.10.refs_3_ = bf16[128,1024]{1,0:T(8,128)(2,1)} collective-permute-done((bf16[128,1024]{1,0:T(8,128)(2,1)}, bf16[128,1024]{1,0:T(8,128)(2,1)}, u32[]{:S(2)}, u32[]{:S(2)}) %collective-permute-start.10) | collective-permute-done | bytes 262176 | tf_op jit(solution)/shard_map/ppermute | solution.py:39
  68.1 14.6 %collective-permute-done.9.refs_2_ = bf16[128,1024]{1,0:T(8,128)(2,1)} collective-permute-done((bf16[128,1024]{1,0:T(8,128)(2,1)}, bf16[128,1024]{1,0:T(8,128)(2,1)}, u32[]{:S(2)}, u32[]{:S(2)}) %collective-permute-start.9) | collective-permute-done | bytes 262176 | tf_op jit(solution)/shard_map/ppermute | solution.py:39
  101.1 3.1 %collective-permute-start.17 = (bf16[256,512]{1,0:T(8,128)(2,1)S(1)}, bf16[256,512]{1,0:T(8,128)(2,1)S(1)}, u32[]{:S(2)}, u32[]{:S(2)}) collective-permute-start(bf16[256,512]{1,0:T(8,128)(2,1)S(1)} %copy-done.23), channel_id=1, source_target_pairs={{0,8},{4,12},{8,0},{12,4},{16,24},{20,28},{24,16},{28,20},{1,9},{5... | collective-permute-start | bytes 786440 | tf_op jit(solution)/shard_map/ppermute | solution.py:39
  105.3 6.7 %all_gather.14.rows_ref.refs_0_ = bf16[256,1024]{1,0:T(8,128)(2,1)S(1)} all-gather(bf16[64,1024]{1,0:T(8,128)(2,1)S(1)} %multiply_convert_fusion), channel_id=1, replica_groups=mesh['dp'=8,'tensor'=4] {'tensor'}, dimensions={0}, use_global_device_ids=true | all-gather | bytes 655360 | tf_op jit(solution)/shard_map/all_gather | solution.py:615
  112.1 10.6 %collective-permute-done.18.refs_4_ = bf16[256,512]{1,0:T(8,128)(2,1)S(1)} collective-permute-done((bf16[256,512]{1,0:T(8,128)(2,1)S(1)}, bf16[256,512]{1,0:T(8,128)(2,1)S(1)}, u32[]{:S(2)}, u32[]{:S(2)}) %collective-permute-start.18) | collective-permute-done | bytes 262176 | tf_op jit(solution)/shard_map/ppermute | solution.py:39
  127.7 3.1 %collective-permute-start.22 = (bf16[256,512]{1,0:T(8,128)(2,1)S(1)}, bf16[256,512]{1,0:T(8,128)(2,1)S(1)}, u32[]{:S(2)}, u32[]{:S(2)}) collective-permute-start(bf16[256,512]{1,0:T(8,128)(2,1)S(1)} %get-tuple-element.124), channel_id=1, source_target_pairs={{0,16},{4,20},{8,24},{12,28},{16,0},{20,4},{24,8},{28,12},{1,17},{... | collective-permute-start | bytes 786440 | tf_op jit(solution)/shard_map/ppermute | solution.py:39
  135.5 5.7 %collective-permute-done.21 = bf16[256,512]{1,0:T(8,128)(2,1)S(1)} collective-permute-done((bf16[256,512]{1,0:T(8,128)(2,1)S(1)}, bf16[256,512]{1,0:T(8,128)(2,1)S(1)}, u32[]{:S(2)}, u32[]{:S(2)}) %collective-permute-start.21) | collective-permute-done | bytes 262176 | tf_op jit(solution)/shard_map/ppermute | solution.py:39
  141.2 7.9 %collective-permute-done.22 = bf16[256,512]{1,0:T(8,128)(2,1)S(1)} collective-permute-done((bf16[256,512]{1,0:T(8,128)(2,1)S(1)}, bf16[256,512]{1,0:T(8,128)(2,1)S(1)}, u32[]{:S(2)}, u32[]{:S(2)}) %collective-permute-start.22) | collective-permute-done | bytes 262176 | tf_op jit(solution)/shard_map/ppermute | solution.py:39
  151.1 7.8 %all_gather.15.grad_ref.refs_1_ = bf16[256,1024]{1,0:T(8,128)(2,1)} all-gather(bf16[64,1024]{1,0:T(8,128)(2,1)S(1)} %fusion.30), channel_id=1, replica_groups=mesh['dp'=8,'tensor'=4] {'tensor'}, dimensions={0}, use_global_device_ids=true | all-gather | bytes 655360 | tf_op jit(solution)/shard_map/all_gather | solution.py:615
  163.4 4.5 %collective-permute-start.27 = (bf16[128,1024]{1,0:T(8,128)(2,1)}, bf16[128,1024]{1,0:T(8,128)(2,1)}, u32[]{:S(2)}, u32[]{:S(2)}) collective-permute-start(bf16[128,1024]{1,0:T(8,128)(2,1)} %get-tuple-element.207), channel_id=1, source_target_pairs={{0,16},{4,20},{8,24},{12,28},{16,0},{20,4},{24,8},{28,12},{1,17},{... | collective-permute-start | bytes 786440 | tf_op jit(solution)/shard_map/ppermute | solution.py:39
  179.3 9.1 %collective-permute-done.27 = bf16[128,1024]{1,0:T(8,128)(2,1)} collective-permute-done((bf16[128,1024]{1,0:T(8,128)(2,1)}, bf16[128,1024]{1,0:T(8,128)(2,1)}, u32[]{:S(2)}, u32[]{:S(2)}) %collective-permute-start.27) | collective-permute-done | bytes 262176 | tf_op jit(solution)/shard_map/ppermute | solution.py:39
  188.5 3.1 %shard_map.249 = (bf16[256,512]{1,0:T(8,128)(2,1)S(1)}, f32[8,640]{1,0:T(8,128)S(1)}, f32[8,128]{1,0:T(8,128)S(1)}, f32[256,512]{1,0:T(8,128)S(1)}) custom-call(s32[1]{0:T(128)} %bitcast.14.owner_ref, f32[256,384]{1,0:T(8,128)S(1)} %get-tuple-element.133.pre_grad_ref, f32[256,1792]{1,0:T(8,128)S(1)} %copy-done.17, bf16[256,1024]{1,0:T(8,128)(2,1)S(1)} %copy-done.15, ...), custom_call_target="tpu_custom_call" | custom-call | flops 1000 | bytes 1000 | tf_op jit(solution)/shard_map/pallas_call | solution.py:547
  198.9 6.2 %collective-permute-done.30 = bf16[256,512]{1,0:T(8,128)(2,1)S(1)} collective-permute-done((bf16[256,512]{1,0:T(8,128)(2,1)S(1)}, bf16[256,512]{1,0:T(8,128)(2,1)S(1)}, u32[]{:S(2)}, u32[]{:S(2)}) %collective-permute-start.30) | collective-permute-done | bytes 262176 | tf_op jit(solution)/shard_map/ppermute | solution.py:39
  217.2 3.2 %collective-permute-done.37 = bf16[64,1024]{1,0:T(8,128)(2,1)S(1)} collective-permute-done((bf16[64,1024]{1,0:T(8,128)(2,1)S(1)}, bf16[64,1024]{1,0:T(8,128)(2,1)S(1)}, u32[]{:S(2)}, u32[]{:S(2)}) %collective-permute-start.37) | collective-permute-done | bytes 131104 | tf_op jit(solution)/shard_map/ppermute | solution.py:39
  220.6 6.3 %collective-permute-done.35 = bf16[128,1024]{1,0:T(8,128)(2,1)S(1)} collective-permute-done((bf16[128,1024]{1,0:T(8,128)(2,1)S(1)}, bf16[128,1024]{1,0:T(8,128)(2,1)S(1)}, u32[]{:S(2)}, u32[]{:S(2)}) %collective-permute-start.35) | collective-permute-done | bytes 262176 | tf_op jit(solution)/shard_map/ppermute | solution.py:39
  226.9 11.2 %collective-permute-done.34 = bf16[128,1024]{1,0:T(8,128)(2,1)S(1)} collective-permute-done((bf16[128,1024]{1,0:T(8,128)(2,1)S(1)}, bf16[128,1024]{1,0:T(8,128)(2,1)S(1)}, u32[]{:S(2)}, u32[]{:S(2)}) %collective-permute-start.34) | collective-permute-done | bytes 262176 | tf_op jit(solution)/shard_map/ppermute | solution.py:39
  240.7 3.2 %collective-permute-done.39 = f32[8,1792]{1,0:T(8,128)S(1)} collective-permute-done((f32[8,1792]{1,0:T(8,128)S(1)}, f32[8,1792]{1,0:T(8,128)S(1)}, u32[]{:S(2)}, u32[]{:S(2)}) %collective-permute-start.39) | collective-permute-done | bytes 57376 | tf_op jit(solution)/shard_map/ppermute | solution.py:39
  256.3 6.0 %collective-permute-done.44 = bf16[160,512]{1,0:T(8,128)(2,1)S(1)} collective-permute-done((bf16[160,512]{1,0:T(8,128)(2,1)}, bf16[160,512]{1,0:T(8,128)(2,1)S(1)}, u32[]{:S(2)}, u32[]{:S(2)}) %collective-permute-start.44) | collective-permute-done | bytes 163872 | tf_op jit(solution)/shard_map/ppermute | solution.py:39
  (374 shorter events, 124.6 us)
Async XLA Ops:
  4.1 20.2 %collective-permute-start.2 = (bf16[128,768]{1,0:T(8,128)(2,1)S(1)}, bf16[128,768]{1,0:T(8,128)(2,1)S(1)}, u32[]{:S(2)}, u32[]{:S(2)}) collective-permute-start(bf16[128,768]{1,0:T(8,128)(2,1)S(1)} %fusion.15.refs_0_), channel_id=1, source_target_pairs={{0,24},{4,28},{8,16},{12,20},{16,8},{20,12},{24,0},{28,4},{1,25},{... | collective-permute-start | bytes 589832 | tf_op jit(solution)/shard_map/ppermute | solution.py:39
  9.3 16.7 %collective-permute-start.1 = (bf16[128,768]{1,0:T(8,128)(2,1)S(1)}, bf16[128,768]{1,0:T(8,128)(2,1)S(1)}, u32[]{:S(2)}, u32[]{:S(2)}) collective-permute-start(bf16[128,768]{1,0:T(8,128)(2,1)S(1)} %fusion.15.refs_0_), channel_id=1, source_target_pairs={{0,16},{4,20},{8,24},{12,28},{16,0},{20,4},{24,8},{28,12},{1,17},{... | collective-permute-start | bytes 589832 | tf_op jit(solution)/shard_map/ppermute | solution.py:39
  9.3 16.7 %collective-permute-start = (bf16[128,768]{1,0:T(8,128)(2,1)S(1)}, bf16[128,768]{1,0:T(8,128)(2,1)S(1)}, u32[]{:S(2)}, u32[]{:S(2)}) collective-permute-start(bf16[128,768]{1,0:T(8,128)(2,1)S(1)} %fusion.15.refs_0_), channel_id=1, source_target_pairs={{0,8},{4,12},{8,0},{12,4},{16,24},{20,28},{24,16},{28,20},{1,9},{5... | collective-permute-start | bytes 589832 | tf_op jit(solution)/shard_map/ppermute | solution.py:39
  26.0 22.2 %collective-permute-start.7 = (bf16[512,768]{1,0:T(8,128)(2,1)S(1)}, bf16[512,768]{1,0:T(8,128)(2,1)S(1)}, u32[]{:S(2)}, u32[]{:S(2)}) collective-permute-start(bf16[512,768]{1,0:T(8,128)(2,1)S(1)} %shard_map.238.near_ref.early_near_ref), channel_id=1, source_target_pairs={{0,4},{4,0},{8,12},{12,8},{16,20},{20,16},{24,28},{28,24},{1,5},{5... | collective-permute-start | bytes 2359304 | tf_op jit(solution)/shard_map/ppermute | solution.py:39
  30.2 17.9 %collective-permute-start.5 = (bf16[128,896]{1,0:T(8,128)(2,1)S(1)}, bf16[128,896]{1,0:T(8,128)(2,1)S(1)}, u32[]{:S(2)}, u32[]{:S(2)}) collective-permute-start(bf16[128,896]{1,0:T(8,128)(2,1)S(1)} %pad_maximum_fusion.7.refs_0_), channel_id=1, source_target_pairs={{0,16},{4,20},{8,24},{12,28},{16,0},{20,4},{24,8},{28,12},{1,17},{... | collective-permute-start | bytes 688136 | tf_op jit(solution)/shard_map/ppermute | solution.py:39
  30.2 17.9 %collective-permute-start.4 = (bf16[128,896]{1,0:T(8,128)(2,1)S(1)}, bf16[128,896]{1,0:T(8,128)(2,1)S(1)}, u32[]{:S(2)}, u32[]{:S(2)}) collective-permute-start(bf16[128,896]{1,0:T(8,128)(2,1)S(1)} %pad_maximum_fusion.7.refs_0_), channel_id=1, source_target_pairs={{0,8},{4,12},{8,0},{12,4},{16,24},{20,28},{24,16},{28,20},{1,9},{5... | collective-permute-start | bytes 688136 | tf_op jit(solution)/shard_map/ppermute | solution.py:39
  56.7 27.3 %collective-permute-start.13 = (bf16[2,8,32,512]{3,2,0,1:T(8,128)(2,1)}, bf16[2,8,32,512]{3,2,0,1:T(8,128)(2,1)}, u32[]{:S(2)}, u32[]{:S(2)}) collective-permute-start(bf16[2,8,32,512]{3,2,0,1:T(8,128)(2,1)} %get-tuple-element.222), channel_id=1, source_target_pairs={{0,1},{1,0},{2,3},{3,2},{4,5},{5,4},{6,7},{7,6},{8,9},{9,8},{10,11... | collective-permute-start | bytes 1572872 | tf_op jit(solution)/shard_map/ppermute | solution.py:39
  60.2 22.5 %collective-permute-start.9 = (bf16[128,1024]{1,0:T(8,128)(2,1)}, bf16[128,1024]{1,0:T(8,128)(2,1)}, u32[]{:S(2)}, u32[]{:S(2)}) collective-permute-start(bf16[128,1024]{1,0:T(8,128)(2,1)} %pad_maximum_fusion.4.refs_0_), channel_id=1, source_target_pairs={{0,16},{4,20},{8,24},{12,28},{16,0},{20,4},{24,8},{28,12},{1,17},{... | collective-permute-start | bytes 786440 | tf_op jit(solution)/shard_map/ppermute | solution.py:39
  60.2 22.5 %collective-permute-start.8 = (bf16[128,1024]{1,0:T(8,128)(2,1)}, bf16[128,1024]{1,0:T(8,128)(2,1)}, u32[]{:S(2)}, u32[]{:S(2)}) collective-permute-start(bf16[128,1024]{1,0:T(8,128)(2,1)} %pad_maximum_fusion.4.refs_0_), channel_id=1, source_target_pairs={{0,8},{4,12},{8,0},{12,4},{16,24},{20,28},{24,16},{28,20},{1,9},{5... | collective-permute-start | bytes 786440 | tf_op jit(solution)/shard_map/ppermute | solution.py:39
  61.4 30.3 %collective-permute-start.11 = (bf16[512,896]{1,0:T(8,128)(2,1)S(1)}, bf16[512,896]{1,0:T(8,128)(2,1)S(1)}, u32[]{:S(2)}, u32[]{:S(2)}) collective-permute-start(bf16[512,896]{1,0:T(8,128)(2,1)S(1)} %shard_map.241.near_ref), channel_id=1, source_target_pairs={{0,4},{4,0},{8,12},{12,8},{16,20},{20,16},{24,28},{28,24},{1,5},{5... | collective-permute-start | bytes 2752520 | tf_op jit(solution)/shard_map/ppermute | solution.py:39
  95.8 26.9 %collective-permute-start.16 = (bf16[512,1024]{1,0:T(8,128)(2,1)}, bf16[512,1024]{1,0:T(8,128)(2,1)S(1)}, u32[]{:S(2)}, u32[]{:S(2)}) collective-permute-start(bf16[512,1024]{1,0:T(8,128)(2,1)} %copy-done.6), channel_id=1, source_target_pairs={{0,4},{4,0},{8,12},{12,8},{16,20},{20,16},{24,28},{28,24},{1,5},{5... | collective-permute-start | bytes 3145736 | tf_op jit(solution)/shard_map/ppermute | solution.py:39
  101.1 21.5 %collective-permute-start.18 = (bf16[256,512]{1,0:T(8,128)(2,1)S(1)}, bf16[256,512]{1,0:T(8,128)(2,1)S(1)}, u32[]{:S(2)}, u32[]{:S(2)}) collective-permute-start(bf16[256,512]{1,0:T(8,128)(2,1)S(1)} %copy-done.23), channel_id=1, source_target_pairs={{0,16},{4,20},{8,24},{12,28},{16,0},{20,4},{24,8},{28,12},{1,17},{... | collective-permute-start | bytes 786440 | tf_op jit(solution)/shard_map/ppermute | solution.py:39
  101.1 21.5 %collective-permute-start.17 = (bf16[256,512]{1,0:T(8,128)(2,1)S(1)}, bf16[256,512]{1,0:T(8,128)(2,1)S(1)}, u32[]{:S(2)}, u32[]{:S(2)}) collective-permute-start(bf16[256,512]{1,0:T(8,128)(2,1)S(1)} %copy-done.23), channel_id=1, source_target_pairs={{0,8},{4,12},{8,0},{12,4},{16,24},{20,28},{24,16},{28,20},{1,9},{5... | collective-permute-start | bytes 786440 | tf_op jit(solution)/shard_map/ppermute | solution.py:39
  127.7 21.5 %collective-permute-start.22 = (bf16[256,512]{1,0:T(8,128)(2,1)S(1)}, bf16[256,512]{1,0:T(8,128)(2,1)S(1)}, u32[]{:S(2)}, u32[]{:S(2)}) collective-permute-start(bf16[256,512]{1,0:T(8,128)(2,1)S(1)} %get-tuple-element.124), channel_id=1, source_target_pairs={{0,16},{4,20},{8,24},{12,28},{16,0},{20,4},{24,8},{28,12},{1,17},{... | collective-permute-start | bytes 786440 | tf_op jit(solution)/shard_map/ppermute | solution.py:39
  130.8 18.4 %collective-permute-start.23 = (bf16[256,512]{1,0:T(8,128)(2,1)S(1)}, bf16[256,512]{1,0:T(8,128)(2,1)S(1)}, u32[]{:S(2)}, u32[]{:S(2)}) collective-permute-start(bf16[256,512]{1,0:T(8,128)(2,1)S(1)} %get-tuple-element.125), channel_id=1, source_target_pairs={{0,24},{4,28},{8,16},{12,20},{16,8},{20,12},{24,0},{28,4},{1,25},{... | collective-permute-start | bytes 786440 | tf_op jit(solution)/shard_map/ppermute | solution.py:39
  132.0 26.8 %collective-permute-start.20 = (bf16[512,1024]{1,0:T(8,128)(2,1)S(1)}, bf16[512,1024]{1,0:T(8,128)(2,1)S(1)}, u32[]{:S(2)}, u32[]{:S(2)}) collective-permute-start(bf16[512,1024]{1,0:T(8,128)(2,1)S(1)} %get-tuple-element.121), channel_id=1, source_target_pairs={{0,4},{4,0},{8,12},{12,8},{16,20},{20,16},{24,28},{28,24},{1,5},{5... | collective-permute-start | bytes 3145736 | tf_op jit(solution)/shard_map/ppermute | solution.py:39
  134.1 16.1 %collective-permute-start.25 = (bf16[64,1024]{1,0:T(8,128)(2,1)S(1)}, bf16[64,1024]{1,0:T(8,128)(2,1)S(1)}, u32[]{:S(2)}, u32[]{:S(2)}) collective-permute-start(bf16[64,1024]{1,0:T(8,128)(2,1)S(1)} %fusion.17), channel_id=1, source_target_pairs={{0,2},{1,3},{2,0},{3,1},{4,6},{5,7},{6,4},{7,5},{8,10},{9,11},{10,... | collective-permute-start | bytes 393224 | tf_op jit(solution)/shard_map/ppermute | solution.py:39
  160.9 18.4 %collective-permute-start.28 = (bf16[128,1024]{1,0:T(8,128)(2,1)}, bf16[128,1024]{1,0:T(8,128)(2,1)}, u32[]{:S(2)}, u32[]{:S(2)}) collective-permute-start(bf16[128,1024]{1,0:T(8,128)(2,1)} %get-tuple-element.206), channel_id=1, source_target_pairs={{0,24},{4,28},{8,16},{12,20},{16,8},{20,12},{24,0},{28,4},{1,25},{... | collective-permute-start | bytes 786440 | tf_op jit(solution)/shard_map/ppermute | solution.py:39
  163.4 25.1 %collective-permute-start.27 = (bf16[128,1024]{1,0:T(8,128)(2,1)}, bf16[128,1024]{1,0:T(8,128)(2,1)}, u32[]{:S(2)}, u32[]{:S(2)}) collective-permute-start(bf16[128,1024]{1,0:T(8,128)(2,1)} %get-tuple-element.207), channel_id=1, source_target_pairs={{0,16},{4,20},{8,24},{12,28},{16,0},{20,4},{24,8},{28,12},{1,17},{... | collective-permute-start | bytes 786440 | tf_op jit(solution)/shard_map/ppermute | solution.py:39
  167.9 20.6 %collective-permute-start.26 = (bf16[128,1024]{1,0:T(8,128)(2,1)}, bf16[128,1024]{1,0:T(8,128)(2,1)}, u32[]{:S(2)}, u32[]{:S(2)}) collective-permute-start(bf16[128,1024]{1,0:T(8,128)(2,1)} %get-tuple-element.208), channel_id=1, source_target_pairs={{0,8},{4,12},{8,0},{12,4},{16,24},{20,28},{24,16},{28,20},{1,9},{5... | collective-permute-start | bytes 786440 | tf_op jit(solution)/shard_map/ppermute | solution.py:39
  177.8 28.0 %collective-permute-start.31 = (bf16[512,1024]{1,0:T(8,128)(2,1)}, bf16[512,1024]{1,0:T(8,128)(2,1)}, u32[]{:S(2)}, u32[]{:S(2)}) collective-permute-start(bf16[512,1024]{1,0:T(8,128)(2,1)} %get-tuple-element.142), channel_id=1, source_target_pairs={{0,4},{4,0},{8,12},{12,8},{16,20},{20,16},{24,28},{28,24},{1,5},{5... | collective-permute-start | bytes 3145736 | tf_op jit(solution)/shard_map/ppermute | solution.py:39
  209.8 28.6 %collective-permute-start.32 = (bf16[640,512]{1,0:T(8,128)(2,1)S(1)}, bf16[640,512]{1,0:T(8,128)(2,1)S(1)}, u32[]{:S(2)}, u32[]{:S(2)}) collective-permute-start(bf16[640,512]{1,0:T(8,128)(2,1)S(1)} %fusion.24), channel_id=1, source_target_pairs={{0,4},{4,0},{8,12},{12,8},{16,20},{20,16},{24,28},{28,24},{1,5},{5... | collective-permute-start | bytes 1966088 | tf_op jit(solution)/shard_map/ppermute | solution.py:39
  214.2 23.9 %collective-permute-start.34 = (bf16[128,1024]{1,0:T(8,128)(2,1)S(1)}, bf16[128,1024]{1,0:T(8,128)(2,1)S(1)}, u32[]{:S(2)}, u32[]{:S(2)}) collective-permute-start(bf16[128,1024]{1,0:T(8,128)(2,1)S(1)} %get-tuple-element.205), channel_id=1, source_target_pairs={{0,16},{4,20},{8,24},{12,28},{16,0},{20,4},{24,8},{28,12},{1,17},{... | collective-permute-start | bytes 786440 | tf_op jit(solution)/shard_map/ppermute | solution.py:39
  254.6 17.5 %collective-permute-start.40 = (f32[2,64,1024]{2,1,0:T(8,128)S(1)}, f32[2,64,1024]{2,1,0:T(8,128)}, u32[]{:S(2)}, u32[]{:S(2)}) collective-permute-start(f32[2,64,1024]{2,1,0:T(8,128)S(1)} %copy-done.43), channel_id=1, source_target_pairs={{0,1},{1,0},{2,3},{3,2},{4,5},{5,4},{6,7},{7,6},{8,9},{9,8},{10,11... | collective-permute-start | bytes 1572872 | tf_op jit(solution)/shard_map/ppermute | solution.py:39
  (102 other events, 918.4 us)

commit v3 on v2

--- a/solution.py
+++ b/solution.py
@@ -213,12 +213,51 @@
     return rows(stay), [rows([r ^ m for r in stay]).astype(BFLOAT) for m in group], stay
 
 
-def finish(total, order, groups, count, sizes=None):
+def add_split_kernel(spans, kept_ref, *refs):
+    got, outs = refs[: len(refs) - len(spans)], refs[len(refs) - len(spans) :]
+    for out, found in zip(outs, spans):
+        row = 0
+        for start, size in found:
+            total = kept_ref[start : start + size, :]
+            for part in got:
+                total = total + part[start : start + size, :].astype(FLOAT)
+            out[row : row + size, :] = total.astype(out.dtype)
+            row += size
+
+
+def add_split(kept, got, order, group, sizes):
+    span = 0
+    for m in group:
+        span |= m
+    stay = [r for r in order if r & span == 0]
+    spans = []
+    for blocks in [stay] + [[r ^ m for r in stay] for m in group]:
+        start, found = 0, []
+        for size in sizes:
+            found += [(start + order.index(r) * size, size) for r in blocks]
+            start += size * len(order)
+        spans.append(found)
+    shape = (sum(sizes) * len(stay), kept.shape[1])
+    kept, *sent = pl.pallas_call(
+        functools.partial(add_split_kernel, spans),
+        out_shape=[jax.ShapeDtypeStruct(shape, FLOAT)]
+        + [jax.ShapeDtypeStruct(shape, BFLOAT)] * len(group),
+        in_specs=[WHOLE] * (1 + len(got)),
+        out_specs=[WHOLE] * (1 + len(group)),
+        compiler_params=pltpu.CompilerParams(vmem_limit_bytes=16 * 1024 * 1024),
+        cost_estimate=pl.CostEstimate(flops=1000, bytes_accessed=1000, transcendentals=0),
+    )(kept, *got)
+    return kept, sent, stay
+
+
+def finish(kept, got, order, groups, count, sizes=None):
     if sizes is None:
-        sizes = [total.shape[0] // len(order)]
-    kept, got = total, []
+        sizes = [kept.shape[0] // len(order)]
     for group in groups:
-        kept, sent, order = split(add(kept, got), order, group, sizes)
+        if min(sizes) % 16 == 0:
+            kept, sent, order = add_split(kept, got, order, group, sizes)
+        else:
+            kept, sent, order = split(add(kept, got), order, group, sizes)
         got = send(sent, group, count)
     return kept, got
 
@@ -656,7 +695,9 @@
     gains = relocate([norm_gains], dp_index, count, True)[0]
     normed_one, norm_one_back = jax.vjp(rms_norm, token_f, gains[0])
     normed_rows = gather_tensor(normed_one.astype(BFLOAT))
-    cot_rows = gather_tensor(cot_local)
+
+    seg_wide = jnp.broadcast_to(segments.astype(FLOAT)[:, None], (length, 128))
+    seg_row = jnp.broadcast_to(segments.astype(FLOAT)[None], (8, length))
 
     shared_pack = shared_weight.reshape(share_rows, 4, share_cols // 4)
     shared_pack = jnp.concatenate([shared_pack[:, k] for k in range(4)], axis=0)
@@ -669,27 +710,25 @@
     gu_piece = jnp.concatenate([gate_up_weight[0], gate_up_weight[1]], axis=1)
     down_half, down_have = joined(*gather(down_weight.T, [0], last, count))
     early_half, have = joined(*gather(lead_piece, [0], first, count))
-    early_half, down_half, mid_piece, normed_rows = lax.optimization_barrier(
-        (early_half, down_half, mid_piece, normed_rows)
-    )
+    early_half, down_half, mid_piece, normed_rows, seg_row = together(
+        early_half, down_half, mid_piece, normed_rows, seg_row
+    )
+    cot_rows = gather_tensor(cot_local)
     (early_near, early_far), _ = two(*gather(early_half, have, last, count))
     mid_half, _ = joined(*gather(mid_piece, [0], first, count))
-    mid_half, early_far, gu_piece, cot_rows = lax.optimization_barrier(
-        (mid_half, early_far, gu_piece, cot_rows)
+    mid_half, early_far, gu_piece, cot_rows, seg_row = together(
+        mid_half, early_far, gu_piece, cot_rows, seg_row
     )
     (mid_near, mid_far), _ = two(*gather(mid_half, have, last, count))
-    gu_half, _ = joined(*gather(gu_piece, [0], first, count))
-    gu_half, mid_far, down_half = lax.optimization_barrier((gu_half, mid_far, down_half))
-    gu_parts, gu_places = gather(gu_half, have, last, count)
-    down_parts, down_places = gather(down_half, down_have, first, count)
+    gu_first, gu_first_places = gather(gu_piece, [0], first, count)
     shared_got = jnp.concatenate([early_near[:, :128], early_far[:, :128]], axis=0)
     shared_got = shared_got.reshape(count, 4, share_rows, share_cols // 4)
     shared_got = jnp.concatenate([shared_got[:, k] for k in range(4)], axis=-1)
-    near = jnp.stack([shared_got, swap(shared_got, "tensor", 4, 2)])
-    both = jnp.stack([near, swap(near, "tensor", 4, 1)])
-    both = jnp.where(shard_index & 1 == 1, both[::-1], both)
-    both = jnp.where(shard_index >> 1 == 1, both[:, ::-1], both)
-    shared_full = both.transpose(2, 1, 0, 3, 4).reshape(count * rows, share_cols)
+    near = jnp.stack([shared_got, swap(shared_got, "tensor", 4, 1)])
+    both = jnp.stack([near, swap(near, "tensor", 4, 2)])
+    both = jnp.where(shard_index >> 1 == 1, both[::-1], both)
+    both = jnp.where(shard_index & 1 == 1, both[:, ::-1], both)
+    shared_full = both.transpose(2, 0, 1, 3, 4).reshape(count * rows, share_cols)
 
     head_mine = lax.dynamic_slice_in_dim(head_params, shard_index * head_local, head_local, 1)
     bc_start = conv_params.shape[1] - 2 * NSTATE
@@ -704,8 +743,6 @@
     taps = jnp.concatenate([conv_mine, jnp.pad(jnp.repeat(head_mine[2], HDM), (0, 2 * NSTATE))[None]], axis=0)
     taps = jnp.pad(taps, ((0, 8 - taps.shape[0]), (0, 0)))
     head_pack = jnp.pad(head_mine, ((0, 5), (0, 128 - head_local)))
-    seg_wide = jnp.broadcast_to(segments.astype(FLOAT)[:, None], (length, 128))
-    seg_row = jnp.broadcast_to(segments.astype(FLOAT)[None], (8, length))
     core = (shard_index & 1)[None]
     owner = ((shard_index * query_local) // (QH // KVH))[None]
     width_full = count * rows
@@ -729,6 +766,11 @@
         seg_wide,
         seg_row,
     )
+    pre_gate, gu_first = together(pre_gate, gu_first)
+    gu_half, _ = joined(gu_first, gu_first_places)
+    gu_half, mid_far, down_half, seg_row = together(gu_half, mid_far, down_half, seg_row)
+    gu_parts, gu_places = gather(gu_half, have, last, count)
+    down_parts, down_places = gather(down_half, down_have, first, count)
     halves = ((2, length // 4, width_full), FLOAT)
     gates, mixed_low, keep, give = call(
         gate_kernel,
@@ -752,21 +794,24 @@
         *gu_parts,
         *down_parts,
     )
+    last_group = last[0]
+    back = groups[:-1][::-1]
+    down_kept, down_sent, down_stay = parted([(cot_rows, act_low)], order, back[0])
+    gu_kept, gu_sent, stay = parted([(ffn_rows, gu_low)], order, last_group)
+    gu_sent, down_sent, seg_row = together(gu_sent, down_sent, seg_row)
+    gu_got = send(gu_sent, last_group, count)
+    down_got = send(down_sent, back[0], count)
     normed_two_grad = finish_tensor(keep, give, shard_index)
     hidden_norm_grad, gain_two_grad = norm_two_back(normed_two_grad)
     hidden_grad = cot_local.astype(FLOAT) + hidden_norm_grad
     mix_grad_rows = gather_tensor(hidden_grad.astype(BFLOAT))
-    last_group = last[0]
-    back = groups[:-1][::-1]
-    down_kept, down_sent, down_stay = parted([(cot_rows, act_low)], order, back[0])
-    gu_kept, gu_sent, stay = parted([(ffn_rows, gu_low)], order, last_group)
-    gu_sent, down_sent = together(gu_sent, down_sent)
-    gu_half_sum = add(gu_kept, send(gu_sent, last_group, count))
-    down_half_sum = add(down_kept, send(down_sent, back[0], count))
-    gu_half_sum, down_half_sum, mix_grad_rows = lax.optimization_barrier(
-        (gu_half_sum, down_half_sum, mix_grad_rows)
-    )
-    gu_kept, gu_got = finish(gu_half_sum, stay, back, count)
+    gu_got, down_got, mix_grad_rows, seg_row = together(gu_got, down_got, mix_grad_rows, seg_row)
+    if len(back) == 1 and rows % 16 == 0:
+        gu_kept, gu_sent, _ = add_split(gu_kept, gu_got, stay, back[0], [rows])
+        gu_sent, mix_grad_rows = together(gu_sent, mix_grad_rows)
+        gu_got = send(gu_sent, back[0], count)
+    else:
+        gu_kept, gu_got = finish(gu_kept, gu_got, stay, back, count)
     zq_low, pre_grad, skip_lanes, kv_grad = call(
         gate_back_kernel,
         [
@@ -785,8 +830,11 @@
         seg_row,
     )
     dt_start = width_local + query_cols
-    pre_grad, *gu_got = together(pre_grad, *gu_got)
-    gu_sum = add(gu_kept, gu_got)
+    mid_kept, mid_sent, _ = parted(
+        [(normed_rows, zq_low), (mix_grad_rows, mixed_low)], order, last_group
+    )
+    mid_sent, seg_row = together(mid_sent, seg_row)
+    mid_got = send(mid_sent, last_group, count)
     in_low, taps_grad, head_grad, share_terms = call(
         functools.partial(mixer_back_kernel, head_local),
         [
@@ -815,19 +863,14 @@
     share_grad = einsum_f32("ld,lk->dk", normed_rows, share_low).reshape(count, 4, share_rows, share_cols)
     share_grad = lax.dynamic_index_in_dim(share_grad, shard_index, 1, keepdims=False)
     share_grad = share_grad.reshape(count * share_rows, share_cols)
-    mid_kept, mid_sent, _ = parted(
-        [(normed_rows, zq_low), (mix_grad_rows, mixed_low)], order, last_group
-    )
-    mid_half_sum = add(mid_kept, send(mid_sent, last_group, count))
     in_kept, in_sent, _ = parted([(normed_rows, in_low)], order, last_group)
     share_kept, share_sent, _ = split(share_grad, order, last_group, [share_rows])
     in_kept = jnp.concatenate([in_kept, share_kept], axis=0)
     in_sent = [jnp.concatenate(pair, axis=0) for pair in zip(in_sent, share_sent)]
-    mid_half_sum, gu_sum, block_low, *in_sent = lax.optimization_barrier(
-        (mid_half_sum, gu_sum, block_low, *in_sent)
-    )
-    mid_sum = add(*finish(mid_half_sum, stay, back, count))
-    in_half_sum = add(in_kept, send(in_sent, last_group, count))
+    mid_got, gu_got, block_low, in_sent = together(mid_got, gu_got, block_low, in_sent)
+    gu_sum = add(gu_kept, gu_got)
+    mid_kept, mid_got = finish(mid_kept, mid_got, stay, back, count)
+    in_got = send(in_sent, last_group, count)
     keep, give = call(
         input_back_kernel,
         [halves, halves],
@@ -869,17 +912,16 @@
     )
     for bits in (1, 2):
         small = group_sum(small, "tensor", 4, [bits])
-    in_half_sum, mid_sum, down_half_sum, out_give, small = together(
-        in_half_sum, mid_sum, down_half_sum, out_give, small
-    )
-    in_sum = add(*finish(in_half_sum, stay, back, count, [rows, share_rows]))
-    down_sum = add(*finish(down_half_sum, down_stay, back[1:] + last, count))
+    in_got, mid_got, down_got, out_give, small = together(in_got, mid_got, down_got, out_give, small)
+    mid_sum = add(mid_kept, mid_got)
+    in_sum = add(*finish(in_kept, in_got, stay, back, count, [rows, share_rows]))
+    down_sum = add(*finish(down_kept, down_got, down_stay, back[1:] + last, count))
     ffn_sum = finish_tensor(out_keep, out_give, shard_index)
     output = (hidden + ffn_sum).astype(BFLOAT)
     z_sum = mid_sum[:, :dt_start]
     out_sum = mid_sum[:, dt_start:]
     small = group_sum(small, "dp", count, last_group)
-    small, in_sum = together(small, in_sum)
+    small, in_sum, output = together(small, in_sum, output)
     for group in first:
         small = group_sum(small, "dp", count, group)
     shared_sum = in_sum[rows:]

time: 280 us -> 255 us (0.911)
  waiting for transfers between devices: 109 us -> 90.3 us
  starting transfers between devices: 63.4 us -> 60.1 us
    ppermute x50, waiting for transfers between devices: 109 us -> 90.3 us  [swap(): return lax.ppermute(values, axis, [(i, i ^ bits) for i in range(count)])]
    add x7 -> x3, other arithmetic: 6.07 us -> 1.37 us  [add(): kept = kept + part.astype(FLOAT)]
    ppermute x50, starting transfers between devices: 63.4 us -> 60.1 us  [swap(): return lax.ppermute(values, axis, [(i, i ^ bits) for i in range(count)])]
    unnamed x162 -> x186, local copies, waits for them, and re-layouts: 25.2 us -> 24.5 us
  transfers between devices with their start and end apart: 50 -> 50, of which waited for: 22 -> 20; matrix products, arithmetic and copies ran while one was open for 10% -> 11% of each run, Pallas kernels for 4% -> 3%
where the time goes in v3:
time: 255 us
  waiting for transfers between devices  90.3 us (35%)
  starting transfers between devices  60.1 us (24%)
  local copies, waits for them, and re-layouts  32.3 us (13%)
  blocking collectives  28.8 us (11%)
  other arithmetic  20.5 us (8%)
  Pallas kernels  20.1 us (8%)
    ppermute x50, waiting for transfers between devices, swap(): return lax.ppermute(values, axis, [(i, i ^ bits) for i in range(count)])  90.3 us
    ppermute x50, starting transfers between devices, swap(): return lax.ppermute(values, axis, [(i, i ^ bits) for i in range(count)])  60.1 us
    all_gather x4, blocking collectives, gather_tensor(): return lax.all_gather(values, 'tensor', axis=0, tiled=True)  28.8 us
    unnamed x186, local copies, waits for them, and re-layouts  24.5 us
    pallas_call x10, Pallas kernels, call(): pl.pallas_call(kernel, out_shape=[jax.ShapeDtypeStruct(shape, dtype) for...  14.5 us
  transfers between devices with their start and end apart: 50, of which 20 were waited for; matrix products, arithmetic and copies ran while one was open for 11% of the time, Pallas kernels for 3%

profile of v3, /device:TPU:0, one launch (start us, length us, event | category | flops | bytes accessed | tf_op | source)
XLA Modules:
  0.0 254.7 jit_solution(2746608031153525437)
XLA Ops:
  4.2 5.1 %collective-permute-start.2 = (bf16[128,768]{1,0:T(8,128)(2,1)S(1)}, bf16[128,768]{1,0:T(8,128)(2,1)S(1)}, u32[]{:S(2)}, u32[]{:S(2)}) collective-permute-start(bf16[128,768]{1,0:T(8,128)(2,1)S(1)} %fusion.13.refs_0_), channel_id=1, source_target_pairs={{0,24},{4,28},{8,16},{12,20},{16,8},{20,12},{24,0},{28,4},{1,25},{... | collective-permute-start | bytes 589832 | tf_op jit(solution)/shard_map/ppermute | solution.py:39
  13.7 7.2 %all_gather.12.normed_ref.refs_0_ = bf16[256,1024]{1,0:T(8,128)(2,1)S(1)} all-gather(bf16[64,1024]{1,0:T(8,128)(2,1)S(1)} %fusion.4), channel_id=1, replica_groups=mesh['dp'=8,'tensor'=4] {'tensor'}, dimensions={0}, use_global_device_ids=true | all-gather | bytes 655360 | tf_op jit(solution)/shard_map/all_gather | solution.py:654
  21.9 4.1 %collective-permute-done.1.refs_2_ = bf16[128,768]{1,0:T(8,128)(2,1)S(1)} collective-permute-done((bf16[128,768]{1,0:T(8,128)(2,1)S(1)}, bf16[128,768]{1,0:T(8,128)(2,1)S(1)}, u32[]{:S(2)}, u32[]{:S(2)}) %collective-permute-start.1) | collective-permute-done | bytes 196640 | tf_op jit(solution)/shard_map/ppermute | solution.py:39
  32.9 7.6 %all_gather.13.cot_ref.refs_0_ = bf16[256,1024]{1,0:T(8,128)(2,1)} all-gather(bf16[64,1024]{1,0:T(8,128)(2,1)S(1)} %get-tuple-element.135), channel_id=1, replica_groups=mesh['dp'=8,'tensor'=4] {'tensor'}, dimensions={0}, use_global_device_ids=true | all-gather | bytes 655360 | tf_op jit(solution)/shard_map/all_gather | solution.py:654
  40.6 7.3 %collective-permute-done.5.refs_2_ = bf16[128,896]{1,0:T(8,128)(2,1)S(1)} collective-permute-done((bf16[128,896]{1,0:T(8,128)(2,1)S(1)}, bf16[128,896]{1,0:T(8,128)(2,1)S(1)}, u32[]{:S(2)}, u32[]{:S(2)}) %collective-permute-start.5) | collective-permute-done | bytes 229408 | tf_op jit(solution)/shard_map/ppermute | solution.py:39
  55.5 2.8 %collective-permute-start.10 = (bf16[128,1024]{1,0:T(8,128)(2,1)}, bf16[128,1024]{1,0:T(8,128)(2,1)S(1)}, u32[]{:S(2)}, u32[]{:S(2)}) collective-permute-start(bf16[128,1024]{1,0:T(8,128)(2,1)} %pad_maximum_fusion.4.refs_0_), channel_id=1, source_target_pairs={{0,8},{4,12},{8,0},{12,4},{16,24},{20,28},{24,16},{28,20},{1,9},{5... | collective-permute-start | bytes 786440 | tf_op jit(solution)/shard_map/ppermute | solution.py:39
  58.4 7.4 %collective-permute-done.9 = bf16[2,8,32,512]{3,2,0,1:T(8,128)(2,1)} collective-permute-done((bf16[2,8,32,512]{3,2,0,1:T(8,128)(2,1)}, bf16[2,8,32,512]{3,2,0,1:T(8,128)(2,1)}, u32[]{:S(2)}, u32[]{:S(2)}) %collective-permute-start.9) | collective-permute-done | bytes 524320 | tf_op jit(solution)/shard_map/ppermute | solution.py:39
  68.6 2.6 %shard_map.242 = (f32[256,1792]{1,0:T(8,128)S(1)}, bf16[256,1024]{1,0:T(8,128)(2,1)S(1)}, f32[256,384]{1,0:T(8,128)S(1)}, bf16[256,128]{1,0:T(8,128)(2,1)S(1)}) custom-call(s32[1]{0:T(128)} %bitcast.14.owner_ref, bf16[256,1024]{1,0:T(8,128)(2,1)S(1)} %all_gather.12.normed_ref.refs_0_, bf16[512,768]{1,0:T(8,128)(2,1)S(1)} %shard_map.237.near_ref.early_near_ref, ...), custom_call_target="tpu_custom_call" | custom-call | flops 1000 | bytes 1000 | tf_op jit(solution)/shard_map/pallas_call | solution.py:586
  72.4 4.6 %collective-permute-done.11.refs_2_ = bf16[128,1024]{1,0:T(8,128)(2,1)S(1)} collective-permute-done((bf16[128,1024]{1,0:T(8,128)(2,1)}, bf16[128,1024]{1,0:T(8,128)(2,1)S(1)}, u32[]{:S(2)}, u32[]{:S(2)}) %collective-permute-start.11) | collective-permute-done | bytes 262176 | tf_op jit(solution)/shard_map/ppermute | solution.py:39
  91.6 6.7 %all_gather.14.rows_ref.refs_0_ = bf16[256,1024]{1,0:T(8,128)(2,1)S(1)} all-gather(bf16[64,1024]{1,0:T(8,128)(2,1)S(1)} %multiply_convert_fusion), channel_id=1, replica_groups=mesh['dp'=8,'tensor'=4] {'tensor'}, dimensions={0}, use_global_device_ids=true | all-gather | bytes 655360 | tf_op jit(solution)/shard_map/all_gather | solution.py:654
  98.4 11.9 %collective-permute-done.18.refs_4_ = bf16[256,512]{1,0:T(8,128)(2,1)S(1)} collective-permute-done((bf16[256,512]{1,0:T(8,128)(2,1)S(1)}, bf16[256,512]{1,0:T(8,128)(2,1)S(1)}, u32[]{:S(2)}, u32[]{:S(2)}) %collective-permute-start.18) | collective-permute-done | bytes 262176 | tf_op jit(solution)/shard_map/ppermute | solution.py:39
  131.4 7.2 %all_gather.15.grad_ref.refs_1_ = bf16[256,1024]{1,0:T(8,128)(2,1)S(1)} all-gather(bf16[64,1024]{1,0:T(8,128)(2,1)S(1)} %fusion.28), channel_id=1, replica_groups=mesh['dp'=8,'tensor'=4] {'tensor'}, dimensions={0}, use_global_device_ids=true | all-gather | bytes 655360 | tf_op jit(solution)/shard_map/all_gather | solution.py:654
  139.3 5.6 %collective-permute-done.22.refs_1_ = bf16[256,512]{1,0:T(8,128)(2,1)S(1)} collective-permute-done((bf16[256,512]{1,0:T(8,128)(2,1)}, bf16[256,512]{1,0:T(8,128)(2,1)S(1)}, u32[]{:S(2)}, u32[]{:S(2)}) %collective-permute-start.22) | collective-permute-done | bytes 262176 | tf_op jit(solution)/shard_map/ppermute | solution.py:39
  152.7 3.8 %shard_map.251 = (bf16[256,512]{1,0:T(8,128)(2,1)S(1)}, f32[8,640]{1,0:T(8,128)S(1)}, f32[8,128]{1,0:T(8,128)S(1)}, f32[256,512]{1,0:T(8,128)}) custom-call(s32[1]{0:T(128)} %bitcast.14.owner_ref, f32[256,384]{1,0:T(8,128)S(1)} %get-tuple-element.186.pre_grad_ref, f32[256,1792]{1,0:T(8,128)S(1)} %copy-done.16, bf16[256,1024]{1,0:T(8,128)(2,1)S(1)} %copy-done.14, ...), custom_call_target="tpu_custom_call" | custom-call | flops 1000 | bytes 1000 | tf_op jit(solution)/shard_map/pallas_call | solution.py:586
  160.0 4.6 %collective-permute-start.27 = (bf16[128,1024]{1,0:T(8,128)(2,1)}, bf16[128,1024]{1,0:T(8,128)(2,1)S(1)}, u32[]{:S(2)}, u32[]{:S(2)}) collective-permute-start(bf16[128,1024]{1,0:T(8,128)(2,1)} %copy-done.55), channel_id=1, source_target_pairs={{0,8},{4,12},{8,0},{12,4},{16,24},{20,28},{24,16},{28,20},{1,9},{5... | collective-permute-start | bytes 786440 | tf_op jit(solution)/shard_map/ppermute | solution.py:39
  171.2 7.3 %collective-permute-done.31 = bf16[256,512]{1,0:T(8,128)(2,1)S(1)} collective-permute-done((bf16[256,512]{1,0:T(8,128)(2,1)S(1)}, bf16[256,512]{1,0:T(8,128)(2,1)S(1)}, u32[]{:S(2)}, u32[]{:S(2)}) %collective-permute-start.31) | collective-permute-done | bytes 262176 | tf_op jit(solution)/shard_map/ppermute | solution.py:39
  179.3 6.8 %collective-permute-done.28 = bf16[128,1024]{1,0:T(8,128)(2,1)S(1)} collective-permute-done((bf16[128,1024]{1,0:T(8,128)(2,1)}, bf16[128,1024]{1,0:T(8,128)(2,1)S(1)}, u32[]{:S(2)}, u32[]{:S(2)}) %collective-permute-start.28) | collective-permute-done | bytes 262176 | tf_op jit(solution)/shard_map/ppermute | solution.py:39
  186.1 6.2 %collective-permute-done.26.refs_0_ = bf16[512,1024]{1,0:T(8,128)(2,1)S(1)} collective-permute-done((bf16[512,1024]{1,0:T(8,128)(2,1)}, bf16[512,1024]{1,0:T(8,128)(2,1)S(1)}, u32[]{:S(2)}, u32[]{:S(2)}) %collective-permute-start.26) | collective-permute-done | bytes 1048608 | tf_op jit(solution)/shard_map/ppermute | solution.py:39
  199.2 4.5 %collective-permute-done.37 = bf16[64,1024]{1,0:T(8,128)(2,1)S(1)} collective-permute-done((bf16[64,1024]{1,0:T(8,128)(2,1)S(1)}, bf16[64,1024]{1,0:T(8,128)(2,1)S(1)}, u32[]{:S(2)}, u32[]{:S(2)}) %collective-permute-start.37) | collective-permute-done | bytes 131104 | tf_op jit(solution)/shard_map/ppermute | solution.py:39
  207.1 3.7 %collective-permute-done.39 = f32[8,1792]{1,0:T(8,128)S(1)} collective-permute-done((f32[8,1792]{1,0:T(8,128)S(1)}, f32[8,1792]{1,0:T(8,128)S(1)}, u32[]{:S(2)}, u32[]{:S(2)}) %collective-permute-start.39) | collective-permute-done | bytes 57376 | tf_op jit(solution)/shard_map/ppermute | solution.py:39
  211.4 4.5 %collective-permute-done.34 = bf16[128,1024]{1,0:T(8,128)(2,1)S(1)} collective-permute-done((bf16[128,1024]{1,0:T(8,128)(2,1)S(1)}, bf16[128,1024]{1,0:T(8,128)(2,1)S(1)}, u32[]{:S(2)}, u32[]{:S(2)}) %collective-permute-start.34) | collective-permute-done | bytes 262176 | tf_op jit(solution)/shard_map/ppermute | solution.py:39
  216.0 4.0 %collective-permute-done.32.refs_0_ = bf16[640,512]{1,0:T(8,128)(2,1)S(1)} collective-permute-done((bf16[640,512]{1,0:T(8,128)(2,1)S(1)}, bf16[640,512]{1,0:T(8,128)(2,1)S(1)}, u32[]{:S(2)}, u32[]{:S(2)}) %collective-permute-start.32) | collective-permute-done | bytes 655392 | tf_op jit(solution)/shard_map/ppermute | solution.py:39
  234.8 7.6 %collective-permute-done.42 = bf16[160,512]{1,0:T(8,128)(2,1)} collective-permute-done((bf16[160,512]{1,0:T(8,128)(2,1)S(1)}, bf16[160,512]{1,0:T(8,128)(2,1)}, u32[]{:S(2)}, u32[]{:S(2)}) %collective-permute-start.42) | collective-permute-done | bytes 163872 | tf_op jit(solution)/shard_map/ppermute | solution.py:39
  245.3 3.0 %collective-permute-start.48 = (f32[8,1792]{1,0:T(8,128)S(1)}, f32[8,1792]{1,0:T(8,128)S(1)}, u32[]{:S(2)}, u32[]{:S(2)}) collective-permute-start(f32[8,1792]{1,0:T(8,128)S(1)} %add.159), channel_id=1, source_target_pairs={{0,16},{4,20},{8,24},{12,28},{16,0},{20,4},{24,8},{28,12},{1,17},{... | collective-permute-start | bytes 172040 | tf_op jit(solution)/shard_map/ppermute | solution.py:39
  (383 shorter events, 116.3 us)
Async XLA Ops:
  4.2 17.7 %collective-permute-start.2 = (bf16[128,768]{1,0:T(8,128)(2,1)S(1)}, bf16[128,768]{1,0:T(8,128)(2,1)S(1)}, u32[]{:S(2)}, u32[]{:S(2)}) collective-permute-start(bf16[128,768]{1,0:T(8,128)(2,1)S(1)} %fusion.13.refs_0_), channel_id=1, source_target_pairs={{0,24},{4,28},{8,16},{12,20},{16,8},{20,12},{24,0},{28,4},{1,25},{... | collective-permute-start | bytes 589832 | tf_op jit(solution)/shard_map/ppermute | solution.py:39
  9.4 16.7 %collective-permute-start.1 = (bf16[128,768]{1,0:T(8,128)(2,1)S(1)}, bf16[128,768]{1,0:T(8,128)(2,1)S(1)}, u32[]{:S(2)}, u32[]{:S(2)}) collective-permute-start(bf16[128,768]{1,0:T(8,128)(2,1)S(1)} %fusion.13.refs_0_), channel_id=1, source_target_pairs={{0,16},{4,20},{8,24},{12,28},{16,0},{20,4},{24,8},{28,12},{1,17},{... | collective-permute-start | bytes 589832 | tf_op jit(solution)/shard_map/ppermute | solution.py:39
  9.4 16.7 %collective-permute-start = (bf16[128,768]{1,0:T(8,128)(2,1)S(1)}, bf16[128,768]{1,0:T(8,128)(2,1)S(1)}, u32[]{:S(2)}, u32[]{:S(2)}) collective-permute-start(bf16[128,768]{1,0:T(8,128)(2,1)S(1)} %fusion.13.refs_0_), channel_id=1, source_target_pairs={{0,8},{4,12},{8,0},{12,4},{16,24},{20,28},{24,16},{28,20},{1,9},{5... | collective-permute-start | bytes 589832 | tf_op jit(solution)/shard_map/ppermute | solution.py:39
  26.1 21.8 %collective-permute-start.7 = (bf16[512,768]{1,0:T(8,128)(2,1)S(1)}, bf16[512,768]{1,0:T(8,128)(2,1)S(1)}, u32[]{:S(2)}, u32[]{:S(2)}) collective-permute-start(bf16[512,768]{1,0:T(8,128)(2,1)S(1)} %shard_map.237.near_ref.early_near_ref), channel_id=1, source_target_pairs={{0,4},{4,0},{8,12},{12,8},{16,20},{20,16},{24,28},{28,24},{1,5},{5... | collective-permute-start | bytes 2359304 | tf_op jit(solution)/shard_map/ppermute | solution.py:39
  30.3 17.6 %collective-permute-start.5 = (bf16[128,896]{1,0:T(8,128)(2,1)S(1)}, bf16[128,896]{1,0:T(8,128)(2,1)S(1)}, u32[]{:S(2)}, u32[]{:S(2)}) collective-permute-start(bf16[128,896]{1,0:T(8,128)(2,1)S(1)} %pad_maximum_fusion.7.refs_0_), channel_id=1, source_target_pairs={{0,16},{4,20},{8,24},{12,28},{16,0},{20,4},{24,8},{28,12},{1,17},{... | collective-permute-start | bytes 688136 | tf_op jit(solution)/shard_map/ppermute | solution.py:39
  30.3 17.6 %collective-permute-start.4 = (bf16[128,896]{1,0:T(8,128)(2,1)S(1)}, bf16[128,896]{1,0:T(8,128)(2,1)S(1)}, u32[]{:S(2)}, u32[]{:S(2)}) collective-permute-start(bf16[128,896]{1,0:T(8,128)(2,1)S(1)} %pad_maximum_fusion.7.refs_0_), channel_id=1, source_target_pairs={{0,8},{4,12},{8,0},{12,4},{16,24},{20,28},{24,16},{28,20},{1,9},{5... | collective-permute-start | bytes 688136 | tf_op jit(solution)/shard_map/ppermute | solution.py:39
  53.3 24.8 %collective-permute-start.13 = (bf16[512,896]{1,0:T(8,128)(2,1)S(1)}, bf16[512,896]{1,0:T(8,128)(2,1)S(1)}, u32[]{:S(2)}, u32[]{:S(2)}) collective-permute-start(bf16[512,896]{1,0:T(8,128)(2,1)S(1)} %shard_map.241.near_ref), channel_id=1, source_target_pairs={{0,4},{4,0},{8,12},{12,8},{16,20},{20,16},{24,28},{28,24},{1,5},{5... | collective-permute-start | bytes 2752520 | tf_op jit(solution)/shard_map/ppermute | solution.py:39
  53.9 18.5 %collective-permute-start.12 = (bf16[128,1024]{1,0:T(8,128)(2,1)}, bf16[128,1024]{1,0:T(8,128)(2,1)S(1)}, u32[]{:S(2)}, u32[]{:S(2)}) collective-permute-start(bf16[128,1024]{1,0:T(8,128)(2,1)} %pad_maximum_fusion.4.refs_0_), channel_id=1, source_target_pairs={{0,24},{4,28},{8,16},{12,20},{16,8},{20,12},{24,0},{28,4},{1,25},{... | collective-permute-start | bytes 786440 | tf_op jit(solution)/shard_map/ppermute | solution.py:39
  55.5 21.5 %collective-permute-start.11 = (bf16[128,1024]{1,0:T(8,128)(2,1)}, bf16[128,1024]{1,0:T(8,128)(2,1)S(1)}, u32[]{:S(2)}, u32[]{:S(2)}) collective-permute-start(bf16[128,1024]{1,0:T(8,128)(2,1)} %pad_maximum_fusion.4.refs_0_), channel_id=1, source_target_pairs={{0,16},{4,20},{8,24},{12,28},{16,0},{20,4},{24,8},{28,12},{1,17},{... | collective-permute-start | bytes 786440 | tf_op jit(solution)/shard_map/ppermute | solution.py:39
  55.5 21.5 %collective-permute-start.10 = (bf16[128,1024]{1,0:T(8,128)(2,1)}, bf16[128,1024]{1,0:T(8,128)(2,1)S(1)}, u32[]{:S(2)}, u32[]{:S(2)}) collective-permute-start(bf16[128,1024]{1,0:T(8,128)(2,1)} %pad_maximum_fusion.4.refs_0_), channel_id=1, source_target_pairs={{0,8},{4,12},{8,0},{12,4},{16,24},{20,28},{24,16},{28,20},{1,9},{5... | collective-permute-start | bytes 786440 | tf_op jit(solution)/shard_map/ppermute | solution.py:39
  82.2 28.1 %collective-permute-start.16 = (bf16[512,1024]{1,0:T(8,128)(2,1)}, bf16[512,1024]{1,0:T(8,128)(2,1)S(1)}, u32[]{:S(2)}, u32[]{:S(2)}) collective-permute-start(bf16[512,1024]{1,0:T(8,128)(2,1)} %copy-done.4), channel_id=1, source_target_pairs={{0,4},{4,0},{8,12},{12,8},{16,20},{20,16},{24,28},{28,24},{1,5},{5... | collective-permute-start | bytes 3145736 | tf_op jit(solution)/shard_map/ppermute | solution.py:39
  88.6 21.6 %collective-permute-start.18 = (bf16[256,512]{1,0:T(8,128)(2,1)S(1)}, bf16[256,512]{1,0:T(8,128)(2,1)S(1)}, u32[]{:S(2)}, u32[]{:S(2)}) collective-permute-start(bf16[256,512]{1,0:T(8,128)(2,1)S(1)} %copy-done.22), channel_id=1, source_target_pairs={{0,16},{4,20},{8,24},{12,28},{16,0},{20,4},{24,8},{28,12},{1,17},{... | collective-permute-start | bytes 786440 | tf_op jit(solution)/shard_map/ppermute | solution.py:39
  88.6 21.6 %collective-permute-start.17 = (bf16[256,512]{1,0:T(8,128)(2,1)S(1)}, bf16[256,512]{1,0:T(8,128)(2,1)S(1)}, u32[]{:S(2)}, u32[]{:S(2)}) collective-permute-start(bf16[256,512]{1,0:T(8,128)(2,1)S(1)} %copy-done.22), channel_id=1, source_target_pairs={{0,8},{4,12},{8,0},{12,4},{16,24},{20,28},{24,16},{28,20},{1,9},{5... | collective-permute-start | bytes 786440 | tf_op jit(solution)/shard_map/ppermute | solution.py:39
  119.4 26.9 %collective-permute-start.20 = (bf16[512,1024]{1,0:T(8,128)(2,1)}, bf16[512,1024]{1,0:T(8,128)(2,1)}, u32[]{:S(2)}, u32[]{:S(2)}) collective-permute-start(bf16[512,1024]{1,0:T(8,128)(2,1)} %get-tuple-element.163), channel_id=1, source_target_pairs={{0,4},{4,0},{8,12},{12,8},{16,20},{20,16},{24,28},{28,24},{1,5},{5... | collective-permute-start | bytes 3145736 | tf_op jit(solution)/shard_map/ppermute | solution.py:39
  123.4 21.5 %collective-permute-start.22 = (bf16[256,512]{1,0:T(8,128)(2,1)}, bf16[256,512]{1,0:T(8,128)(2,1)S(1)}, u32[]{:S(2)}, u32[]{:S(2)}) collective-permute-start(bf16[256,512]{1,0:T(8,128)(2,1)} %copy-done.57), channel_id=1, source_target_pairs={{0,16},{4,20},{8,24},{12,28},{16,0},{20,4},{24,8},{28,12},{1,17},{... | collective-permute-start | bytes 786440 | tf_op jit(solution)/shard_map/ppermute | solution.py:39
  125.5 20.1 %collective-permute-start.23 = (bf16[256,512]{1,0:T(8,128)(2,1)}, bf16[256,512]{1,0:T(8,128)(2,1)S(1)}, u32[]{:S(2)}, u32[]{:S(2)}) collective-permute-start(bf16[256,512]{1,0:T(8,128)(2,1)} %copy-done.56), channel_id=1, source_target_pairs={{0,24},{4,28},{8,16},{12,20},{16,8},{20,12},{24,0},{28,4},{1,25},{... | collective-permute-start | bytes 786440 | tf_op jit(solution)/shard_map/ppermute | solution.py:39
  160.0 19.3 %collective-permute-start.27 = (bf16[128,1024]{1,0:T(8,128)(2,1)}, bf16[128,1024]{1,0:T(8,128)(2,1)S(1)}, u32[]{:S(2)}, u32[]{:S(2)}) collective-permute-start(bf16[128,1024]{1,0:T(8,128)(2,1)} %copy-done.55), channel_id=1, source_target_pairs={{0,8},{4,12},{8,0},{12,4},{16,24},{20,28},{24,16},{28,20},{1,9},{5... | collective-permute-start | bytes 786440 | tf_op jit(solution)/shard_map/ppermute | solution.py:39
  164.6 21.5 %collective-permute-start.28 = (bf16[128,1024]{1,0:T(8,128)(2,1)}, bf16[128,1024]{1,0:T(8,128)(2,1)S(1)}, u32[]{:S(2)}, u32[]{:S(2)}) collective-permute-start(bf16[128,1024]{1,0:T(8,128)(2,1)} %copy-done.54), channel_id=1, source_target_pairs={{0,16},{4,20},{8,24},{12,28},{16,0},{20,4},{24,8},{28,12},{1,17},{... | collective-permute-start | bytes 786440 | tf_op jit(solution)/shard_map/ppermute | solution.py:39
  164.7 21.4 %collective-permute-start.29 = (bf16[128,1024]{1,0:T(8,128)(2,1)}, bf16[128,1024]{1,0:T(8,128)(2,1)S(1)}, u32[]{:S(2)}, u32[]{:S(2)}) collective-permute-start(bf16[128,1024]{1,0:T(8,128)(2,1)} %copy-done.53), channel_id=1, source_target_pairs={{0,24},{4,28},{8,16},{12,20},{16,8},{20,12},{24,0},{28,4},{1,25},{... | collective-permute-start | bytes 786440 | tf_op jit(solution)/shard_map/ppermute | solution.py:39
  167.0 25.3 %collective-permute-start.26 = (bf16[512,1024]{1,0:T(8,128)(2,1)}, bf16[512,1024]{1,0:T(8,128)(2,1)S(1)}, u32[]{:S(2)}, u32[]{:S(2)}) collective-permute-start(bf16[512,1024]{1,0:T(8,128)(2,1)} %copy-done.50), channel_id=1, source_target_pairs={{0,4},{4,0},{8,12},{12,8},{16,20},{20,16},{24,28},{28,24},{1,5},{5... | collective-permute-start | bytes 3145736 | tf_op jit(solution)/shard_map/ppermute | solution.py:39
  193.8 17.6 %collective-permute-start.33 = (bf16[128,1024]{1,0:T(8,128)(2,1)S(1)}, bf16[128,1024]{1,0:T(8,128)(2,1)S(1)}, u32[]{:S(2)}, u32[]{:S(2)}) collective-permute-start(bf16[128,1024]{1,0:T(8,128)(2,1)S(1)} %get-tuple-element.196), channel_id=1, source_target_pairs={{0,8},{4,12},{8,0},{12,4},{16,24},{20,28},{24,16},{28,20},{1,9},{5... | collective-permute-start | bytes 786440 | tf_op jit(solution)/shard_map/ppermute | solution.py:39
  194.7 21.3 %collective-permute-start.34 = (bf16[128,1024]{1,0:T(8,128)(2,1)S(1)}, bf16[128,1024]{1,0:T(8,128)(2,1)S(1)}, u32[]{:S(2)}, u32[]{:S(2)}) collective-permute-start(bf16[128,1024]{1,0:T(8,128)(2,1)S(1)} %get-tuple-element.197), channel_id=1, source_target_pairs={{0,16},{4,20},{8,24},{12,28},{16,0},{20,4},{24,8},{28,12},{1,17},{... | collective-permute-start | bytes 786440 | tf_op jit(solution)/shard_map/ppermute | solution.py:39
  196.0 20.0 %collective-permute-start.35 = (bf16[128,1024]{1,0:T(8,128)(2,1)S(1)}, bf16[128,1024]{1,0:T(8,128)(2,1)S(1)}, u32[]{:S(2)}, u32[]{:S(2)}) collective-permute-start(bf16[128,1024]{1,0:T(8,128)(2,1)S(1)} %get-tuple-element.198), channel_id=1, source_target_pairs={{0,24},{4,28},{8,16},{12,20},{16,8},{20,12},{24,0},{28,4},{1,25},{... | collective-permute-start | bytes 786440 | tf_op jit(solution)/shard_map/ppermute | solution.py:39
  204.6 15.4 %collective-permute-start.32 = (bf16[640,512]{1,0:T(8,128)(2,1)S(1)}, bf16[640,512]{1,0:T(8,128)(2,1)S(1)}, u32[]{:S(2)}, u32[]{:S(2)}) collective-permute-start(bf16[640,512]{1,0:T(8,128)(2,1)S(1)} %fusion.22), channel_id=1, source_target_pairs={{0,4},{4,0},{8,12},{12,8},{16,20},{20,16},{24,28},{28,24},{1,5},{5... | collective-permute-start | bytes 1966088 | tf_op jit(solution)/shard_map/ppermute | solution.py:39
  (112 other events, 868.8 us)

commit v4 on v3

--- a/solution.py
+++ b/solution.py
@@ -142,11 +142,11 @@
     return found
 
 
-def products_kernel(runs_of, block, widths, *refs):
-    lefts, rights, outs = refs[: len(widths)], refs[len(widths) : 2 * len(widths)], refs[2 * len(widths) :]
+def write_products(runs_of, block, lefts, rights, outs):
     start = 0
-    for left, right, width in zip(lefts, rights, widths):
+    for left, right in zip(lefts, rights):
         right_now = right[...]
+        width = right_now.shape[1]
         for out, runs in zip(outs, runs_of):
             row = 0
             for col, n in runs:
@@ -156,8 +156,11 @@
         start += width
 
 
-def parted(pairs, order, group):
-    block = pairs[0][0].shape[1] // len(order)
+def products_kernel(runs_of, block, count, *refs):
+    write_products(runs_of, block, refs[:count], refs[count : 2 * count], refs[2 * count :])
+
+
+def plan(order, group):
     span = 0
     for m in group:
         span |= m
@@ -172,10 +175,19 @@
             else:
                 runs.append((col, 1))
         runs_of.append(runs)
-    widths = [right.shape[1] for _, right in pairs]
-    shape = (len(stay) * block, sum(widths))
+    return runs_of, stay
+
+
+def product_shapes(stay, block, width, group):
+    return [((len(stay) * block, width), FLOAT)] + [((len(stay) * block, width), BFLOAT)] * len(group)
+
+
+def parted(pairs, order, group):
+    block = pairs[0][0].shape[1] // len(order)
+    runs_of, stay = plan(order, group)
+    shape = (len(stay) * block, sum(right.shape[1] for _, right in pairs))
     kept, *sent = pl.pallas_call(
-        functools.partial(products_kernel, runs_of, block, widths),
+        functools.partial(products_kernel, runs_of, block, len(pairs)),
         out_shape=[jax.ShapeDtypeStruct(shape, FLOAT)]
         + [jax.ShapeDtypeStruct(shape, BFLOAT)] * len(group),
         in_specs=[WHOLE] * (2 * len(pairs)),
@@ -609,11 +621,13 @@
 
 
 def ffn_kernel(
-    gu_runs, down_runs, core_ref, rows_ref, cot_ref, *refs
+    gu_runs, down_runs, gu_plan, down_plan, core_ref, rows_ref, cot_ref, *refs
 ):
     gu_refs, refs = refs[: len(gu_runs)], refs[len(gu_runs) :]
     down_refs, refs = refs[: len(down_runs)], refs[len(down_runs) :]
-    gu_low_ref, act_ref, keep_ref, give_ref, out_keep_ref, out_give_ref = refs
+    keep_ref, give_ref, out_keep_ref, out_give_ref, *refs = refs
+    gu_outs, refs = refs[: len(gu_plan)], refs[len(gu_plan) :]
+    down_outs, (gu_low_ref, act_ref) = refs[: len(down_plan)], refs[len(down_plan) :]
     width = act_ref.shape[1]
     block = sum(n for runs in gu_runs for _, _, n in runs)
     block = rows_ref.shape[1] // block
@@ -648,6 +662,8 @@
     gu_low_ref[:, width:] = (act_grad * silu).astype(BFLOAT)
     outer(gu_low_ref[...], gu_refs, gu_runs, keep_ref, give_ref)
     outer(act, down_refs, down_runs, out_keep_ref, out_give_ref)
+    write_products(gu_plan, block, [rows_ref], [gu_low_ref], gu_outs)
+    write_products(down_plan, block, [cot_ref], [act_ref], down_outs)
 
 
 def gather_tensor(values):
@@ -785,19 +801,27 @@
     hidden = token_f + finish_tensor(keep, give, shard_index)
     normed_two, norm_two_back = jax.vjp(rms_norm, hidden, gains[1])
     ffn_rows = gather_tensor(normed_two.astype(BFLOAT))
-    gu_low, act_low, keep, give, out_keep, out_give = call(
-        functools.partial(ffn_kernel, column_runs(gu_places, order), column_runs(down_places, order)),
-        [((length, 2 * ff_local), BFLOAT), ((length, ff_local), BFLOAT), halves, halves, halves, halves],
+    last_group = last[0]
+    back = groups[:-1][::-1]
+    gu_plan, stay = plan(order, last_group)
+    down_plan, down_stay = plan(order, back[0])
+    keep, give, out_keep, out_give, *found = call(
+        functools.partial(
+            ffn_kernel, column_runs(gu_places, order), column_runs(down_places, order), gu_plan, down_plan
+        ),
+        [halves] * 4
+        + product_shapes(stay, rows, 2 * ff_local, last_group)
+        + product_shapes(down_stay, rows, ff_local, back[0]),
         core,
         ffn_rows,
         cot_rows,
         *gu_parts,
         *down_parts,
-    )
-    last_group = last[0]
-    back = groups[:-1][::-1]
-    down_kept, down_sent, down_stay = parted([(cot_rows, act_low)], order, back[0])
-    gu_kept, gu_sent, stay = parted([(ffn_rows, gu_low)], order, last_group)
+        scratch=[pltpu.VMEM((length, 2 * ff_local), BFLOAT), pltpu.VMEM((length, ff_local), BFLOAT)],
+    )
+    gu_found, down_found = found[: len(gu_plan)], found[len(gu_plan) :]
+    gu_kept, gu_sent = gu_found[0], gu_found[1:]
+    down_kept, down_sent = down_found[0], down_found[1:]
     gu_sent, down_sent, seg_row = together(gu_sent, down_sent, seg_row)
     gu_got = send(gu_sent, last_group, count)
     down_got = send(down_sent, back[0], count)

time: 255 us -> 253 us (level)
    unnamed x186 -> x182, local copies, waits for them, and re-layouts: 24.5 us -> 22.8 us
  transfers between devices with their start and end apart: 50 -> 50, of which waited for: 20 -> 22; matrix products, arithmetic and copies ran while one was open for 11% -> 10% of each run, Pallas kernels for 3% -> 2%
where the time goes in v4:
time: 253 us; the launch traced here: 252 us
  waiting for transfers between devices  90.9 us (36%)
  starting transfers between devices  62.2 us (25%)
  local copies, waits for them, and re-layouts  29.8 us (12%)
  blocking collectives  28.7 us (11%)
  Pallas kernels  19.4 us (8%)
  other arithmetic  18.4 us (7%)
    ppermute x50, waiting for transfers between devices, swap(): return lax.ppermute(values, axis, [(i, i ^ bits) for i in range(count)])  90.9 us
    ppermute x50, starting transfers between devices, swap(): return lax.ppermute(values, axis, [(i, i ^ bits) for i in range(count)])  62.2 us
    all_gather x4, blocking collectives, gather_tensor(): return lax.all_gather(values, 'tensor', axis=0, tiled=True)  28.7 us
    unnamed x182, local copies, waits for them, and re-layouts  22.8 us
    pallas_call x10, Pallas kernels, call(): pl.pallas_call(kernel, out_shape=[jax.ShapeDtypeStruct(shape, dtype) for...  16 us
  transfers between devices with their start and end apart: 50, of which 22 were waited for; matrix products, arithmetic and copies ran while one was open for 10% of the time, Pallas kernels for 2%

profile of v4, /device:TPU:0, one launch (start us, length us, event | category | flops | bytes accessed | tf_op | source)
XLA Modules:
  0.0 252.0 jit_solution(1570490786404768665)
XLA Ops:
  4.2 5.1 %collective-permute-start.2 = (bf16[128,768]{1,0:T(8,128)(2,1)S(1)}, bf16[128,768]{1,0:T(8,128)(2,1)S(1)}, u32[]{:S(2)}, u32[]{:S(2)}) collective-permute-start(bf16[128,768]{1,0:T(8,128)(2,1)S(1)} %fusion.13.refs_0_), channel_id=1, source_target_pairs={{0,24},{4,28},{8,16},{12,20},{16,8},{20,12},{24,0},{28,4},{1,25},{... | collective-permute-start | bytes 589832 | tf_op jit(solution)/shard_map/ppermute | solution.py:39
  13.6 7.2 %all_gather.12.normed_ref.refs_0_ = bf16[256,1024]{1,0:T(8,128)(2,1)S(1)} all-gather(bf16[64,1024]{1,0:T(8,128)(2,1)S(1)} %fusion.4), channel_id=1, replica_groups=mesh['dp'=8,'tensor'=4] {'tensor'}, dimensions={0}, use_global_device_ids=true | all-gather | bytes 655360 | tf_op jit(solution)/shard_map/all_gather | solution.py:670
  21.9 4.2 %collective-permute-done.1.refs_2_ = bf16[128,768]{1,0:T(8,128)(2,1)S(1)} collective-permute-done((bf16[128,768]{1,0:T(8,128)(2,1)S(1)}, bf16[128,768]{1,0:T(8,128)(2,1)S(1)}, u32[]{:S(2)}, u32[]{:S(2)}) %collective-permute-start.1) | collective-permute-done | bytes 196640 | tf_op jit(solution)/shard_map/ppermute | solution.py:39
  32.9 7.6 %all_gather.13.cot_ref = bf16[256,1024]{1,0:T(8,128)(2,1)} all-gather(bf16[64,1024]{1,0:T(8,128)(2,1)S(1)} %get-tuple-element.133), channel_id=1, replica_groups=mesh['dp'=8,'tensor'=4] {'tensor'}, dimensions={0}, use_global_device_ids=true | all-gather | bytes 655360 | tf_op jit(solution)/shard_map/all_gather | solution.py:670
  40.5 7.3 %collective-permute-done.5.refs_2_ = bf16[128,896]{1,0:T(8,128)(2,1)S(1)} collective-permute-done((bf16[128,896]{1,0:T(8,128)(2,1)S(1)}, bf16[128,896]{1,0:T(8,128)(2,1)S(1)}, u32[]{:S(2)}, u32[]{:S(2)}) %collective-permute-start.5) | collective-permute-done | bytes 229408 | tf_op jit(solution)/shard_map/ppermute | solution.py:39
  55.5 2.8 %collective-permute-start.10 = (bf16[128,1024]{1,0:T(8,128)(2,1)}, bf16[128,1024]{1,0:T(8,128)(2,1)S(1)}, u32[]{:S(2)}, u32[]{:S(2)}) collective-permute-start(bf16[128,1024]{1,0:T(8,128)(2,1)} %pad_maximum_fusion.4.refs_0_), channel_id=1, source_target_pairs={{0,8},{4,12},{8,0},{12,4},{16,24},{20,28},{24,16},{28,20},{1,9},{5... | collective-permute-start | bytes 786440 | tf_op jit(solution)/shard_map/ppermute | solution.py:39
  58.4 7.4 %collective-permute-done.9 = bf16[2,8,32,512]{3,2,0,1:T(8,128)(2,1)} collective-permute-done((bf16[2,8,32,512]{3,2,0,1:T(8,128)(2,1)}, bf16[2,8,32,512]{3,2,0,1:T(8,128)(2,1)}, u32[]{:S(2)}, u32[]{:S(2)}) %collective-permute-start.9) | collective-permute-done | bytes 524320 | tf_op jit(solution)/shard_map/ppermute | solution.py:39
  72.5 4.5 %collective-permute-done.11.refs_2_ = bf16[128,1024]{1,0:T(8,128)(2,1)S(1)} collective-permute-done((bf16[128,1024]{1,0:T(8,128)(2,1)}, bf16[128,1024]{1,0:T(8,128)(2,1)S(1)}, u32[]{:S(2)}, u32[]{:S(2)}) %collective-permute-start.11) | collective-permute-done | bytes 262176 | tf_op jit(solution)/shard_map/ppermute | solution.py:39
  91.6 6.6 %all_gather.14.rows_ref = bf16[256,1024]{1,0:T(8,128)(2,1)S(1)} all-gather(bf16[64,1024]{1,0:T(8,128)(2,1)S(1)} %multiply_convert_fusion), channel_id=1, replica_groups=mesh['dp'=8,'tensor'=4] {'tensor'}, dimensions={0}, use_global_device_ids=true | all-gather | bytes 655360 | tf_op jit(solution)/shard_map/all_gather | solution.py:670
  98.1 12.0 %collective-permute-done.18.refs_4_ = bf16[256,512]{1,0:T(8,128)(2,1)S(1)} collective-permute-done((bf16[256,512]{1,0:T(8,128)(2,1)S(1)}, bf16[256,512]{1,0:T(8,128)(2,1)S(1)}, u32[]{:S(2)}, u32[]{:S(2)}) %collective-permute-start.18) | collective-permute-done | bytes 262176 | tf_op jit(solution)/shard_map/ppermute | solution.py:39
  110.2 4.1 %shard_map.245 = (f32[2,64,1024]{2,1,0:T(8,128)S(1)}, f32[2,64,1024]{2,1,0:T(8,128)S(1)}, f32[2,64,1024]{2,1,0:T(8,128)S(1)}, f32[2,64,1024]{2,1,0:T(8,128)S(1)}...) custom-call(s32[1]{0:T(128)} %bitcast.11.core_ref, ...), custom_call_target="tpu_custom_call" | custom-call | flops 1000 | bytes 1000 | tf_op jit(solution)/shard_map/pallas_call | solution.py:598
  129.0 7.3 %all_gather.15.grad_ref.refs_1_ = bf16[256,1024]{1,0:T(8,128)(2,1)S(1)} all-gather(bf16[64,1024]{1,0:T(8,128)(2,1)S(1)} %fusion.28), channel_id=1, replica_groups=mesh['dp'=8,'tensor'=4] {'tensor'}, dimensions={0}, use_global_device_ids=true | all-gather | bytes 655360 | tf_op jit(solution)/shard_map/all_gather | solution.py:670
  137.0 5.5 %collective-permute-done.22.refs_1_ = bf16[256,512]{1,0:T(8,128)(2,1)S(1)} collective-permute-done((bf16[256,512]{1,0:T(8,128)(2,1)}, bf16[256,512]{1,0:T(8,128)(2,1)S(1)}, u32[]{:S(2)}, u32[]{:S(2)}) %collective-permute-start.22) | collective-permute-done | bytes 262176 | tf_op jit(solution)/shard_map/ppermute | solution.py:39
  150.2 3.8 %shard_map.249 = (bf16[256,512]{1,0:T(8,128)(2,1)S(1)}, f32[8,640]{1,0:T(8,128)S(1)}, f32[8,128]{1,0:T(8,128)S(1)}, f32[256,512]{1,0:T(8,128)}) custom-call(s32[1]{0:T(128)} %bitcast.14.owner_ref, f32[256,384]{1,0:T(8,128)S(1)} %get-tuple-element.182.pre_grad_ref, f32[256,1792]{1,0:T(8,128)S(1)} %copy-done.16, bf16[256,1024]{1,0:T(8,128)(2,1)S(1)} %copy-done.14, ...), custom_call_target="tpu_custom_call" | custom-call | flops 1000 | bytes 1000 | tf_op jit(solution)/shard_map/pallas_call | solution.py:598
  157.5 4.5 %collective-permute-start.27 = (bf16[128,1024]{1,0:T(8,128)(2,1)}, bf16[128,1024]{1,0:T(8,128)(2,1)S(1)}, u32[]{:S(2)}, u32[]{:S(2)}) collective-permute-start(bf16[128,1024]{1,0:T(8,128)(2,1)} %copy-done.55), channel_id=1, source_target_pairs={{0,8},{4,12},{8,0},{12,4},{16,24},{20,28},{24,16},{28,20},{1,9},{5... | collective-permute-start | bytes 786440 | tf_op jit(solution)/shard_map/ppermute | solution.py:39
  169.6 7.3 %collective-permute-done.31 = bf16[256,512]{1,0:T(8,128)(2,1)S(1)} collective-permute-done((bf16[256,512]{1,0:T(8,128)(2,1)S(1)}, bf16[256,512]{1,0:T(8,128)(2,1)S(1)}, u32[]{:S(2)}, u32[]{:S(2)}) %collective-permute-start.31) | collective-permute-done | bytes 262176 | tf_op jit(solution)/shard_map/ppermute | solution.py:39
  177.7 5.8 %collective-permute-done.28 = bf16[128,1024]{1,0:T(8,128)(2,1)S(1)} collective-permute-done((bf16[128,1024]{1,0:T(8,128)(2,1)}, bf16[128,1024]{1,0:T(8,128)(2,1)S(1)}, u32[]{:S(2)}, u32[]{:S(2)}) %collective-permute-start.28) | collective-permute-done | bytes 262176 | tf_op jit(solution)/shard_map/ppermute | solution.py:39
  183.5 6.2 %collective-permute-done.26.refs_0_ = bf16[512,1024]{1,0:T(8,128)(2,1)S(1)} collective-permute-done((bf16[512,1024]{1,0:T(8,128)(2,1)}, bf16[512,1024]{1,0:T(8,128)(2,1)S(1)}, u32[]{:S(2)}, u32[]{:S(2)}) %collective-permute-start.26) | collective-permute-done | bytes 1048608 | tf_op jit(solution)/shard_map/ppermute | solution.py:39
  196.6 4.5 %collective-permute-done.37 = bf16[64,1024]{1,0:T(8,128)(2,1)S(1)} collective-permute-done((bf16[64,1024]{1,0:T(8,128)(2,1)S(1)}, bf16[64,1024]{1,0:T(8,128)(2,1)S(1)}, u32[]{:S(2)}, u32[]{:S(2)}) %collective-permute-start.37) | collective-permute-done | bytes 131104 | tf_op jit(solution)/shard_map/ppermute | solution.py:39
  204.8 3.7 %collective-permute-done.39 = f32[8,1792]{1,0:T(8,128)S(1)} collective-permute-done((f32[8,1792]{1,0:T(8,128)S(1)}, f32[8,1792]{1,0:T(8,128)S(1)}, u32[]{:S(2)}, u32[]{:S(2)}) %collective-permute-start.39) | collective-permute-done | bytes 57376 | tf_op jit(solution)/shard_map/ppermute | solution.py:39
  208.5 4.9 %collective-permute-done.34 = bf16[128,1024]{1,0:T(8,128)(2,1)S(1)} collective-permute-done((bf16[128,1024]{1,0:T(8,128)(2,1)S(1)}, bf16[128,1024]{1,0:T(8,128)(2,1)S(1)}, u32[]{:S(2)}, u32[]{:S(2)}) %collective-permute-start.34) | collective-permute-done | bytes 262176 | tf_op jit(solution)/shard_map/ppermute | solution.py:39
  213.4 3.3 %collective-permute-done.32.refs_0_ = bf16[640,512]{1,0:T(8,128)(2,1)S(1)} collective-permute-done((bf16[640,512]{1,0:T(8,128)(2,1)S(1)}, bf16[640,512]{1,0:T(8,128)(2,1)S(1)}, u32[]{:S(2)}, u32[]{:S(2)}) %collective-permute-start.32) | collective-permute-done | bytes 655392 | tf_op jit(solution)/shard_map/ppermute | solution.py:39
  231.7 8.0 %collective-permute-done.42 = bf16[160,512]{1,0:T(8,128)(2,1)} collective-permute-done((bf16[160,512]{1,0:T(8,128)(2,1)S(1)}, bf16[160,512]{1,0:T(8,128)(2,1)}, u32[]{:S(2)}, u32[]{:S(2)}) %collective-permute-start.42) | collective-permute-done | bytes 163872 | tf_op jit(solution)/shard_map/ppermute | solution.py:39
  242.7 3.0 %collective-permute-start.48 = (f32[8,1792]{1,0:T(8,128)S(1)}, f32[8,1792]{1,0:T(8,128)S(1)}, u32[]{:S(2)}, u32[]{:S(2)}) collective-permute-start(f32[8,1792]{1,0:T(8,128)S(1)} %add.159), channel_id=1, source_target_pairs={{0,16},{4,20},{8,24},{12,28},{16,0},{20,4},{24,8},{28,12},{1,17},{... | collective-permute-start | bytes 172040 | tf_op jit(solution)/shard_map/ppermute | solution.py:39
  (377 shorter events, 113.1 us)
Async XLA Ops:
  4.2 17.6 %collective-permute-start.2 = (bf16[128,768]{1,0:T(8,128)(2,1)S(1)}, bf16[128,768]{1,0:T(8,128)(2,1)S(1)}, u32[]{:S(2)}, u32[]{:S(2)}) collective-permute-start(bf16[128,768]{1,0:T(8,128)(2,1)S(1)} %fusion.13.refs_0_), channel_id=1, source_target_pairs={{0,24},{4,28},{8,16},{12,20},{16,8},{20,12},{24,0},{28,4},{1,25},{... | collective-permute-start | bytes 589832 | tf_op jit(solution)/shard_map/ppermute | solution.py:39
  9.3 16.7 %collective-permute-start.1 = (bf16[128,768]{1,0:T(8,128)(2,1)S(1)}, bf16[128,768]{1,0:T(8,128)(2,1)S(1)}, u32[]{:S(2)}, u32[]{:S(2)}) collective-permute-start(bf16[128,768]{1,0:T(8,128)(2,1)S(1)} %fusion.13.refs_0_), channel_id=1, source_target_pairs={{0,16},{4,20},{8,24},{12,28},{16,0},{20,4},{24,8},{28,12},{1,17},{... | collective-permute-start | bytes 589832 | tf_op jit(solution)/shard_map/ppermute | solution.py:39
  9.4 16.7 %collective-permute-start = (bf16[128,768]{1,0:T(8,128)(2,1)S(1)}, bf16[128,768]{1,0:T(8,128)(2,1)S(1)}, u32[]{:S(2)}, u32[]{:S(2)}) collective-permute-start(bf16[128,768]{1,0:T(8,128)(2,1)S(1)} %fusion.13.refs_0_), channel_id=1, source_target_pairs={{0,8},{4,12},{8,0},{12,4},{16,24},{20,28},{24,16},{28,20},{1,9},{5... | collective-permute-start | bytes 589832 | tf_op jit(solution)/shard_map/ppermute | solution.py:39
  26.1 21.8 %collective-permute-start.7 = (bf16[512,768]{1,0:T(8,128)(2,1)S(1)}, bf16[512,768]{1,0:T(8,128)(2,1)S(1)}, u32[]{:S(2)}, u32[]{:S(2)}) collective-permute-start(bf16[512,768]{1,0:T(8,128)(2,1)S(1)} %shard_map.237.near_ref.early_near_ref), channel_id=1, source_target_pairs={{0,4},{4,0},{8,12},{12,8},{16,20},{20,16},{24,28},{28,24},{1,5},{5... | collective-permute-start | bytes 2359304 | tf_op jit(solution)/shard_map/ppermute | solution.py:39
  30.2 17.6 %collective-permute-start.5 = (bf16[128,896]{1,0:T(8,128)(2,1)S(1)}, bf16[128,896]{1,0:T(8,128)(2,1)S(1)}, u32[]{:S(2)}, u32[]{:S(2)}) collective-permute-start(bf16[128,896]{1,0:T(8,128)(2,1)S(1)} %pad_maximum_fusion.7.refs_0_), channel_id=1, source_target_pairs={{0,16},{4,20},{8,24},{12,28},{16,0},{20,4},{24,8},{28,12},{1,17},{... | collective-permute-start | bytes 688136 | tf_op jit(solution)/shard_map/ppermute | solution.py:39
  30.2 17.6 %collective-permute-start.4 = (bf16[128,896]{1,0:T(8,128)(2,1)S(1)}, bf16[128,896]{1,0:T(8,128)(2,1)S(1)}, u32[]{:S(2)}, u32[]{:S(2)}) collective-permute-start(bf16[128,896]{1,0:T(8,128)(2,1)S(1)} %pad_maximum_fusion.7.refs_0_), channel_id=1, source_target_pairs={{0,8},{4,12},{8,0},{12,4},{16,24},{20,28},{24,16},{28,20},{1,9},{5... | collective-permute-start | bytes 688136 | tf_op jit(solution)/shard_map/ppermute | solution.py:39
  53.3 24.7 %collective-permute-start.13 = (bf16[512,896]{1,0:T(8,128)(2,1)S(1)}, bf16[512,896]{1,0:T(8,128)(2,1)S(1)}, u32[]{:S(2)}, u32[]{:S(2)}) collective-permute-start(bf16[512,896]{1,0:T(8,128)(2,1)S(1)} %shard_map.241.near_ref), channel_id=1, source_target_pairs={{0,4},{4,0},{8,12},{12,8},{16,20},{20,16},{24,28},{28,24},{1,5},{5... | collective-permute-start | bytes 2752520 | tf_op jit(solution)/shard_map/ppermute | solution.py:39
  53.9 18.5 %collective-permute-start.12 = (bf16[128,1024]{1,0:T(8,128)(2,1)}, bf16[128,1024]{1,0:T(8,128)(2,1)S(1)}, u32[]{:S(2)}, u32[]{:S(2)}) collective-permute-start(bf16[128,1024]{1,0:T(8,128)(2,1)} %pad_maximum_fusion.4.refs_0_), channel_id=1, source_target_pairs={{0,24},{4,28},{8,16},{12,20},{16,8},{20,12},{24,0},{28,4},{1,25},{... | collective-permute-start | bytes 786440 | tf_op jit(solution)/shard_map/ppermute | solution.py:39
  55.5 21.5 %collective-permute-start.11 = (bf16[128,1024]{1,0:T(8,128)(2,1)}, bf16[128,1024]{1,0:T(8,128)(2,1)S(1)}, u32[]{:S(2)}, u32[]{:S(2)}) collective-permute-start(bf16[128,1024]{1,0:T(8,128)(2,1)} %pad_maximum_fusion.4.refs_0_), channel_id=1, source_target_pairs={{0,16},{4,20},{8,24},{12,28},{16,0},{20,4},{24,8},{28,12},{1,17},{... | collective-permute-start | bytes 786440 | tf_op jit(solution)/shard_map/ppermute | solution.py:39
  55.5 21.5 %collective-permute-start.10 = (bf16[128,1024]{1,0:T(8,128)(2,1)}, bf16[128,1024]{1,0:T(8,128)(2,1)S(1)}, u32[]{:S(2)}, u32[]{:S(2)}) collective-permute-start(bf16[128,1024]{1,0:T(8,128)(2,1)} %pad_maximum_fusion.4.refs_0_), channel_id=1, source_target_pairs={{0,8},{4,12},{8,0},{12,4},{16,24},{20,28},{24,16},{28,20},{1,9},{5... | collective-permute-start | bytes 786440 | tf_op jit(solution)/shard_map/ppermute | solution.py:39
  82.1 28.1 %collective-permute-start.16 = (bf16[512,1024]{1,0:T(8,128)(2,1)}, bf16[512,1024]{1,0:T(8,128)(2,1)S(1)}, u32[]{:S(2)}, u32[]{:S(2)}) collective-permute-start(bf16[512,1024]{1,0:T(8,128)(2,1)} %copy-done.3), channel_id=1, source_target_pairs={{0,4},{4,0},{8,12},{12,8},{16,20},{20,16},{24,28},{28,24},{1,5},{5... | collective-permute-start | bytes 3145736 | tf_op jit(solution)/shard_map/ppermute | solution.py:39
  88.5 21.6 %collective-permute-start.18 = (bf16[256,512]{1,0:T(8,128)(2,1)S(1)}, bf16[256,512]{1,0:T(8,128)(2,1)S(1)}, u32[]{:S(2)}, u32[]{:S(2)}) collective-permute-start(bf16[256,512]{1,0:T(8,128)(2,1)S(1)} %copy-done.22), channel_id=1, source_target_pairs={{0,16},{4,20},{8,24},{12,28},{16,0},{20,4},{24,8},{28,12},{1,17},{... | collective-permute-start | bytes 786440 | tf_op jit(solution)/shard_map/ppermute | solution.py:39
  88.5 21.6 %collective-permute-start.17 = (bf16[256,512]{1,0:T(8,128)(2,1)S(1)}, bf16[256,512]{1,0:T(8,128)(2,1)S(1)}, u32[]{:S(2)}, u32[]{:S(2)}) collective-permute-start(bf16[256,512]{1,0:T(8,128)(2,1)S(1)} %copy-done.22), channel_id=1, source_target_pairs={{0,8},{4,12},{8,0},{12,4},{16,24},{20,28},{24,16},{28,20},{1,9},{5... | collective-permute-start | bytes 786440 | tf_op jit(solution)/shard_map/ppermute | solution.py:39
  116.6 27.3 %collective-permute-start.20 = (bf16[512,1024]{1,0:T(8,128)(2,1)}, bf16[512,1024]{1,0:T(8,128)(2,1)}, u32[]{:S(2)}, u32[]{:S(2)}) collective-permute-start(bf16[512,1024]{1,0:T(8,128)(2,1)} %get-tuple-element.159), channel_id=1, source_target_pairs={{0,4},{4,0},{8,12},{12,8},{16,20},{20,16},{24,28},{28,24},{1,5},{5... | collective-permute-start | bytes 3145736 | tf_op jit(solution)/shard_map/ppermute | solution.py:39
  120.9 21.5 %collective-permute-start.22 = (bf16[256,512]{1,0:T(8,128)(2,1)}, bf16[256,512]{1,0:T(8,128)(2,1)S(1)}, u32[]{:S(2)}, u32[]{:S(2)}) collective-permute-start(bf16[256,512]{1,0:T(8,128)(2,1)} %copy-done.57), channel_id=1, source_target_pairs={{0,16},{4,20},{8,24},{12,28},{16,0},{20,4},{24,8},{28,12},{1,17},{... | collective-permute-start | bytes 786440 | tf_op jit(solution)/shard_map/ppermute | solution.py:39
  123.0 20.1 %collective-permute-start.23 = (bf16[256,512]{1,0:T(8,128)(2,1)}, bf16[256,512]{1,0:T(8,128)(2,1)S(1)}, u32[]{:S(2)}, u32[]{:S(2)}) collective-permute-start(bf16[256,512]{1,0:T(8,128)(2,1)} %copy-done.56), channel_id=1, source_target_pairs={{0,24},{4,28},{8,16},{12,20},{16,8},{20,12},{24,0},{28,4},{1,25},{... | collective-permute-start | bytes 786440 | tf_op jit(solution)/shard_map/ppermute | solution.py:39
  157.5 20.2 %collective-permute-start.27 = (bf16[128,1024]{1,0:T(8,128)(2,1)}, bf16[128,1024]{1,0:T(8,128)(2,1)S(1)}, u32[]{:S(2)}, u32[]{:S(2)}) collective-permute-start(bf16[128,1024]{1,0:T(8,128)(2,1)} %copy-done.55), channel_id=1, source_target_pairs={{0,8},{4,12},{8,0},{12,4},{16,24},{20,28},{24,16},{28,20},{1,9},{5... | collective-permute-start | bytes 786440 | tf_op jit(solution)/shard_map/ppermute | solution.py:39
  162.0 21.5 %collective-permute-start.28 = (bf16[128,1024]{1,0:T(8,128)(2,1)}, bf16[128,1024]{1,0:T(8,128)(2,1)S(1)}, u32[]{:S(2)}, u32[]{:S(2)}) collective-permute-start(bf16[128,1024]{1,0:T(8,128)(2,1)} %copy-done.54), channel_id=1, source_target_pairs={{0,16},{4,20},{8,24},{12,28},{16,0},{20,4},{24,8},{28,12},{1,17},{... | collective-permute-start | bytes 786440 | tf_op jit(solution)/shard_map/ppermute | solution.py:39
  162.2 21.4 %collective-permute-start.29 = (bf16[128,1024]{1,0:T(8,128)(2,1)}, bf16[128,1024]{1,0:T(8,128)(2,1)S(1)}, u32[]{:S(2)}, u32[]{:S(2)}) collective-permute-start(bf16[128,1024]{1,0:T(8,128)(2,1)} %copy-done.53), channel_id=1, source_target_pairs={{0,24},{4,28},{8,16},{12,20},{16,8},{20,12},{24,0},{28,4},{1,25},{... | collective-permute-start | bytes 786440 | tf_op jit(solution)/shard_map/ppermute | solution.py:39
  164.4 25.3 %collective-permute-start.26 = (bf16[512,1024]{1,0:T(8,128)(2,1)}, bf16[512,1024]{1,0:T(8,128)(2,1)S(1)}, u32[]{:S(2)}, u32[]{:S(2)}) collective-permute-start(bf16[512,1024]{1,0:T(8,128)(2,1)} %copy-done.50), channel_id=1, source_target_pairs={{0,4},{4,0},{8,12},{12,8},{16,20},{20,16},{24,28},{28,24},{1,5},{5... | collective-permute-start | bytes 3145736 | tf_op jit(solution)/shard_map/ppermute | solution.py:39
  191.2 17.2 %collective-permute-start.33 = (bf16[128,1024]{1,0:T(8,128)(2,1)S(1)}, bf16[128,1024]{1,0:T(8,128)(2,1)S(1)}, u32[]{:S(2)}, u32[]{:S(2)}) collective-permute-start(bf16[128,1024]{1,0:T(8,128)(2,1)S(1)} %get-tuple-element.192), channel_id=1, source_target_pairs={{0,8},{4,12},{8,0},{12,4},{16,24},{20,28},{24,16},{28,20},{1,9},{5... | collective-permute-start | bytes 786440 | tf_op jit(solution)/shard_map/ppermute | solution.py:39
  192.1 21.3 %collective-permute-start.34 = (bf16[128,1024]{1,0:T(8,128)(2,1)S(1)}, bf16[128,1024]{1,0:T(8,128)(2,1)S(1)}, u32[]{:S(2)}, u32[]{:S(2)}) collective-permute-start(bf16[128,1024]{1,0:T(8,128)(2,1)S(1)} %get-tuple-element.193), channel_id=1, source_target_pairs={{0,16},{4,20},{8,24},{12,28},{16,0},{20,4},{24,8},{28,12},{1,17},{... | collective-permute-start | bytes 786440 | tf_op jit(solution)/shard_map/ppermute | solution.py:39
  193.4 20.0 %collective-permute-start.35 = (bf16[128,1024]{1,0:T(8,128)(2,1)S(1)}, bf16[128,1024]{1,0:T(8,128)(2,1)S(1)}, u32[]{:S(2)}, u32[]{:S(2)}) collective-permute-start(bf16[128,1024]{1,0:T(8,128)(2,1)S(1)} %get-tuple-element.194), channel_id=1, source_target_pairs={{0,24},{4,28},{8,16},{12,20},{16,8},{20,12},{24,0},{28,4},{1,25},{... | collective-permute-start | bytes 786440 | tf_op jit(solution)/shard_map/ppermute | solution.py:39
  201.3 15.4 %collective-permute-start.32 = (bf16[640,512]{1,0:T(8,128)(2,1)S(1)}, bf16[640,512]{1,0:T(8,128)(2,1)S(1)}, u32[]{:S(2)}, u32[]{:S(2)}) collective-permute-start(bf16[640,512]{1,0:T(8,128)(2,1)S(1)} %fusion.22), channel_id=1, source_target_pairs={{0,4},{4,0},{8,12},{12,8},{16,20},{20,16},{24,28},{28,24},{1,5},{5... | collective-permute-start | bytes 1966088 | tf_op jit(solution)/shard_map/ppermute | solution.py:39
  (110 other events, 840.9 us)

commit v5 on v4

--- a/solution.py
+++ b/solution.py
@@ -937,8 +937,15 @@
     for bits in (1, 2):
         small = group_sum(small, "tensor", 4, [bits])
     in_got, mid_got, down_got, out_give, small = together(in_got, mid_got, down_got, out_give, small)
+    if len(back) == 1 and share_rows % 16 == 0:
+        in_kept, in_sent, _ = add_split(in_kept, in_got, stay, back[0], [rows, share_rows])
+        in_sent, mid_kept, mid_got, down_kept, down_got, out_give = together(
+            in_sent, mid_kept, mid_got, down_kept, down_got, out_give
+        )
+        in_sum = add(in_kept, send(in_sent, back[0], count))
+    else:
+        in_sum = add(*finish(in_kept, in_got, stay, back, count, [rows, share_rows]))
     mid_sum = add(mid_kept, mid_got)
-    in_sum = add(*finish(in_kept, in_got, stay, back, count, [rows, share_rows]))
     down_sum = add(*finish(down_kept, down_got, down_stay, back[1:] + last, count))
     ffn_sum = finish_tensor(out_keep, out_give, shard_index)
     output = (hidden + ffn_sum).astype(BFLOAT)

time: 253 us -> 251 us (level)
  transfers between devices with their start and end apart: 50 -> 50, of which waited for: 22 -> 21; matrix products, arithmetic and copies ran while one was open for 10% -> 10% of each run, Pallas kernels for 2% -> 2%
where the time goes in v5:
time: 251 us; the launch traced here: 250 us
  waiting for transfers between devices  89.6 us (36%)
  starting transfers between devices  62.6 us (25%)
  local copies, waits for them, and re-layouts  28.8 us (11%)
  blocking collectives  28.7 us (11%)
  Pallas kernels  19.4 us (8%)
  other arithmetic  18.4 us (7%)
    ppermute x50, waiting for transfers between devices, swap(): return lax.ppermute(values, axis, [(i, i ^ bits) for i in range(count)])  89.6 us
    ppermute x50, starting transfers between devices, swap(): return lax.ppermute(values, axis, [(i, i ^ bits) for i in range(count)])  62.6 us
    all_gather x4, blocking collectives, gather_tensor(): return lax.all_gather(values, 'tensor', axis=0, tiled=True)  28.7 us
    unnamed x182, local copies, waits for them, and re-layouts  21.8 us
    pallas_call x10, Pallas kernels, call(): pl.pallas_call(kernel, out_shape=[jax.ShapeDtypeStruct(shape, dtype) for...  16 us
  transfers between devices with their start and end apart: 50, of which 21 were waited for; matrix products, arithmetic and copies ran while one was open for 10% of the time, Pallas kernels for 2%

profile of v5, /device:TPU:0, one launch (start us, length us, event | category | flops | bytes accessed | tf_op | source)
XLA Modules:
  0.0 250.0 jit_solution(2145960116450236313)
XLA Ops:
  4.2 5.1 %collective-permute-start.2 = (bf16[128,768]{1,0:T(8,128)(2,1)S(1)}, bf16[128,768]{1,0:T(8,128)(2,1)S(1)}, u32[]{:S(2)}, u32[]{:S(2)}) collective-permute-start(bf16[128,768]{1,0:T(8,128)(2,1)S(1)} %fusion.13.refs_0_), channel_id=1, source_target_pairs={{0,24},{4,28},{8,16},{12,20},{16,8},{20,12},{24,0},{28,4},{1,25},{... | collective-permute-start | bytes 589832 | tf_op jit(solution)/shard_map/ppermute | solution.py:39
  13.6 7.2 %all_gather.12.normed_ref.refs_0_ = bf16[256,1024]{1,0:T(8,128)(2,1)S(1)} all-gather(bf16[64,1024]{1,0:T(8,128)(2,1)S(1)} %fusion.4), channel_id=1, replica_groups=mesh['dp'=8,'tensor'=4] {'tensor'}, dimensions={0}, use_global_device_ids=true | all-gather | bytes 655360 | tf_op jit(solution)/shard_map/all_gather | solution.py:670
  21.9 4.2 %collective-permute-done.1.refs_2_ = bf16[128,768]{1,0:T(8,128)(2,1)S(1)} collective-permute-done((bf16[128,768]{1,0:T(8,128)(2,1)S(1)}, bf16[128,768]{1,0:T(8,128)(2,1)S(1)}, u32[]{:S(2)}, u32[]{:S(2)}) %collective-permute-start.1) | collective-permute-done | bytes 196640 | tf_op jit(solution)/shard_map/ppermute | solution.py:39
  32.9 7.6 %all_gather.13.cot_ref = bf16[256,1024]{1,0:T(8,128)(2,1)} all-gather(bf16[64,1024]{1,0:T(8,128)(2,1)S(1)} %get-tuple-element.145), channel_id=1, replica_groups=mesh['dp'=8,'tensor'=4] {'tensor'}, dimensions={0}, use_global_device_ids=true | all-gather | bytes 655360 | tf_op jit(solution)/shard_map/all_gather | solution.py:670
  40.5 7.3 %collective-permute-done.5.refs_2_ = bf16[128,896]{1,0:T(8,128)(2,1)S(1)} collective-permute-done((bf16[128,896]{1,0:T(8,128)(2,1)S(1)}, bf16[128,896]{1,0:T(8,128)(2,1)S(1)}, u32[]{:S(2)}, u32[]{:S(2)}) %collective-permute-start.5) | collective-permute-done | bytes 229408 | tf_op jit(solution)/shard_map/ppermute | solution.py:39
  55.5 2.8 %collective-permute-start.10 = (bf16[128,1024]{1,0:T(8,128)(2,1)}, bf16[128,1024]{1,0:T(8,128)(2,1)S(1)}, u32[]{:S(2)}, u32[]{:S(2)}) collective-permute-start(bf16[128,1024]{1,0:T(8,128)(2,1)} %pad_maximum_fusion.4.refs_0_), channel_id=1, source_target_pairs={{0,8},{4,12},{8,0},{12,4},{16,24},{20,28},{24,16},{28,20},{1,9},{5... | collective-permute-start | bytes 786440 | tf_op jit(solution)/shard_map/ppermute | solution.py:39
  58.4 7.4 %collective-permute-done.9 = bf16[2,8,32,512]{3,2,0,1:T(8,128)(2,1)} collective-permute-done((bf16[2,8,32,512]{3,2,0,1:T(8,128)(2,1)}, bf16[2,8,32,512]{3,2,0,1:T(8,128)(2,1)}, u32[]{:S(2)}, u32[]{:S(2)}) %collective-permute-start.9) | collective-permute-done | bytes 524320 | tf_op jit(solution)/shard_map/ppermute | solution.py:39
  72.5 4.5 %collective-permute-done.11.refs_2_ = bf16[128,1024]{1,0:T(8,128)(2,1)S(1)} collective-permute-done((bf16[128,1024]{1,0:T(8,128)(2,1)}, bf16[128,1024]{1,0:T(8,128)(2,1)S(1)}, u32[]{:S(2)}, u32[]{:S(2)}) %collective-permute-start.11) | collective-permute-done | bytes 262176 | tf_op jit(solution)/shard_map/ppermute | solution.py:39
  91.6 6.6 %all_gather.14.rows_ref = bf16[256,1024]{1,0:T(8,128)(2,1)S(1)} all-gather(bf16[64,1024]{1,0:T(8,128)(2,1)S(1)} %multiply_convert_fusion), channel_id=1, replica_groups=mesh['dp'=8,'tensor'=4] {'tensor'}, dimensions={0}, use_global_device_ids=true | all-gather | bytes 655360 | tf_op jit(solution)/shard_map/all_gather | solution.py:670
  98.1 12.0 %collective-permute-done.18.refs_4_ = bf16[256,512]{1,0:T(8,128)(2,1)S(1)} collective-permute-done((bf16[256,512]{1,0:T(8,128)(2,1)S(1)}, bf16[256,512]{1,0:T(8,128)(2,1)S(1)}, u32[]{:S(2)}, u32[]{:S(2)}) %collective-permute-start.18) | collective-permute-done | bytes 262176 | tf_op jit(solution)/shard_map/ppermute | solution.py:39
  110.2 4.1 %shard_map.245 = (f32[2,64,1024]{2,1,0:T(8,128)S(1)}, f32[2,64,1024]{2,1,0:T(8,128)S(1)}, f32[2,64,1024]{2,1,0:T(8,128)S(1)}, f32[2,64,1024]{2,1,0:T(8,128)S(1)}...) custom-call(s32[1]{0:T(128)} %bitcast.11.core_ref, ...), custom_call_target="tpu_custom_call" | custom-call | flops 1000 | bytes 1000 | tf_op jit(solution)/shard_map/pallas_call | solution.py:598
  129.0 7.3 %all_gather.15.grad_ref.refs_1_ = bf16[256,1024]{1,0:T(8,128)(2,1)S(1)} all-gather(bf16[64,1024]{1,0:T(8,128)(2,1)S(1)} %fusion.28), channel_id=1, replica_groups=mesh['dp'=8,'tensor'=4] {'tensor'}, dimensions={0}, use_global_device_ids=true | all-gather | bytes 655360 | tf_op jit(solution)/shard_map/all_gather | solution.py:670
  137.0 5.5 %collective-permute-done.22.refs_1_ = bf16[256,512]{1,0:T(8,128)(2,1)S(1)} collective-permute-done((bf16[256,512]{1,0:T(8,128)(2,1)}, bf16[256,512]{1,0:T(8,128)(2,1)S(1)}, u32[]{:S(2)}, u32[]{:S(2)}) %collective-permute-start.22) | collective-permute-done | bytes 262176 | tf_op jit(solution)/shard_map/ppermute | solution.py:39
  150.2 3.8 %shard_map.249 = (bf16[256,512]{1,0:T(8,128)(2,1)S(1)}, f32[8,640]{1,0:T(8,128)S(1)}, f32[8,128]{1,0:T(8,128)S(1)}, f32[256,512]{1,0:T(8,128)}) custom-call(s32[1]{0:T(128)} %bitcast.14.owner_ref, f32[256,384]{1,0:T(8,128)S(1)} %get-tuple-element.194.pre_grad_ref, f32[256,1792]{1,0:T(8,128)S(1)} %copy-done.16, bf16[256,1024]{1,0:T(8,128)(2,1)S(1)} %copy-done.14, ...), custom_call_target="tpu_custom_call" | custom-call | flops 1000 | bytes 1000 | tf_op jit(solution)/shard_map/pallas_call | solution.py:598
  157.5 4.5 %collective-permute-start.27 = (bf16[128,1024]{1,0:T(8,128)(2,1)}, bf16[128,1024]{1,0:T(8,128)(2,1)S(1)}, u32[]{:S(2)}, u32[]{:S(2)}) collective-permute-start(bf16[128,1024]{1,0:T(8,128)(2,1)} %copy-done.55), channel_id=1, source_target_pairs={{0,8},{4,12},{8,0},{12,4},{16,24},{20,28},{24,16},{28,20},{1,9},{5... | collective-permute-start | bytes 786440 | tf_op jit(solution)/shard_map/ppermute | solution.py:39
  169.6 7.3 %collective-permute-done.31 = bf16[256,512]{1,0:T(8,128)(2,1)S(1)} collective-permute-done((bf16[256,512]{1,0:T(8,128)(2,1)S(1)}, bf16[256,512]{1,0:T(8,128)(2,1)S(1)}, u32[]{:S(2)}, u32[]{:S(2)}) %collective-permute-start.31) | collective-permute-done | bytes 262176 | tf_op jit(solution)/shard_map/ppermute | solution.py:39
  177.7 5.8 %collective-permute-done.28 = bf16[128,1024]{1,0:T(8,128)(2,1)S(1)} collective-permute-done((bf16[128,1024]{1,0:T(8,128)(2,1)}, bf16[128,1024]{1,0:T(8,128)(2,1)S(1)}, u32[]{:S(2)}, u32[]{:S(2)}) %collective-permute-start.28) | collective-permute-done | bytes 262176 | tf_op jit(solution)/shard_map/ppermute | solution.py:39
  183.5 6.2 %collective-permute-done.26.refs_0_ = bf16[512,1024]{1,0:T(8,128)(2,1)S(1)} collective-permute-done((bf16[512,1024]{1,0:T(8,128)(2,1)}, bf16[512,1024]{1,0:T(8,128)(2,1)S(1)}, u32[]{:S(2)}, u32[]{:S(2)}) %collective-permute-start.26) | collective-permute-done | bytes 1048608 | tf_op jit(solution)/shard_map/ppermute | solution.py:39
  196.6 4.5 %collective-permute-done.37 = bf16[64,1024]{1,0:T(8,128)(2,1)S(1)} collective-permute-done((bf16[64,1024]{1,0:T(8,128)(2,1)S(1)}, bf16[64,1024]{1,0:T(8,128)(2,1)S(1)}, u32[]{:S(2)}, u32[]{:S(2)}) %collective-permute-start.37) | collective-permute-done | bytes 131104 | tf_op jit(solution)/shard_map/ppermute | solution.py:39
  204.8 3.7 %collective-permute-done.39 = f32[8,1792]{1,0:T(8,128)S(1)} collective-permute-done((f32[8,1792]{1,0:T(8,128)S(1)}, f32[8,1792]{1,0:T(8,128)S(1)}, u32[]{:S(2)}, u32[]{:S(2)}) %collective-permute-start.39) | collective-permute-done | bytes 57376 | tf_op jit(solution)/shard_map/ppermute | solution.py:39
  208.5 4.9 %collective-permute-done.34 = bf16[128,1024]{1,0:T(8,128)(2,1)S(1)} collective-permute-done((bf16[128,1024]{1,0:T(8,128)(2,1)S(1)}, bf16[128,1024]{1,0:T(8,128)(2,1)S(1)}, u32[]{:S(2)}, u32[]{:S(2)}) %collective-permute-start.34) | collective-permute-done | bytes 262176 | tf_op jit(solution)/shard_map/ppermute | solution.py:39
  213.4 3.3 %collective-permute-done.32.refs_0_ = bf16[640,512]{1,0:T(8,128)(2,1)S(1)} collective-permute-done((bf16[640,512]{1,0:T(8,128)(2,1)S(1)}, bf16[640,512]{1,0:T(8,128)(2,1)S(1)}, u32[]{:S(2)}, u32[]{:S(2)}) %collective-permute-start.32) | collective-permute-done | bytes 655392 | tf_op jit(solution)/shard_map/ppermute | solution.py:39
  229.6 7.6 %collective-permute-done.42 = bf16[160,512]{1,0:T(8,128)(2,1)} collective-permute-done((bf16[160,512]{1,0:T(8,128)(2,1)S(1)}, bf16[160,512]{1,0:T(8,128)(2,1)}, u32[]{:S(2)}, u32[]{:S(2)}) %collective-permute-start.42) | collective-permute-done | bytes 163872 | tf_op jit(solution)/shard_map/ppermute | solution.py:39
  240.2 3.3 %collective-permute-start.48 = (f32[8,1792]{1,0:T(8,128)S(1)}, f32[8,1792]{1,0:T(8,128)S(1)}, u32[]{:S(2)}, u32[]{:S(2)}) collective-permute-start(f32[8,1792]{1,0:T(8,128)S(1)} %add.159), channel_id=1, source_target_pairs={{0,16},{4,20},{8,24},{12,28},{16,0},{20,4},{24,8},{28,12},{1,17},{... | collective-permute-start | bytes 172040 | tf_op jit(solution)/shard_map/ppermute | solution.py:39
  (377 shorter events, 111.4 us)
Async XLA Ops:
  4.2 17.6 %collective-permute-start.2 = (bf16[128,768]{1,0:T(8,128)(2,1)S(1)}, bf16[128,768]{1,0:T(8,128)(2,1)S(1)}, u32[]{:S(2)}, u32[]{:S(2)}) collective-permute-start(bf16[128,768]{1,0:T(8,128)(2,1)S(1)} %fusion.13.refs_0_), channel_id=1, source_target_pairs={{0,24},{4,28},{8,16},{12,20},{16,8},{20,12},{24,0},{28,4},{1,25},{... | collective-permute-start | bytes 589832 | tf_op jit(solution)/shard_map/ppermute | solution.py:39
  9.3 16.7 %collective-permute-start.1 = (bf16[128,768]{1,0:T(8,128)(2,1)S(1)}, bf16[128,768]{1,0:T(8,128)(2,1)S(1)}, u32[]{:S(2)}, u32[]{:S(2)}) collective-permute-start(bf16[128,768]{1,0:T(8,128)(2,1)S(1)} %fusion.13.refs_0_), channel_id=1, source_target_pairs={{0,16},{4,20},{8,24},{12,28},{16,0},{20,4},{24,8},{28,12},{1,17},{... | collective-permute-start | bytes 589832 | tf_op jit(solution)/shard_map/ppermute | solution.py:39
  9.4 16.7 %collective-permute-start = (bf16[128,768]{1,0:T(8,128)(2,1)S(1)}, bf16[128,768]{1,0:T(8,128)(2,1)S(1)}, u32[]{:S(2)}, u32[]{:S(2)}) collective-permute-start(bf16[128,768]{1,0:T(8,128)(2,1)S(1)} %fusion.13.refs_0_), channel_id=1, source_target_pairs={{0,8},{4,12},{8,0},{12,4},{16,24},{20,28},{24,16},{28,20},{1,9},{5... | collective-permute-start | bytes 589832 | tf_op jit(solution)/shard_map/ppermute | solution.py:39
  26.1 21.8 %collective-permute-start.7 = (bf16[512,768]{1,0:T(8,128)(2,1)S(1)}, bf16[512,768]{1,0:T(8,128)(2,1)S(1)}, u32[]{:S(2)}, u32[]{:S(2)}) collective-permute-start(bf16[512,768]{1,0:T(8,128)(2,1)S(1)} %shard_map.237.near_ref.early_near_ref), channel_id=1, source_target_pairs={{0,4},{4,0},{8,12},{12,8},{16,20},{20,16},{24,28},{28,24},{1,5},{5... | collective-permute-start | bytes 2359304 | tf_op jit(solution)/shard_map/ppermute | solution.py:39
  30.2 17.6 %collective-permute-start.5 = (bf16[128,896]{1,0:T(8,128)(2,1)S(1)}, bf16[128,896]{1,0:T(8,128)(2,1)S(1)}, u32[]{:S(2)}, u32[]{:S(2)}) collective-permute-start(bf16[128,896]{1,0:T(8,128)(2,1)S(1)} %pad_maximum_fusion.7.refs_0_), channel_id=1, source_target_pairs={{0,16},{4,20},{8,24},{12,28},{16,0},{20,4},{24,8},{28,12},{1,17},{... | collective-permute-start | bytes 688136 | tf_op jit(solution)/shard_map/ppermute | solution.py:39
  30.2 17.6 %collective-permute-start.4 = (bf16[128,896]{1,0:T(8,128)(2,1)S(1)}, bf16[128,896]{1,0:T(8,128)(2,1)S(1)}, u32[]{:S(2)}, u32[]{:S(2)}) collective-permute-start(bf16[128,896]{1,0:T(8,128)(2,1)S(1)} %pad_maximum_fusion.7.refs_0_), channel_id=1, source_target_pairs={{0,8},{4,12},{8,0},{12,4},{16,24},{20,28},{24,16},{28,20},{1,9},{5... | collective-permute-start | bytes 688136 | tf_op jit(solution)/shard_map/ppermute | solution.py:39
  53.3 24.7 %collective-permute-start.13 = (bf16[512,896]{1,0:T(8,128)(2,1)S(1)}, bf16[512,896]{1,0:T(8,128)(2,1)S(1)}, u32[]{:S(2)}, u32[]{:S(2)}) collective-permute-start(bf16[512,896]{1,0:T(8,128)(2,1)S(1)} %shard_map.241.near_ref), channel_id=1, source_target_pairs={{0,4},{4,0},{8,12},{12,8},{16,20},{20,16},{24,28},{28,24},{1,5},{5... | collective-permute-start | bytes 2752520 | tf_op jit(solution)/shard_map/ppermute | solution.py:39
  53.9 18.5 %collective-permute-start.12 = (bf16[128,1024]{1,0:T(8,128)(2,1)}, bf16[128,1024]{1,0:T(8,128)(2,1)S(1)}, u32[]{:S(2)}, u32[]{:S(2)}) collective-permute-start(bf16[128,1024]{1,0:T(8,128)(2,1)} %pad_maximum_fusion.4.refs_0_), channel_id=1, source_target_pairs={{0,24},{4,28},{8,16},{12,20},{16,8},{20,12},{24,0},{28,4},{1,25},{... | collective-permute-start | bytes 786440 | tf_op jit(solution)/shard_map/ppermute | solution.py:39
  55.5 21.5 %collective-permute-start.11 = (bf16[128,1024]{1,0:T(8,128)(2,1)}, bf16[128,1024]{1,0:T(8,128)(2,1)S(1)}, u32[]{:S(2)}, u32[]{:S(2)}) collective-permute-start(bf16[128,1024]{1,0:T(8,128)(2,1)} %pad_maximum_fusion.4.refs_0_), channel_id=1, source_target_pairs={{0,16},{4,20},{8,24},{12,28},{16,0},{20,4},{24,8},{28,12},{1,17},{... | collective-permute-start | bytes 786440 | tf_op jit(solution)/shard_map/ppermute | solution.py:39
  55.5 21.5 %collective-permute-start.10 = (bf16[128,1024]{1,0:T(8,128)(2,1)}, bf16[128,1024]{1,0:T(8,128)(2,1)S(1)}, u32[]{:S(2)}, u32[]{:S(2)}) collective-permute-start(bf16[128,1024]{1,0:T(8,128)(2,1)} %pad_maximum_fusion.4.refs_0_), channel_id=1, source_target_pairs={{0,8},{4,12},{8,0},{12,4},{16,24},{20,28},{24,16},{28,20},{1,9},{5... | collective-permute-start | bytes 786440 | tf_op jit(solution)/shard_map/ppermute | solution.py:39
  82.1 28.1 %collective-permute-start.16 = (bf16[512,1024]{1,0:T(8,128)(2,1)}, bf16[512,1024]{1,0:T(8,128)(2,1)S(1)}, u32[]{:S(2)}, u32[]{:S(2)}) collective-permute-start(bf16[512,1024]{1,0:T(8,128)(2,1)} %copy-done.3), channel_id=1, source_target_pairs={{0,4},{4,0},{8,12},{12,8},{16,20},{20,16},{24,28},{28,24},{1,5},{5... | collective-permute-start | bytes 3145736 | tf_op jit(solution)/shard_map/ppermute | solution.py:39
  88.5 21.6 %collective-permute-start.18 = (bf16[256,512]{1,0:T(8,128)(2,1)S(1)}, bf16[256,512]{1,0:T(8,128)(2,1)S(1)}, u32[]{:S(2)}, u32[]{:S(2)}) collective-permute-start(bf16[256,512]{1,0:T(8,128)(2,1)S(1)} %copy-done.22), channel_id=1, source_target_pairs={{0,16},{4,20},{8,24},{12,28},{16,0},{20,4},{24,8},{28,12},{1,17},{... | collective-permute-start | bytes 786440 | tf_op jit(solution)/shard_map/ppermute | solution.py:39
  88.5 21.6 %collective-permute-start.17 = (bf16[256,512]{1,0:T(8,128)(2,1)S(1)}, bf16[256,512]{1,0:T(8,128)(2,1)S(1)}, u32[]{:S(2)}, u32[]{:S(2)}) collective-permute-start(bf16[256,512]{1,0:T(8,128)(2,1)S(1)} %copy-done.22), channel_id=1, source_target_pairs={{0,8},{4,12},{8,0},{12,4},{16,24},{20,28},{24,16},{28,20},{1,9},{5... | collective-permute-start | bytes 786440 | tf_op jit(solution)/shard_map/ppermute | solution.py:39
  116.6 27.3 %collective-permute-start.20 = (bf16[512,1024]{1,0:T(8,128)(2,1)}, bf16[512,1024]{1,0:T(8,128)(2,1)}, u32[]{:S(2)}, u32[]{:S(2)}) collective-permute-start(bf16[512,1024]{1,0:T(8,128)(2,1)} %get-tuple-element.171), channel_id=1, source_target_pairs={{0,4},{4,0},{8,12},{12,8},{16,20},{20,16},{24,28},{28,24},{1,5},{5... | collective-permute-start | bytes 3145736 | tf_op jit(solution)/shard_map/ppermute | solution.py:39
  120.9 21.5 %collective-permute-start.22 = (bf16[256,512]{1,0:T(8,128)(2,1)}, bf16[256,512]{1,0:T(8,128)(2,1)S(1)}, u32[]{:S(2)}, u32[]{:S(2)}) collective-permute-start(bf16[256,512]{1,0:T(8,128)(2,1)} %copy-done.57), channel_id=1, source_target_pairs={{0,16},{4,20},{8,24},{12,28},{16,0},{20,4},{24,8},{28,12},{1,17},{... | collective-permute-start | bytes 786440 | tf_op jit(solution)/shard_map/ppermute | solution.py:39
  123.0 20.1 %collective-permute-start.23 = (bf16[256,512]{1,0:T(8,128)(2,1)}, bf16[256,512]{1,0:T(8,128)(2,1)S(1)}, u32[]{:S(2)}, u32[]{:S(2)}) collective-permute-start(bf16[256,512]{1,0:T(8,128)(2,1)} %copy-done.56), channel_id=1, source_target_pairs={{0,24},{4,28},{8,16},{12,20},{16,8},{20,12},{24,0},{28,4},{1,25},{... | collective-permute-start | bytes 786440 | tf_op jit(solution)/shard_map/ppermute | solution.py:39
  157.5 20.2 %collective-permute-start.27 = (bf16[128,1024]{1,0:T(8,128)(2,1)}, bf16[128,1024]{1,0:T(8,128)(2,1)S(1)}, u32[]{:S(2)}, u32[]{:S(2)}) collective-permute-start(bf16[128,1024]{1,0:T(8,128)(2,1)} %copy-done.55), channel_id=1, source_target_pairs={{0,8},{4,12},{8,0},{12,4},{16,24},{20,28},{24,16},{28,20},{1,9},{5... | collective-permute-start | bytes 786440 | tf_op jit(solution)/shard_map/ppermute | solution.py:39
  162.0 21.5 %collective-permute-start.28 = (bf16[128,1024]{1,0:T(8,128)(2,1)}, bf16[128,1024]{1,0:T(8,128)(2,1)S(1)}, u32[]{:S(2)}, u32[]{:S(2)}) collective-permute-start(bf16[128,1024]{1,0:T(8,128)(2,1)} %copy-done.54), channel_id=1, source_target_pairs={{0,16},{4,20},{8,24},{12,28},{16,0},{20,4},{24,8},{28,12},{1,17},{... | collective-permute-start | bytes 786440 | tf_op jit(solution)/shard_map/ppermute | solution.py:39
  162.2 21.4 %collective-permute-start.29 = (bf16[128,1024]{1,0:T(8,128)(2,1)}, bf16[128,1024]{1,0:T(8,128)(2,1)S(1)}, u32[]{:S(2)}, u32[]{:S(2)}) collective-permute-start(bf16[128,1024]{1,0:T(8,128)(2,1)} %copy-done.53), channel_id=1, source_target_pairs={{0,24},{4,28},{8,16},{12,20},{16,8},{20,12},{24,0},{28,4},{1,25},{... | collective-permute-start | bytes 786440 | tf_op jit(solution)/shard_map/ppermute | solution.py:39
  164.4 25.3 %collective-permute-start.26 = (bf16[512,1024]{1,0:T(8,128)(2,1)}, bf16[512,1024]{1,0:T(8,128)(2,1)S(1)}, u32[]{:S(2)}, u32[]{:S(2)}) collective-permute-start(bf16[512,1024]{1,0:T(8,128)(2,1)} %copy-done.50), channel_id=1, source_target_pairs={{0,4},{4,0},{8,12},{12,8},{16,20},{20,16},{24,28},{28,24},{1,5},{5... | collective-permute-start | bytes 3145736 | tf_op jit(solution)/shard_map/ppermute | solution.py:39
  191.2 17.2 %collective-permute-start.33 = (bf16[128,1024]{1,0:T(8,128)(2,1)S(1)}, bf16[128,1024]{1,0:T(8,128)(2,1)S(1)}, u32[]{:S(2)}, u32[]{:S(2)}) collective-permute-start(bf16[128,1024]{1,0:T(8,128)(2,1)S(1)} %get-tuple-element.204), channel_id=1, source_target_pairs={{0,8},{4,12},{8,0},{12,4},{16,24},{20,28},{24,16},{28,20},{1,9},{5... | collective-permute-start | bytes 786440 | tf_op jit(solution)/shard_map/ppermute | solution.py:39
  192.1 21.3 %collective-permute-start.34 = (bf16[128,1024]{1,0:T(8,128)(2,1)S(1)}, bf16[128,1024]{1,0:T(8,128)(2,1)S(1)}, u32[]{:S(2)}, u32[]{:S(2)}) collective-permute-start(bf16[128,1024]{1,0:T(8,128)(2,1)S(1)} %get-tuple-element.205), channel_id=1, source_target_pairs={{0,16},{4,20},{8,24},{12,28},{16,0},{20,4},{24,8},{28,12},{1,17},{... | collective-permute-start | bytes 786440 | tf_op jit(solution)/shard_map/ppermute | solution.py:39
  193.4 20.0 %collective-permute-start.35 = (bf16[128,1024]{1,0:T(8,128)(2,1)S(1)}, bf16[128,1024]{1,0:T(8,128)(2,1)S(1)}, u32[]{:S(2)}, u32[]{:S(2)}) collective-permute-start(bf16[128,1024]{1,0:T(8,128)(2,1)S(1)} %get-tuple-element.206), channel_id=1, source_target_pairs={{0,24},{4,28},{8,16},{12,20},{16,8},{20,12},{24,0},{28,4},{1,25},{... | collective-permute-start | bytes 786440 | tf_op jit(solution)/shard_map/ppermute | solution.py:39
  201.3 15.4 %collective-permute-start.32 = (bf16[640,512]{1,0:T(8,128)(2,1)S(1)}, bf16[640,512]{1,0:T(8,128)(2,1)S(1)}, u32[]{:S(2)}, u32[]{:S(2)}) collective-permute-start(bf16[640,512]{1,0:T(8,128)(2,1)S(1)} %fusion.22), channel_id=1, source_target_pairs={{0,4},{4,0},{8,12},{12,8},{16,20},{20,16},{24,28},{28,24},{1,5},{5... | collective-permute-start | bytes 1966088 | tf_op jit(solution)/shard_map/ppermute | solution.py:39
  (110 other events, 866.2 us)
